TPU v7x, 32 devices: a whole 2x2x4 slice. The times are simulated.
32 devices in a mesh: side: 2 (over core), row: 4 (over y, x), col: 4 (over z).
Axes of the slice: x: 2, y: 2, z: 4, core: 2. Of those that a mesh axis runs over, the one named last changes fastest.
Arguments:
- queries: bfloat16 [512, 128, 576], P(('side', 'row'), 'col'), may hold values from -48 to 48
- cache: bfloat16 [512, 128, 576], P(('side', 'row')), may hold values from -4 to 4
- lengths: int32 [512], P(('side', 'row')), may hold values from 2 to 128, as said below
- w_uv: bfloat16 [128, 512, 128], P('col'), may hold values from -0.25 to 0.25
- w_out: bfloat16 [16384, 7168], P('col', ('side', 'row')), may hold values from -0.046875 to 0.046875
- residual_in: bfloat16 [512, 7168], P('col', ('side', 'row')), may hold values from -8 to 8
- norm_gain: bfloat16 [7168], P(('side', 'row')), may hold values from 0.099609375 to 1.8984375
- expert_ids: int32 [512, 4], P('col'), may hold values from 0 to 7, all different within a row; in each aligned block of 128 rows (0 to 127, 128 to 255, ...) at most 96 rows name the same one
- gate_vals: float32 [512, 4], P('col'), may hold values from 0.05 to 0.5
- w_gate: bfloat16 [8, 7168, 2048], P(('side', 'row'), None, 'col'), may hold values from -0.0625 to 0.0625
- w_up: bfloat16 [8, 7168, 2048], P(('side', 'row'), None, 'col'), may hold values from -0.0625 to 0.0625
- w_down: bfloat16 [8, 2048, 7168], P(('side', 'row'), 'col'), may hold values from -0.125 to 0.125
Outputs:
- mixed: bfloat16 [512, 7168], P('col', ('side', 'row'))
Inputs may be any that keep to these rules, and one draw needn't show every extreme that they name: Row b's cache holds its keys in slots below lengths[b]; some row has all 128 slots live. `expert_ids`: each row names 4 different experts; within each aligned block of 128 rows no expert is named by more than 96 rows.
All inputs are finite; a program needn't handle non-finite values.
Results may differ from a plain program's by a relative error of at most 0.015.
Values may be sent and summed in bfloat16 or wider, within the bound.
No kernel may reach another device: no remote copies, remote signals or barrier semaphores. Data moves between devices by JAX's collectives and lax.ppermute only.
A program may use at most 192 MiB of HBM per device.

v0:
```python
import jax
import jax.numpy as jnp
from jax import lax
from jax.sharding import PartitionSpec as P

D = 7168
ROPE = 64
HD = 128


def shards(
    queries,
    cache,
    lengths,
    w_uv,
    w_out,
    residual_in,
    norm_gain,
    expert_ids,
    gate_vals,
    w_gate,
    w_up,
    w_down,
):
    score_scale = (HD + ROPE) ** (-0.5)
    scores = (
        jnp.einsum("rhk,rlk->rhl", queries, cache, preferred_element_type=jnp.float32) * score_scale
    )
    places = lax.broadcasted_iota(jnp.int32, (1, 1, cache.shape[1]), 2)
    scores = jnp.where(places < lengths[:, None, None], scores, -jnp.inf)
    row_top = jnp.max(scores, axis=2, keepdims=True)
    exp_terms = jnp.exp(scores - row_top)
    attn_probs = (exp_terms / jnp.sum(exp_terms, axis=2, keepdims=True)).astype(jnp.bfloat16)
    latent_width = w_uv.shape[1]
    latent = jnp.einsum(
        "rhl,rlk->rhk", attn_probs, cache[:, :, :latent_width], preferred_element_type=jnp.float32
    ).astype(jnp.bfloat16)
    head_out = jnp.einsum("rhk,hkd->rhd", latent, w_uv, preferred_element_type=jnp.float32).astype(
        jnp.bfloat16
    )
    head_out = head_out.reshape(head_out.shape[0], -1)
    partial_rows = jnp.dot(
        lax.all_gather(head_out, ("side", "row"), axis=0, tiled=True),
        w_out,
        preferred_element_type=jnp.float32,
    )
    attn_slice = lax.psum_scatter(
        partial_rows.astype(jnp.bfloat16), "col", scatter_dimension=0, tiled=True
    ).astype(jnp.float32)
    hidden = residual_in.astype(jnp.float32) + attn_slice
    squares_total = lax.psum(jnp.sum(hidden * hidden, axis=1), ("side", "row"))
    inverse = lax.rsqrt(squares_total / D + 1e-06)
    normed = (hidden * inverse[:, None] * norm_gain.astype(jnp.float32)).astype(jnp.bfloat16)
    owner_index = lax.axis_index(("side", "row"))
    chosen = expert_ids == owner_index
    my_gate = jnp.sum(jnp.where(chosen, gate_vals, 0.0), axis=1)
    gate_dev = w_gate[0]
    up_dev = w_up[0]
    down_dev = w_down[0]
    full_block = lax.all_gather(normed, ("side", "row"), axis=1, tiled=True)
    row_piece = lax.all_gather(full_block, "col", axis=0, tiled=True)
    gate_part = jnp.dot(row_piece, gate_dev, preferred_element_type=jnp.float32)
    up_part = jnp.dot(row_piece, up_dev, preferred_element_type=jnp.float32)
    activations = (jax.nn.silu(gate_part) * up_part).astype(jnp.bfloat16)
    expert_rows = lax.psum_scatter(
        jnp.dot(activations, down_dev, preferred_element_type=jnp.float32).astype(jnp.bfloat16),
        "col",
        scatter_dimension=0,
        tiled=True,
    ).astype(jnp.float32)
    weighted = my_gate[:, None] * expert_rows
    expert_total = lax.psum_scatter(
        weighted.astype(jnp.bfloat16), ("side", "row"), scatter_dimension=1, tiled=True
    ).astype(jnp.float32)
    return (hidden + expert_total).astype(jnp.bfloat16)


def solution(mesh):
    placed = (
        P(("side", "row"), "col", None),
        P(("side", "row"), None, None),
        P(("side", "row")),
        P("col", None, None),
        P("col", ("side", "row")),
        P("col", ("side", "row")),
        P(("side", "row")),
        P("col", None),
        P("col", None),
        P(("side", "row"), None, "col"),
        P(("side", "row"), None, "col"),
        P(("side", "row"), "col", None),
    )
    return jax.shard_map(
        shards, mesh=mesh, in_specs=placed, out_specs=P("col", ("side", "row")), check_vma=False
    )
```

profile of v0, /device:TPU:0, one launch (start us, length us, event | category | flops | bytes accessed | tf_op | source)
XLA Modules:
  0.0 487.3 jit_solution(3034885577712282374)
XLA Ops:
  6.5 0.9 iota_compare_fusion
  7.4 0.9 copy-done
  8.3 4.7 fusion.18
  13.0 1.0 copy-done.2
  14.6 7.7 %fusion.10 = bf16[64,32,512]{2,1,0:T(8,128)(2,1)S(1)} fusion(bf16[64,128,576]{1,2,0:T(8,128)(2,1)} %param.13, f32[64,32]{1,0:T(8,128)S(1)} %fusion.30, f32[64,32,128]{2,1,0:T(8,128)} %copy-done.2), kind=kOutput, calls=%fused_computation.12 | convolution fusion | flops 270272640 | bytes 12591104 | tf_op jit(solution)/shard_map/rhl,rlk->rhk/dot_general | solution.py:35
  22.3 4.7 fusion.25
  27.0 0.9 copy.28
  28.0 39.5 %all-gather.4.cloned.1.call-done = bf16[512,4096]{1,0:T(8,128)(2,1)} async-done(((bf16[64,4096]{1,0:T(8,128)(2,1)}), bf16[512,4096]{1,0:T(8,128)(2,1)}) %all-gather.4.cloned.1.call-update) | async-done | bytes 4194320 | tf_op jit(solution)/shard_map/all_gather | solution.py:43
  67.5 9.8 %convolution_convert_fusion.1 = bf16[512,896]{1,0:T(8,128)(2,1)} fusion(bf16[512,4096]{1,0:T(8,128)(2,1)} %all-gather.4.cloned.1.call-done, bf16[4096,896]{1,0:T(8,128)(2,1)} %param.16), kind=kOutput, calls=%fused_computation.14 | convolution fusion | flops 3758555136 | bytes 12451840 | tf_op jit(solution)/shard_map/dot_general | solution.py:42
  77.3 25.2 %reduce-scatter.6.cloned.1.call-done = bf16[128,896]{1,0:T(8,128)(2,1)} async-done(((bf16[512,896]{1,0:T(8,128)(2,1)}), bf16[128,896]{1,0:T(8,128)(2,1)}) %reduce-scatter.6.cloned.1.call-update) | async-done | bytes 229392 | tf_op jit(solution)/shard_map/reduce_scatter | solution.py:47
  102.5 1.1 multiply_reduce_fusion
  103.6 14.3 %psum.7 = f32[128]{0:T(128)S(1)} all-reduce(f32[128]{0:T(128)S(1)} %multiply_reduce_fusion), channel_id=1, replica_groups=mesh['side'=2,'row'=4,'col'=4] {'side','row'}, use_global_device_ids=true, to_apply=%region_5.6 | all-reduce | flops 128 | bytes 1024 | tf_op jit(solution)/shard_map/psum | solution.py:51
  117.9 1.7 multiply_convert_fusion.1
  119.7 25.7 %all-gather.6.cloned.1.call-done = bf16[128,7168]{1,0:T(8,128)(2,1)} async-done(((bf16[128,896]{1,0:T(8,128)(2,1)}), bf16[128,7168]{1,0:T(8,128)(2,1)}) %all-gather.6.cloned.1.call-update) | async-done | bytes 1835024 | tf_op jit(solution)/shard_map/all_gather | solution.py:60
  145.7 133.7 %all-gather.8.cloned.1.call-done = bf16[512,7168]{1,0:T(8,128)(2,1)} async-done(((bf16[128,7168]{1,0:T(8,128)(2,1)}), bf16[512,7168]{1,0:T(8,128)(2,1)}) %all-gather.8.cloned.1.call-update) | async-done | bytes 7340048 | tf_op jit(solution)/shard_map/all_gather | solution.py:61
  279.4 9.3 %fusion.6 = f32[512,512]{1,0:T(8,128)S(1)} fusion(bf16[512,7168]{1,0:T(8,128)(2,1)} %all-gather.8.cloned.1.call-done, bf16[1,7168,512]{2,1,0:T(8,128)(2,1)} %param.21), kind=kOutput, calls=%fused_computation.7 | convolution fusion | flops 3758096384 | bytes 15728640 | tf_op jit(solution)/shard_map/dot_general | solution.py:62
  288.7 7.2 %fusion.19 = bf16[512,512]{1,0:T(8,128)(2,1)S(1)} fusion(bf16[512,7168]{1,0:T(8,128)(2,1)S(1)} %copy-done.8, bf16[1,7168,512]{2,1,0:T(8,128)(2,1)} %param.22, f32[512,512]{1,0:T(8,128)S(1)} %fusion.6), kind=kOutput, calls=%fused_computation.19 | convolution fusion | flops 3759669248 | bytes 16252928 | tf_op jit(solution)/shard_map/dot_general | solution.py:63
  295.8 9.1 %convolution_convert_fusion = bf16[512,7168]{1,0:T(8,128)(2,1)} fusion(bf16[512,512]{1,0:T(8,128)(2,1)S(1)} %fusion.19, bf16[1,512,7168]{2,1,0:T(8,128)(2,1)} %param.23), kind=kOutput, calls=%fused_computation.1 | convolution fusion | flops 3761766400 | bytes 15204352 | tf_op jit(solution)/shard_map/dot_general | solution.py:66
  305.7 125.4 %reduce-scatter.8.cloned.1.call-done = bf16[128,7168]{1,0:T(8,128)(2,1)} async-done(((bf16[512,7168]{1,0:T(8,128)(2,1)}), bf16[128,7168]{1,0:T(8,128)(2,1)}) %reduce-scatter.8.cloned.1.call-update) | async-done | bytes 1835024 | tf_op jit(solution)/shard_map/reduce_scatter | solution.py:65
  431.1 3.2 multiply_convert_fusion
  434.3 3.9 copy.17
  438.2 40.4 %reduce-scatter.10.cloned.1.call-done = bf16[896,128]{1,0:T(8,128)(2,1)} async-done(((bf16[7168,128]{1,0:T(8,128)(2,1)}), bf16[896,128]{1,0:T(8,128)(2,1)}) %reduce-scatter.10.cloned.1.call-update) | async-done | bytes 229392
  478.5 1.1 copy.18
  479.6 0.8 add_convert_fusion
  (32 shorter events, 1.8 us)
Async XLA Ops:
  6.5 1.8 copy-start
  6.5 60.9 %all-gather.4.cloned.1.call-start = ((), (), s32[]{:S(2)}) async-start(), calls=%async_computation.3 | async-start | bytes 4718592 | tf_op jit(solution)/shard_map/all_gather | solution.py:43
  13.0 1.0 copy-start.2
  27.9 49.4 %copy-start.5 = (bf16[896]{0:T(1024)(128)(2,1)S(1)}, bf16[896]{0:T(1024)(128)(2,1)}, u32[]{:S(2)}) copy-start(bf16[896]{0:T(1024)(128)(2,1)} %param.18) | copy-start | bytes 5380
  27.9 74.6 %copy-start.3 = (bf16[128,896]{1,0:T(8,128)(2,1)S(1)}, bf16[128,896]{1,0:T(8,128)(2,1)}, u32[]{:S(2)}) copy-start(bf16[128,896]{1,0:T(8,128)(2,1)} %param.17) | copy-start | bytes 688132
  27.9 74.6 %reduce-scatter.6.cloned.1.call-start = ((), (), s32[]{:S(2)}) async-start(), calls=%async_computation.4 | async-start | bytes 1146880 | tf_op jit(solution)/shard_map/reduce_scatter | solution.py:47
  77.3 68.2 %all-gather.6.cloned.1.call-start = ((), (), s32[]{:S(2)}) async-start(), calls=%async_computation.5 | async-start | bytes 2064384 | tf_op jit(solution)/shard_map/all_gather | solution.py:60
  119.7 159.7 %all-gather.8.cloned.1.call-start = ((), (), s32[]{:S(2)}) async-start(), calls=%async_computation.6 | async-start | bytes 9175040 | tf_op jit(solution)/shard_map/all_gather | solution.py:61
  145.5 285.6 %reduce-scatter.8.cloned.1.call-start = ((), (), s32[]{:S(2)}) async-start(), calls=%async_computation.7 | async-start | bytes 9175040 | tf_op jit(solution)/shard_map/reduce_scatter | solution.py:65
  279.4 9.3 %copy-start.8 = (bf16[512,7168]{1,0:T(8,128)(2,1)S(1)}, bf16[512,7168]{1,0:T(8,128)(2,1)}, u32[]{:S(2)}) copy-start(bf16[512,7168]{1,0:T(8,128)(2,1)} %all-gather.8.cloned.1.call-done) | copy-start | bytes 22020100
  304.9 0.7 copy-start.6
  304.9 0.7 copy-start.7
  304.9 175.5 %copy-start.1 = (bf16[64,32,576]{2,1,0:T(8,128)(2,1)S(1)}, bf16[64,32,576]{2,1,0:T(8,128)(2,1)}, u32[]{:S(2)}) copy-start(bf16[64,32,576]{2,1,0:T(8,128)(2,1)} %param.12) | copy-start | bytes 7077892
  304.9 174.7 %copy-start.4 = (bf16[128,896]{1,0:T(8,128)(2,1)S(1)}, bf16[128,896]{1,0:T(8,128)(2,1)}, u32[]{:S(2)}) copy-start(bf16[128,896]{1,0:T(8,128)(2,1)} %reduce-scatter.6.cloned.1.call-done) | copy-start | bytes 688132
  305.0 173.5 %reduce-scatter.10.cloned.1.call-start = ((), (), s32[]{:S(2)}) async-start(), calls=%async_computation.8 | async-start | bytes 2064384
Sparse Core Ops, SparseCore 0:
  28.0 39.4 all-gather.3
  77.4 25.0 reduce-scatter.5
  119.8 25.5 all-gather.5
  146.9 132.4 all-gather.7
  305.1 125.9 reduce-scatter.7
  438.3 40.1 reduce-scatter.9
where the time goes:
time: 488 us; the launch traced here: 487 us
  waiting for transfers between devices  390 us (80%)
  matrix products  52.4 us (11%)
  blocking collectives  14.3 us (3%)
  between operations  13.6 us (3%)
  local copies, waits for them, and re-layouts  8.34 us (2%)
  other arithmetic  8.29 us (2%)
    all_gather x1, waiting for transfers between devices, shards(): row_piece = lax.all_gather(full_block, 'col', axis=0, tiled=True)  134 us
    reduce_scatter x1, waiting for transfers between devices, shards(): lax.psum_scatter(jnp.dot(activations, down_dev, preferred_element_type=jn...  125 us
    unnamed x7, waiting for transfers between devices  40.5 us
    all_gather x1, waiting for transfers between devices, shards(): lax.all_gather(head_out, ('side', 'row'), axis=0, tiled=True)  39.5 us
    all_gather x1, waiting for transfers between devices, shards(): full_block = lax.all_gather(normed, ('side', 'row'), axis=1, tiled=True)  25.7 us
    reduce_scatter x1, waiting for transfers between devices, shards(): lax.psum_scatter(partial_rows.astype(jnp.bfloat16), 'col', scatter_dimens...  25.2 us
    psum x1, blocking collectives, shards(): squares_total = lax.psum(jnp.sum(hidden * hidden, axis=1), ('side', 'row'))  14.3 us
    dot_general x1, matrix products, shards(): jnp.dot(lax.all_gather(head_out, ('side', 'row'), axis=0, tiled=True), w_...  9.77 us
  transfers between devices with their start and end apart: 6, of which 6 were waited for; matrix products, arithmetic and copies ran while one was open for 0% of the time, Pallas kernels for 0%

commit v1 on v0

v1 whole, which is shorter than its diff:
```python
import functools

import jax
import jax.numpy as jnp
from jax import lax
from jax.experimental import pallas as pl
from jax.experimental.pallas import tpu as pltpu
from jax.sharding import PartitionSpec as P

ROPE = 64
EPS = 1e-06
MIB = 1024 * 1024
EXTRA = 16
ANY = pl.BlockSpec(memory_space=pl.ANY)
VMEM = pl.BlockSpec(memory_space=pltpu.VMEM)
SMEM = pl.BlockSpec(memory_space=pltpu.SMEM)


def cost(us):
    return pl.CostEstimate(flops=int(us * 1e9), bytes_accessed=1024, transcendentals=0)


LIGHT, STACK, HEAVY = cost(0.001), cost(0.5), cost(100)


def in_hbm(x):
    return pltpu.with_memory_space_constraint(x, pltpu.HBM)


def swap(x, axis, count, d):
    return lax.ppermute(x, axis, [(i, i ^ d) for i in range(count)])


def stack_kernel(n, *refs):
    pieces, (out_ref, held_ref, in_sems, out_sems) = refs[:n], refs[-4:]
    loads, stores, start = [], [], 0
    for i in range(n):
        height = pieces[i].shape[0]
        at = held_ref.at[pl.ds(start, height)]
        loads.append(pltpu.make_async_copy(pieces[i], at, in_sems.at[i]))
        stores.append(
            pltpu.make_async_copy(at, out_ref.at[pl.ds(start, height)], out_sems.at[i])
        )
        start += height
    for load in loads:
        load.start()
    for load, store in zip(loads, stores):
        load.wait()
        store.start()
    for store in stores:
        store.wait()


def stack(pieces, after, estimate=HEAVY):
    n = len(pieces)
    shape = (sum(piece.shape[0] for piece in pieces), pieces[0].shape[1])
    return pl.pallas_call(
        functools.partial(stack_kernel, n),
        in_specs=[ANY] * (n + len(after)),
        out_specs=ANY,
        out_shape=jax.ShapeDtypeStruct(shape, pieces[0].dtype),
        scratch_shapes=[
            pltpu.VMEM(shape, pieces[0].dtype),
            pltpu.SemaphoreType.DMA((n,)),
            pltpu.SemaphoreType.DMA((n,)),
        ],
        compiler_params=pltpu.CompilerParams(vmem_limit_bytes=8 * MIB),
        cost_estimate=estimate,
    )(*pieces, *after)


def hand_on_kernel(x_ref, *refs):
    refs[-1][...] = x_ref[...]


def hand_on(x, after):
    return pl.pallas_call(
        hand_on_kernel,
        in_specs=[VMEM] + [ANY] * len(after),
        out_specs=VMEM,
        out_shape=jax.ShapeDtypeStruct(x.shape, x.dtype),
        compiler_params=pltpu.CompilerParams(vmem_limit_bytes=2 * MIB),
        cost_estimate=HEAVY,
    )(x, *after)


def project_kernel(blocks, n_gate, pos_ref, near_ref, far_ref, w_hbm, *refs):
    outs, (rows_ref, w_ref, acc_ref, sems, w_sems) = refs[-5 - blocks : -5], refs[-5:]
    half, height, full = near_ref.shape
    n = 2 * half
    pieces = [near_ref.at[i] for i in range(half)] + [far_ref.at[i] for i in range(half)]
    copies = [
        pltpu.make_async_copy(
            pieces[i],
            rows_ref.at[pl.ds(pl.multiple_of(pos_ref[i] * height, height), height)],
            sems.at[i],
        )
        for i in range(n)
    ]
    depth = min(512, full)

    def load(k):
        at = pl.ds(pl.multiple_of(k * depth, depth), depth)
        return pltpu.make_async_copy(w_hbm.at[at], w_ref.at[at], w_sems.at[k])

    for copy in copies:
        copy.start()
    for k in range(full // depth):
        load(k).start()
    acc_ref[...] = jnp.zeros_like(acc_ref)
    for copy in copies:
        copy.wait()

    @pl.loop(0, full // depth)
    def _(k):
        load(k).wait()
        at = pl.ds(pl.multiple_of(k * depth, depth), depth)
        acc_ref[...] += jnp.dot(
            rows_ref[:, at], w_ref[at, :], preferred_element_type=jnp.float32
        )

    size = acc_ref.shape[0] // blocks
    for d in range(blocks):
        outs[d][:size, :] = acc_ref[d * size : (d + 1) * size, :].astype(jnp.bfloat16)
    if n_gate:
        gate_ref = refs[0]
        rest, parts = gate_ref[...], []
        for _ in range(3):
            parts.append(rest.astype(jnp.bfloat16).astype(jnp.float32))
            rest = rest - parts[-1]
        parts.append(jnp.zeros((EXTRA - 3, rest.shape[1]), jnp.float32))
        parts = jnp.concatenate(parts, axis=0).astype(jnp.bfloat16)
        for d in range(blocks):
            outs[d][size:, :] = jnp.zeros((EXTRA, outs[d].shape[1]), jnp.bfloat16)
            outs[d][size:, : rest.shape[1]] = parts


def project(near, far, places, w_out, blocks, gate, after):
    half, height, full = near.shape
    n = 2 * half
    width = w_out.shape[1]
    rows = n * height
    held = rows // blocks + EXTRA * len(gate)
    return pl.pallas_call(
        functools.partial(project_kernel, blocks, len(gate)),
        in_specs=[SMEM, ANY, ANY, ANY] + [VMEM] * len(gate) + [ANY] * len(after),
        out_specs=[VMEM] * blocks,
        out_shape=[jax.ShapeDtypeStruct((held, width), jnp.bfloat16)] * blocks,
        scratch_shapes=[
            pltpu.VMEM((rows, full), jnp.bfloat16),
            pltpu.VMEM(w_out.shape, jnp.bfloat16),
            pltpu.VMEM((rows, width), jnp.float32),
            pltpu.SemaphoreType.DMA((n,)),
            pltpu.SemaphoreType.DMA((full // min(512, full),)),
        ],
        compiler_params=pltpu.CompilerParams(vmem_limit_bytes=18 * MIB),
        cost_estimate=HEAVY,
    )(places, near, far, in_hbm(w_out), *gate, *after)


def norm_kernel(chunk, per, n, n_gate, residual_ref, gain_ref, *refs):
    pieces, outs = refs[:n], refs[len(refs) - 2 - n_gate :]
    hidden_ref, scaled_ref = outs[:2]
    rows = hidden_ref.shape[0]
    part = rows // per
    height = residual_ref.shape[0] // per
    for p in range(per):
        to = slice(p * part, (p + 1) * part)
        start = p * height + chunk * part
        hidden = residual_ref[start : start + part, :].astype(jnp.float32)
        for piece in pieces:
            hidden = hidden + piece[to, :].astype(jnp.float32)
        hidden_ref[to, :] = hidden
        scaled_ref[to, :] = (hidden * gain_ref[...].astype(jnp.float32)).astype(jnp.bfloat16)
    if n_gate:
        for d in range(n):
            parts = pieces[d][rows:, : outs[2].shape[1]].astype(jnp.float32)
            outs[2][d : d + 1, :] = parts[0:1] + parts[1:2] + parts[2:3]


def norm(residual, gain, pieces, chunk, per, n_gate, after):
    n = len(pieces)
    block, width = residual.shape
    shape = (pieces[0].shape[0] - EXTRA * n_gate, width)
    return pl.pallas_call(
        functools.partial(norm_kernel, chunk, per, n, n_gate),
        in_specs=[VMEM] * (n + 2) + [ANY] * len(after),
        out_specs=[VMEM] * (2 + n_gate),
        out_shape=[
            jax.ShapeDtypeStruct(shape, jnp.float32),
            jax.ShapeDtypeStruct(shape, jnp.bfloat16),
        ]
        + [jax.ShapeDtypeStruct((n, block), jnp.float32)] * n_gate,
        compiler_params=pltpu.CompilerParams(vmem_limit_bytes=4 * MIB),
        cost_estimate=HEAVY,
    )(residual, gain[None, :], *pieces, *after)


def gate_up_kernel(n_ref, idx_ref, *refs):
    pieces = []
    for ref in refs[:n_ref]:
        pieces += [ref] if len(ref.shape) == 2 else [ref.at[i] for i in range(ref.shape[0])]
    n = len(pieces)
    wg_hbm, wu_hbm, weight_ref = refs[n_ref : n_ref + 3]
    out_ref, x_ref, wg_ref, wu_ref, g_ref, u_ref, sq_ref, sems, wg_sems, wu_sems = refs[-10:]
    width = pieces[0].shape[1]
    rows = out_ref.shape[0]

    def load(i):
        at = pl.ds(pl.multiple_of(idx_ref[i] * width, width), width)
        return (
            pltpu.make_async_copy(wg_hbm.at[at], wg_ref.at[i], wg_sems.at[i]),
            pltpu.make_async_copy(wu_hbm.at[at], wu_ref.at[i], wu_sems.at[i]),
        )

    for i in range(n):
        pltpu.make_async_copy(pieces[i], x_ref.at[i], sems.at[i]).start()
        for copy in load(i):
            copy.start()
    g_ref[...] = jnp.zeros_like(g_ref)
    u_ref[...] = jnp.zeros_like(u_ref)
    sq_ref[...] = jnp.zeros_like(sq_ref)

    @pl.loop(0, n)
    def _(i):
        pltpu.make_async_copy(pieces[0], x_ref.at[i], sems.at[i]).wait()
        x = x_ref[i, :rows, :]
        inverse_gain = 1.0 / x_ref[i, rows:, :][0:1].astype(jnp.float32)
        for copy in load(i):
            copy.wait()
        g_ref[...] += jnp.dot(x, wg_ref[i], preferred_element_type=jnp.float32)
        u_ref[...] += jnp.dot(x, wu_ref[i], preferred_element_type=jnp.float32)
        hidden = x.astype(jnp.float32) * inverse_gain
        sq_ref[...] += jnp.sum(hidden * hidden, axis=1, keepdims=True)

    inv = lax.rsqrt(sq_ref[...] / (n * width) + EPS)
    g = g_ref[...] * inv
    u = u_ref[...] * inv
    out_ref[...] = (g / (1.0 + jnp.exp(-g)) * u * weight_ref[...]).astype(jnp.bfloat16)


def gate_up(pieces, owners, w_gate, w_up, weight):
    n = owners.shape[0]
    held, width = pieces[0].shape[-2:]
    rows = held - EXTRA
    full, units = w_gate.shape
    return pl.pallas_call(
        functools.partial(gate_up_kernel, len(pieces)),
        in_specs=[SMEM] + [ANY] * (len(pieces) + 2) + [VMEM],
        out_specs=VMEM,
        out_shape=jax.ShapeDtypeStruct((rows, units), jnp.bfloat16),
        scratch_shapes=[
            pltpu.VMEM((n, held, width), jnp.bfloat16),
            pltpu.VMEM((n, width, units), jnp.bfloat16),
            pltpu.VMEM((n, width, units), jnp.bfloat16),
            pltpu.VMEM((rows, units), jnp.float32),
            pltpu.VMEM((rows, units), jnp.float32),
            pltpu.VMEM((rows, 1), jnp.float32),
            pltpu.SemaphoreType.DMA((n,)),
            pltpu.SemaphoreType.DMA((n,)),
            pltpu.SemaphoreType.DMA((n,)),
        ],
        compiler_params=pltpu.CompilerParams(vmem_limit_bytes=30 * MIB),
        cost_estimate=HEAVY,
    )(owners, *pieces, in_hbm(w_gate), in_hbm(w_up), weight)


def down_kernel(idx_ref, act_ref, w_ref, out_ref):
    m, _, width = out_ref.shape

    @pl.loop(0, m)
    def _(j):
        at = pl.ds(pl.multiple_of(idx_ref[j] * width, 128), width)
        out_ref[j] = jnp.dot(
            act_ref[...], w_ref[:, at], preferred_element_type=jnp.float32
        ).astype(jnp.bfloat16)


def down(act, owners, w_down, width):
    rows, units = act.shape
    m = owners.shape[0]
    if width % 128:
        cut = [
            lax.dynamic_slice_in_dim(w_down, owners[j] * width, width, axis=1) for j in range(m)
        ]
        return jnp.stack(
            [jnp.dot(act, w, preferred_element_type=jnp.float32).astype(jnp.bfloat16) for w in cut]
        )
    return pl.pallas_call(
        down_kernel,
        in_specs=[SMEM, VMEM, VMEM],
        out_specs=VMEM,
        out_shape=jax.ShapeDtypeStruct((m, rows, width), jnp.bfloat16),
        compiler_params=pltpu.CompilerParams(vmem_limit_bytes=8 * MIB),
        cost_estimate=HEAVY,
    )(owners, act, w_down)


def combine_kernel(n, near_ref, got_ref, *refs):
    outs = refs
    for d in range(n):
        both = near_ref[d].astype(jnp.float32) + got_ref[d].astype(jnp.float32)
        outs[d][...] = both.astype(outs[d].dtype)


def combine(near, got):
    n, rows, width = near.shape
    return pl.pallas_call(
        functools.partial(combine_kernel, n),
        in_specs=[VMEM] * 2,
        out_specs=[VMEM] * n,
        out_shape=[
            jax.ShapeDtypeStruct((rows, width), jnp.bfloat16 if d else jnp.float32)
            for d in range(n)
        ],
        compiler_params=pltpu.CompilerParams(vmem_limit_bytes=12 * MIB),
        cost_estimate=HEAVY,
    )(near, got)


def reduce_kernel(n, blocks, *refs):
    pieces, outs = refs[:n], refs[-blocks:]
    size = outs[0].shape[0]
    for b in range(blocks):
        at = slice(b * size, (b + 1) * size)
        total = pieces[0][at, :]
        for piece in pieces[1:]:
            total = total + piece[at, :].astype(jnp.float32)
        outs[b][...] = total.astype(outs[b].dtype)


def reduce(pieces, blocks, after):
    n = len(pieces)
    rows, width = pieces[0].shape
    return pl.pallas_call(
        functools.partial(reduce_kernel, n, blocks),
        in_specs=[VMEM] * n + [ANY] * len(after),
        out_specs=[VMEM] * blocks,
        out_shape=[
            jax.ShapeDtypeStruct((rows // blocks, width), jnp.bfloat16 if b else jnp.float32)
            for b in range(blocks)
        ],
        compiler_params=pltpu.CompilerParams(vmem_limit_bytes=8 * MIB),
        cost_estimate=HEAVY,
    )(*pieces, *after)


def finish_kernel(chunks, per, n, *refs):
    out_ref = refs[-1]
    part = out_ref.shape[0] // (chunks * per)
    for c in range(chunks):
        pieces = refs[c * n : (c + 1) * n]
        for p in range(per):
            at = slice(p * part, (p + 1) * part)
            total = pieces[0][at, :]
            for piece in pieces[1:]:
                total = total + piece[at, :].astype(jnp.float32)
            start = (p * chunks + c) * part
            out_ref[start : start + part, :] = total.astype(jnp.bfloat16)


def finish(terms, per):
    chunks, n = len(terms), len(terms[0])
    rows, width = terms[0][0].shape
    return pl.pallas_call(
        functools.partial(finish_kernel, chunks, per, n),
        in_specs=[VMEM] * (chunks * n),
        out_specs=VMEM,
        out_shape=jax.ShapeDtypeStruct((chunks * rows, width), jnp.bfloat16),
        compiler_params=pltpu.CompilerParams(vmem_limit_bytes=8 * MIB),
        cost_estimate=HEAVY,
    )(*[x for chunk in terms for x in chunk])


def attend_kernel(scale, chunk, len_ref, q_ref, c_ref, w_hbm, *refs):
    out_ref, w_ref, score_ref, prob_ref, lat_ref, sem = refs[-6:]
    step, steps = pl.program_id(0), pl.num_programs(0)
    group, heads, _ = q_ref.shape
    slots = c_ref.shape[2]
    _, latent_width, size = w_ref.shape
    load = pltpu.make_async_copy(w_hbm, w_ref, sem)

    @pl.when(step == 0)
    def _():
        load.start()

    places = lax.broadcasted_iota(jnp.int32, (heads, slots), 1)
    for r in range(group):
        scores = jnp.dot(q_ref[r], c_ref[r], preferred_element_type=jnp.float32) * scale
        live = len_ref[(chunk * steps + step) * group + r]
        score_ref[r * heads : (r + 1) * heads, :] = jnp.where(places < live, scores, -jnp.inf)
    scores = score_ref[...]
    exp_terms = jnp.exp(scores - jnp.max(scores, axis=1, keepdims=True))
    probs = exp_terms / jnp.sum(exp_terms, axis=1, keepdims=True)
    prob_ref[...] = probs.astype(jnp.bfloat16)
    for r in range(group):
        latent = lax.dot_general(
            prob_ref[r * heads : (r + 1) * heads, :],
            c_ref[r, :latent_width, :],
            (((1,), (1,)), ((), ())),
            preferred_element_type=jnp.float32,
        )
        at = pl.ds(pl.multiple_of((step * group + r) * heads, heads), heads)
        for k in range(latent_width // 128):
            lat_ref[k, at, :] = latent[:, k * 128 : (k + 1) * 128]

    @pl.when(step == steps - 1)
    def _():
        load.wait()
        for h in range(heads):
            at = pl.ds(h, out_ref.shape[0], stride=heads)
            latent = jnp.concatenate(
                [lat_ref[k, at, :] for k in range(latent_width // 128)], axis=1
            ).astype(jnp.bfloat16)
            out_ref[:, h * size : (h + 1) * size] = jnp.dot(
                latent, w_ref[h], preferred_element_type=jnp.float32
            ).astype(jnp.bfloat16)


def attend(queries, cache, lengths, w_uv, chunk, chunks, after):
    rows, heads, entries = queries.shape
    slots = cache.shape[1]
    _, latent_width, size = w_uv.shape
    group = 16
    steps = rows // chunks // group
    return pl.pallas_call(
        functools.partial(attend_kernel, (size + ROPE) ** (-0.5), chunk),
        grid_spec=pltpu.PrefetchScalarGridSpec(
            num_scalar_prefetch=1,
            grid=(steps,),
            in_specs=[
                pl.BlockSpec((group, heads, entries), lambda i, _: (chunk * steps + i, 0, 0)),
                pl.BlockSpec((group, entries, slots), lambda i, _: (chunk * steps + i, 0, 0)),
                ANY,
            ]
            + [ANY] * len(after),
            out_specs=pl.BlockSpec((steps * group, heads * size), lambda i, _: (0, 0)),
            scratch_shapes=[
                pltpu.VMEM(w_uv.shape, jnp.bfloat16),
                pltpu.VMEM((group * heads, slots), jnp.float32),
                pltpu.VMEM((group * heads, slots), jnp.bfloat16),
                pltpu.VMEM((latent_width // 128, steps * group * heads, 128), jnp.float32),
                pltpu.SemaphoreType.DMA,
            ],
        ),
        out_shape=jax.ShapeDtypeStruct((steps * group, heads * size), jnp.bfloat16),
        compiler_params=pltpu.CompilerParams(vmem_limit_bytes=20 * MIB),
        cost_estimate=HEAVY,
    )(
        lengths,
        in_hbm(queries),
        in_hbm(jnp.swapaxes(cache, 1, 2)),
        in_hbm(w_uv),
        *after,
    )


def shards(
    n_row,
    n_col,
    queries,
    cache,
    lengths,
    w_uv,
    w_out,
    residual_in,
    norm_gain,
    expert_ids,
    gate_vals,
    w_gate,
    w_up,
    w_down,
):
    side, row, col = lax.axis_index("side"), lax.axis_index("row"), lax.axis_index("col")
    block, width = residual_in.shape
    height = queries.shape[0]
    per = block // height
    chunks = 2
    part = height // chunks
    owners = jnp.stack(
        [(side ^ ds) * n_row + (row ^ d) for ds in range(2) for d in range(n_row)]
    ).astype(jnp.int32)
    places = (((owners // per) ^ col) * per + owners % per).astype(jnp.int32)

    chosen = expert_ids == owners[0]
    my_gate = jnp.sum(jnp.where(chosen, gate_vals, 0.0), axis=1)[None, :]
    gain = jnp.broadcast_to(norm_gain, (EXTRA, width))

    first = attend(queries, cache, lengths, w_uv, 0, chunks, [])
    second = attend(queries, cache, lengths, w_uv, 1, chunks, [first])
    gate_dev, up_dev, down_dev = w_gate[0], w_up[0], w_down[0]

    def over_col(pieces):
        return [pieces[0]] + [swap(pieces[d], "col", n_col, d) for d in range(1, n_col)]

    def over_row(pieces):
        return [pieces[0]] + [swap(pieces[d], "row", n_row, d) for d in range(1, n_row)]

    def other_core(x):
        return swap(x, "side", 2, 1)

    def experts(near, held):
        far = [other_core(piece) for piece in near]
        act = gate_up(near + far, owners, gate_dev, up_dev, held)
        far_rows = down(act, owners[n_row:], down_dev, width)
        near_rows = down(act, owners[:n_row], down_dev, width)
        return combine(near_rows, other_core(far_rows))

    def stack_rows(x, after, estimate=HEAVY):
        return stack(over_row([x] * n_row), after, estimate).reshape(n_row, *x.shape)

    near_0 = stack_rows(first, [second], STACK)
    partial_0 = project(near_0, other_core(near_0), places, w_out, n_col, [], [])
    near_1 = stack_rows(second, partial_0[:1], STACK)
    hidden_0, scaled_0 = norm(residual_in, norm_gain, over_col(partial_0), 0, per, 0, [])
    partial_1 = project(near_1, other_core(near_1), places, w_out, n_col, [my_gate], [scaled_0])
    rows_0 = stack(over_col([scaled_0] * n_col) + [gain], partial_1[:1])
    hidden_1, scaled_1, gates = norm(
        residual_in, norm_gain, over_col(partial_1), 1, per, 1, [rows_0]
    )
    weight = gates.reshape(n_col, per, chunks, part)
    weight = [weight[:, :, c].reshape(-1, 1) for c in range(chunks)]
    near_0 = over_row([rows_0] * n_row)
    both_0 = experts(near_0, weight[0])
    rows_1 = stack(over_col([scaled_1] * n_col) + [gain], near_0[1:])
    near_1 = stack_rows(rows_1, both_0[:1])
    both_1 = experts([near_1], hand_on(weight[1], [near_1]))
    total_0 = reduce(over_row(both_0), n_col, both_1[:1])
    total_1 = reduce(over_row(both_1), n_col, [])
    terms = [[hidden_0, *over_col(total_0)], [hidden_1, *over_col(total_1)]]
    return finish(terms, per)


def solution(mesh):
    placed = (
        P(("side", "row"), "col", None),
        P(("side", "row"), None, None),
        P(("side", "row")),
        P("col", None, None),
        P("col", ("side", "row")),
        P("col", ("side", "row")),
        P(("side", "row")),
        P("col", None),
        P("col", None),
        P(("side", "row"), None, "col"),
        P(("side", "row"), None, "col"),
        P(("side", "row"), "col", None),
    )
    return jax.shard_map(
        functools.partial(shards, mesh.shape["row"], mesh.shape["col"]),
        mesh=mesh,
        in_specs=placed,
        out_specs=P("col", ("side", "row")),
        check_vma=False,
    )
```

time: 488 us -> 170 us (0.35)
  waiting for transfers between devices: 390 us -> 48.2 us
  Pallas kernels: 0 us -> 65.4 us
  starting transfers between devices: 0.39 us -> 54.5 us
  matrix products: 52.4 us -> 0 us
  blocking collectives: 14.3 us -> 0 us
  between operations: 13.6 us -> 0.31 us
  other arithmetic: 8.29 us -> 0.19 us
  local copies, waits for them, and re-layouts: 8.34 us -> 1.15 us
    all_gather x3 -> x0, waiting for transfers between devices: 199 us -> none  [the longest x1 134 us: shards(): row_piece = lax.all_gather(full_block, 'col', axis=0, tiled=True)]
    reduce_scatter x2 -> x0, waiting for transfers between devices: 151 us -> none  [the longest x1 125 us: shards(): lax.psum_scatter(jnp.dot(activations, down_dev, preferred_element_type=jn...]
    pallas_call x0 -> x23, Pallas kernels: none -> 65.4 us  [the longest x2 19.4 us: gate_up(): pl.pallas_call(functools.partial(gate_up_kernel, len(pieces)), in_specs=[...]
    ppermute x0 -> x45, starting transfers between devices: none -> 54.5 us  [swap(): return lax.ppermute(x, axis, [(i, i ^ d) for i in range(count)])]
    dot_general x7 -> x0, matrix products: 52.4 us -> none  [the longest x1 9.77 us: shards(): jnp.dot(lax.all_gather(head_out, ('side', 'row'), axis=0, tiled=True), w_...]
    ppermute x0 -> x45, waiting for transfers between devices: none -> 48.2 us  [swap(): return lax.ppermute(x, axis, [(i, i ^ d) for i in range(count)])]
    unnamed x7 -> x0, waiting for transfers between devices: 40.5 us -> none
    psum x1 -> x0, blocking collectives: 14.3 us -> none  [shards(): squares_total = lax.psum(jnp.sum(hidden * hidden, axis=1), ('side', 'row'))]
  transfers between devices with their start and end apart: 6 -> 45, of which waited for: 6 -> 18; matrix products, arithmetic and copies ran while one was open for 0% -> 0% of each run, Pallas kernels for 0% -> 32%
where the time goes in v1:
time: 170 us
  Pallas kernels  65.4 us (38%)
  starting transfers between devices  54.5 us (32%)
  waiting for transfers between devices  48.2 us (28%)
    ppermute x45, starting transfers between devices, swap(): return lax.ppermute(x, axis, [(i, i ^ d) for i in range(count)])  54.5 us
    ppermute x45, waiting for transfers between devices, swap(): return lax.ppermute(x, axis, [(i, i ^ d) for i in range(count)])  48.2 us
    pallas_call x2, Pallas kernels, gate_up(): pl.pallas_call(functools.partial(gate_up_kernel, len(pieces)), in_specs=[...  19.4 us
    pallas_call x2, Pallas kernels, attend(): pl.pallas_call(functools.partial(attend_kernel, (size + ROPE) ** (-0.5),...  15.4 us
    pallas_call x2, Pallas kernels, project(): pl.pallas_call(functools.partial(project_kernel, blocks, len(gate)), in_s...  11.2 us
    pallas_call x4, Pallas kernels, down(): pl.pallas_call(down_kernel, in_specs=[SMEM, VMEM, VMEM], out_specs=VMEM,...  9.52 us
    pallas_call x5, Pallas kernels, stack(): pl.pallas_call(functools.partial(stack_kernel, n), in_specs=[ANY] * (n +...  5.62 us
  transfers between devices with their start and end apart: 45, of which 18 were waited for; matrix products, arithmetic and copies ran while one was open for 0% of the time, Pallas kernels for 32%

profile of v1, /device:TPU:0, one launch (start us, length us, event | category | flops | bytes accessed | tf_op | source)
XLA Modules:
  0.0 169.8 jit_solution(12326257006682433254)
XLA Ops:
  0.7 7.7 %shard_map.118.refs_0_ = bf16[32,4096]{1,0:T(8,128)(2,1)S(1)} custom-call(s32[64]{0:T(128)S(1)} %copy-done.3, bf16[64,32,576]{2,1,0:T(8,128)(2,1)} %q_ref.3, bf16[64,576,128]{2,1,0:T(8,128)(2,1)} %bitcast.36, bf16[32,512,128]{2,1,0:T(8,128)(2,1)} %w_hbm.5), custom_call_target="tpu_custom_call" | custom-call | flops 99999997952 | bytes 1024 | tf_op jit(solution)/shard_map/pallas_call | solution.py:426
  8.3 4.0 %collective-permute-start.2 = (bf16[32,4096]{1,0:T(8,128)(2,1)S(1)}, bf16[32,4096]{1,0:T(8,128)(2,1)S(1)}, u32[]{:S(2)}, u32[]{:S(2)}) collective-permute-start(bf16[32,4096]{1,0:T(8,128)(2,1)S(1)} %shard_map.118.refs_0_), channel_id=1, source_target_pairs={{0,12},{4,8},{8,4},{12,0},{1,13},{5,9},{9,5},{13,1},{2,14},{6,10},... | collective-permute-start | bytes 786440 | tf_op jit(solution)/shard_map/ppermute | solution.py:31
  12.9 7.7 %shard_map.119.refs_4_.refs_0_ = bf16[32,4096]{1,0:T(8,128)(2,1)S(1)} custom-call(s32[64]{0:T(128)S(1)} %copy-done.3, bf16[64,32,576]{2,1,0:T(8,128)(2,1)} %q_ref.3, bf16[64,576,128]{2,1,0:T(8,128)(2,1)} %bitcast.37, bf16[32,512,128]{2,1,0:T(8,128)(2,1)} %w_hbm.5, bf16[32,4096]{1,0:T(8,128)(2,1)S(1)} %shard_map.118.refs_0_), custom_call_target="tpu_custom_call" | custom-call | flops 99999997952 | bytes 1024 | tf_op jit(solution)/shard_map/pallas_call | solution.py:426
  20.6 3.6 %collective-permute-done.1.refs_2_ = bf16[32,4096]{1,0:T(8,128)(2,1)S(1)} collective-permute-done((bf16[32,4096]{1,0:T(8,128)(2,1)S(1)}, bf16[32,4096]{1,0:T(8,128)(2,1)S(1)}, u32[]{:S(2)}, u32[]{:S(2)}) %collective-permute-start.1) | collective-permute-done | bytes 262176 | tf_op jit(solution)/shard_map/ppermute | solution.py:31
  28.5 5.6 %shard_map.121 = (bf16[64,896]{1,0:T(8,128)(2,1)S(1)}, bf16[64,896]{1,0:T(8,128)(2,1)S(1)}, bf16[64,896]{1,0:T(8,128)(2,1)S(1)}, bf16[64,896]{1,0:T(8,128)(2,1)S(1)}) custom-call(s32[8]{0:T(128)S(1)} %fusion.pos_ref, bf16[4,32,4096]{2,1,0:T(8,128)(2,1)S(1)} %bitcast.23, bf16[4,32,4096]{2,1,0:T(8,128)(2,1)S(1)} %collective-permute-done.3.far_ref, ...), custom_call_target="tpu_custom_call" | custom-call | flops 99999997952 | bytes 1024 | tf_op jit(solution)/shard_map/pallas_call | solution.py:144
  35.8 2.6 %collective-permute-start.5 = (bf16[64,896]{1,0:T(8,128)(2,1)S(1)}, bf16[64,896]{1,0:T(8,128)(2,1)S(1)}, u32[]{:S(2)}, u32[]{:S(2)}) collective-permute-start(bf16[64,896]{1,0:T(8,128)(2,1)S(1)} %get-tuple-element.36), channel_id=1, source_target_pairs={{0,2},{1,3},{2,0},{3,1},{4,6},{5,7},{6,4},{7,5},{8,10},{9,11},{10,... | collective-permute-start | bytes 344072 | tf_op jit(solution)/shard_map/ppermute | solution.py:31
  40.4 6.8 %collective-permute-done.5.refs_2_ = bf16[64,896]{1,0:T(8,128)(2,1)S(1)} collective-permute-done((bf16[64,896]{1,0:T(8,128)(2,1)S(1)}, bf16[64,896]{1,0:T(8,128)(2,1)S(1)}, u32[]{:S(2)}, u32[]{:S(2)}) %collective-permute-start.5) | collective-permute-done | bytes 114720 | tf_op jit(solution)/shard_map/ppermute | solution.py:31
  47.4 2.5 %collective-permute-start.9 = (bf16[64,896]{1,0:T(8,128)(2,1)S(1)}, bf16[64,896]{1,0:T(8,128)(2,1)S(1)}, u32[]{:S(2)}, u32[]{:S(2)}) collective-permute-start(bf16[64,896]{1,0:T(8,128)(2,1)S(1)} %get-tuple-element.39.refs_1_.refs_0_), channel_id=1, source_target_pairs={{0,3},{1,2},{2,1},{3,0},{4,7},{5,6},{6,5},{7,4},{8,11},{9,10},{10,... | collective-permute-start | bytes 344072 | tf_op jit(solution)/shard_map/ppermute | solution.py:31
  52.0 5.6 %shard_map.124 = (bf16[80,896]{1,0:T(8,128)(2,1)S(1)}, bf16[80,896]{1,0:T(8,128)(2,1)S(1)}, bf16[80,896]{1,0:T(8,128)(2,1)S(1)}, bf16[80,896]{1,0:T(8,128)(2,1)S(1)}) custom-call(s32[8]{0:T(128)S(1)} %fusion.pos_ref, bf16[4,32,4096]{2,1,0:T(8,128)(2,1)S(1)} %bitcast.25, bf16[4,32,4096]{2,1,0:T(8,128)(2,1)S(1)} %collective-permute-done.13.far_ref, ...), custom_call_target="tpu_custom_call" | custom-call | flops 99999997952 | bytes 1024 | tf_op jit(solution)/shard_map/pallas_call | solution.py:144
  67.1 4.2 %collective-permute-done.22.refs_2_ = bf16[80,896]{1,0:T(8,128)(2,1)S(1)} collective-permute-done((bf16[80,896]{1,0:T(8,128)(2,1)S(1)}, bf16[80,896]{1,0:T(8,128)(2,1)S(1)}, u32[]{:S(2)}, u32[]{:S(2)}) %collective-permute-start.22) | collective-permute-done | bytes 143392 | tf_op jit(solution)/shard_map/ppermute | solution.py:31
  71.4 2.5 %collective-permute-start.30 = (bf16[64,896]{1,0:T(8,128)(2,1)S(1)}, bf16[64,896]{1,0:T(8,128)(2,1)S(1)}, u32[]{:S(2)}, u32[]{:S(2)}) collective-permute-start(bf16[64,896]{1,0:T(8,128)(2,1)S(1)} %get-tuple-element.49.refs_0_), channel_id=1, source_target_pairs={{0,3},{1,2},{2,1},{3,0},{4,7},{5,6},{6,5},{7,4},{8,11},{9,10},{10,... | collective-permute-start | bytes 344072 | tf_op jit(solution)/shard_map/ppermute | solution.py:31
  75.3 3.6 %collective-permute-done.30.refs_3_ = bf16[64,896]{1,0:T(8,128)(2,1)S(1)} collective-permute-done((bf16[64,896]{1,0:T(8,128)(2,1)S(1)}, bf16[64,896]{1,0:T(8,128)(2,1)S(1)}, u32[]{:S(2)}, u32[]{:S(2)}) %collective-permute-start.30) | collective-permute-done | bytes 114720 | tf_op jit(solution)/shard_map/ppermute | solution.py:31
  78.9 3.4 %collective-permute-start.28 = (bf16[64,896]{1,0:T(8,128)(2,1)S(1)}, bf16[64,896]{1,0:T(8,128)(2,1)S(1)}, u32[]{:S(2)}, u32[]{:S(2)}) collective-permute-start(bf16[64,896]{1,0:T(8,128)(2,1)S(1)} %get-tuple-element.49.refs_0_), channel_id=1, source_target_pairs={{0,1},{1,0},{2,3},{3,2},{4,5},{5,4},{6,7},{7,6},{8,9},{9,8},{10,11... | collective-permute-start | bytes 344072 | tf_op jit(solution)/shard_map/ppermute | solution.py:31
  90.1 9.7 %shard_map.127.act_ref = bf16[256,512]{1,0:T(8,128)(2,1)S(1)} custom-call(s32[8]{0:T(128)S(1)} %stack.39.idx_ref, bf16[272,896]{1,0:T(8,128)(2,1)S(1)} %shard_map.125.refs_4_.refs_0_, bf16[272,896]{1,0:T(8,128)(2,1)S(1)} %collective-permute-done.14.refs_1_.refs_5_, bf16[272,896]{1,0:T(8,128)(2,1)S(1)} %collective-permute-done.15.refs_2_.refs_6_, ...), custom_call_target="tpu_custom_call" | custom-call | flops 99999997952 | bytes 1024 | tf_op jit(solution)/shard_map/pallas_call | solution.py:247
  99.8 2.5 %shard_map.129 = bf16[4,256,896]{2,1,0:T(8,128)(2,1)S(1)} custom-call(s32[4]{0:T(128)S(1)} %pad_add_fusion.1.idx_ref, bf16[256,512]{1,0:T(8,128)(2,1)S(1)} %shard_map.127.act_ref, bf16[512,7168]{1,0:T(8,128)(2,1)S(1)} %bitcast.27), custom_call_target="tpu_custom_call" | custom-call | flops 99999997952 | bytes 1024 | tf_op jit(solution)/shard_map/pallas_call | solution.py:289
  102.4 2.3 %shard_map.128.near_ref = bf16[4,256,896]{2,1,0:T(8,128)(2,1)S(1)} custom-call(s32[4]{0:T(128)S(1)} %pad_add_fusion.idx_ref, bf16[256,512]{1,0:T(8,128)(2,1)S(1)} %shard_map.127.act_ref, bf16[512,7168]{1,0:T(8,128)(2,1)S(1)} %bitcast.28), custom_call_target="tpu_custom_call" | custom-call | flops 99999997952 | bytes 1024 | tf_op jit(solution)/shard_map/pallas_call | solution.py:289
  107.4 3.2 %collective-permute-done.32.refs_2_ = bf16[272,896]{1,0:T(8,128)(2,1)} collective-permute-done((bf16[272,896]{1,0:T(8,128)(2,1)}, bf16[272,896]{1,0:T(8,128)(2,1)}, u32[]{:S(2)}, u32[]{:S(2)}) %collective-permute-start.32) | collective-permute-done | bytes 487456 | tf_op jit(solution)/shard_map/ppermute | solution.py:31
  110.6 2.3 %shard_map.132 = bf16[1088,896]{1,0:T(8,128)(2,1)S(1)} custom-call(bf16[272,896]{1,0:T(8,128)(2,1)} %shard_map.131.refs_0_, bf16[272,896]{1,0:T(8,128)(2,1)} %collective-permute-done.31.refs_1_, bf16[272,896]{1,0:T(8,128)(2,1)} %collective-permute-done.32.refs_2_, bf16[272,896]{1,0:T(8,128)(2,1)} %collective-permute-done.33.refs_3_, ...), custom_call_target="tpu_custom_call" | custom-call | flops 99999997952 | bytes 1024 | tf_op jit(solution)/shard_map/pallas_call | solution.py:57
  117.0 9.7 %shard_map.134.act_ref = bf16[256,512]{1,0:T(8,128)(2,1)S(1)} custom-call(s32[8]{0:T(128)S(1)} %stack.39.idx_ref, bf16[4,272,896]{2,1,0:T(8,128)(2,1)S(1)} %bitcast.33, bf16[4,272,896]{2,1,0:T(8,128)(2,1)S(1)} %collective-permute-done.34.refs_1_, bf16[7168,512]{1,0:T(8,128)(2,1)} %bitcast.39, bf16[7168,512]{1,0:T(8,128)(2,1)} %bitcast.41, ...), custom_call_target="tpu_custom_call" | custom-call | flops 99999997952 | bytes 1024 | tf_op jit(solution)/shard_map/pallas_call | solution.py:247
  126.7 2.3 %shard_map.136 = bf16[4,256,896]{2,1,0:T(8,128)(2,1)S(1)} custom-call(s32[4]{0:T(128)S(1)} %pad_add_fusion.1.idx_ref, bf16[256,512]{1,0:T(8,128)(2,1)S(1)} %shard_map.134.act_ref, bf16[512,7168]{1,0:T(8,128)(2,1)S(1)} %bitcast.29), custom_call_target="tpu_custom_call" | custom-call | flops 99999997952 | bytes 1024 | tf_op jit(solution)/shard_map/pallas_call | solution.py:289
  142.0 4.7 %collective-permute-done.39.refs_1_ = bf16[256,896]{1,0:T(8,128)(2,1)S(1)} collective-permute-done((bf16[256,896]{1,0:T(8,128)(2,1)S(1)}, bf16[256,896]{1,0:T(8,128)(2,1)S(1)}, u32[]{:S(2)}, u32[]{:S(2)}) %collective-permute-start.39) | collective-permute-done | bytes 458784 | tf_op jit(solution)/shard_map/ppermute | solution.py:31
  146.7 2.4 %collective-permute-start.38 = (bf16[64,896]{1,0:T(8,128)(2,1)S(1)}, bf16[64,896]{1,0:T(8,128)(2,1)S(1)}, u32[]{:S(2)}, u32[]{:S(2)}) collective-permute-start(bf16[64,896]{1,0:T(8,128)(2,1)S(1)} %get-tuple-element.54), channel_id=1, source_target_pairs={{0,3},{1,2},{2,1},{3,0},{4,7},{5,6},{6,5},{7,4},{8,11},{9,10},{10,... | collective-permute-start | bytes 344072 | tf_op jit(solution)/shard_map/ppermute | solution.py:31
  149.1 7.8 %collective-permute-done.40.refs_2_ = bf16[256,896]{1,0:T(8,128)(2,1)S(1)} collective-permute-done((bf16[256,896]{1,0:T(8,128)(2,1)S(1)}, bf16[256,896]{1,0:T(8,128)(2,1)S(1)}, u32[]{:S(2)}, u32[]{:S(2)}) %collective-permute-start.40) | collective-permute-done | bytes 458784 | tf_op jit(solution)/shard_map/ppermute | solution.py:31
  162.8 6.1 %collective-permute-done.43.refs_8_ = bf16[64,896]{1,0:T(8,128)(2,1)S(1)} collective-permute-done((bf16[64,896]{1,0:T(8,128)(2,1)S(1)}, bf16[64,896]{1,0:T(8,128)(2,1)S(1)}, u32[]{:S(2)}, u32[]{:S(2)}) %collective-permute-start.43) | collective-permute-done | bytes 114720 | tf_op jit(solution)/shard_map/ppermute | solution.py:31
  (116 shorter events, 56.5 us)
Async XLA Ops:
  8.3 12.3 %collective-permute-start.2 = (bf16[32,4096]{1,0:T(8,128)(2,1)S(1)}, bf16[32,4096]{1,0:T(8,128)(2,1)S(1)}, u32[]{:S(2)}, u32[]{:S(2)}) collective-permute-start(bf16[32,4096]{1,0:T(8,128)(2,1)S(1)} %shard_map.118.refs_0_), channel_id=1, source_target_pairs={{0,12},{4,8},{8,4},{12,0},{1,13},{5,9},{9,5},{13,1},{2,14},{6,10},... | collective-permute-start | bytes 786440 | tf_op jit(solution)/shard_map/ppermute | solution.py:31
  12.3 11.9 %collective-permute-start.1 = (bf16[32,4096]{1,0:T(8,128)(2,1)S(1)}, bf16[32,4096]{1,0:T(8,128)(2,1)S(1)}, u32[]{:S(2)}, u32[]{:S(2)}) collective-permute-start(bf16[32,4096]{1,0:T(8,128)(2,1)S(1)} %shard_map.118.refs_0_), channel_id=1, source_target_pairs={{0,8},{4,12},{8,0},{12,4},{1,9},{5,13},{9,1},{13,5},{2,10},{6,14},... | collective-permute-start | bytes 786440 | tf_op jit(solution)/shard_map/ppermute | solution.py:31
  24.8 13.6 %collective-permute-start.12 = (bf16[32,4096]{1,0:T(8,128)(2,1)S(1)}, bf16[32,4096]{1,0:T(8,128)(2,1)S(1)}, u32[]{:S(2)}, u32[]{:S(2)}) collective-permute-start(bf16[32,4096]{1,0:T(8,128)(2,1)S(1)} %shard_map.119.refs_4_.refs_0_), channel_id=1, source_target_pairs={{0,12},{4,8},{8,4},{12,0},{1,13},{5,9},{9,5},{13,1},{2,14},{6,10},... | collective-permute-start | bytes 786440 | tf_op jit(solution)/shard_map/ppermute | solution.py:31
  26.4 13.6 %collective-permute-start.11 = (bf16[32,4096]{1,0:T(8,128)(2,1)S(1)}, bf16[32,4096]{1,0:T(8,128)(2,1)S(1)}, u32[]{:S(2)}, u32[]{:S(2)}) collective-permute-start(bf16[32,4096]{1,0:T(8,128)(2,1)S(1)} %shard_map.119.refs_4_.refs_0_), channel_id=1, source_target_pairs={{0,8},{4,12},{8,0},{12,4},{1,9},{5,13},{9,1},{13,5},{2,10},{6,14},... | collective-permute-start | bytes 786440 | tf_op jit(solution)/shard_map/ppermute | solution.py:31
  27.9 12.2 %collective-permute-start.10 = (bf16[32,4096]{1,0:T(8,128)(2,1)S(1)}, bf16[32,4096]{1,0:T(8,128)(2,1)S(1)}, u32[]{:S(2)}, u32[]{:S(2)}) collective-permute-start(bf16[32,4096]{1,0:T(8,128)(2,1)S(1)} %shard_map.119.refs_4_.refs_0_), channel_id=1, source_target_pairs={{0,4},{4,0},{8,12},{12,8},{1,5},{5,1},{9,13},{13,9},{2,6},{6,2},{1... | collective-permute-start | bytes 786440 | tf_op jit(solution)/shard_map/ppermute | solution.py:31
  40.3 11.7 %collective-permute-start.13 = (bf16[4,32,4096]{2,1,0:T(8,128)(2,1)S(1)}, bf16[4,32,4096]{2,1,0:T(8,128)(2,1)S(1)}, u32[]{:S(2)}, u32[]{:S(2)}) collective-permute-start(bf16[4,32,4096]{2,1,0:T(8,128)(2,1)S(1)} %bitcast.24), channel_id=1, source_target_pairs={{0,16},{16,0},{1,17},{17,1},{2,18},{18,2},{3,19},{19,3},{4,20},{20... | collective-permute-start | bytes 3145736 | tf_op jit(solution)/shard_map/ppermute | solution.py:31
  47.4 13.4 %collective-permute-start.9 = (bf16[64,896]{1,0:T(8,128)(2,1)S(1)}, bf16[64,896]{1,0:T(8,128)(2,1)S(1)}, u32[]{:S(2)}, u32[]{:S(2)}) collective-permute-start(bf16[64,896]{1,0:T(8,128)(2,1)S(1)} %get-tuple-element.39.refs_1_.refs_0_), channel_id=1, source_target_pairs={{0,3},{1,2},{2,1},{3,0},{4,7},{5,6},{6,5},{7,4},{8,11},{9,10},{10,... | collective-permute-start | bytes 344072 | tf_op jit(solution)/shard_map/ppermute | solution.py:31
  49.9 12.2 %collective-permute-start.8 = (bf16[64,896]{1,0:T(8,128)(2,1)S(1)}, bf16[64,896]{1,0:T(8,128)(2,1)S(1)}, u32[]{:S(2)}, u32[]{:S(2)}) collective-permute-start(bf16[64,896]{1,0:T(8,128)(2,1)S(1)} %get-tuple-element.39.refs_1_.refs_0_), channel_id=1, source_target_pairs={{0,2},{1,3},{2,0},{3,1},{4,6},{5,7},{6,4},{7,5},{8,10},{9,11},{10,... | collective-permute-start | bytes 344072 | tf_op jit(solution)/shard_map/ppermute | solution.py:31
  59.3 12.0 %collective-permute-start.22 = (bf16[80,896]{1,0:T(8,128)(2,1)S(1)}, bf16[80,896]{1,0:T(8,128)(2,1)S(1)}, u32[]{:S(2)}, u32[]{:S(2)}) collective-permute-start(bf16[80,896]{1,0:T(8,128)(2,1)S(1)} %get-tuple-element.42), channel_id=1, source_target_pairs={{0,2},{1,3},{2,0},{3,1},{4,6},{5,7},{6,4},{7,5},{8,10},{9,11},{10,... | collective-permute-start | bytes 430088 | tf_op jit(solution)/shard_map/ppermute | solution.py:31
  63.5 19.4 %collective-permute-start.16 = (bf16[272,896]{1,0:T(8,128)(2,1)S(1)}, bf16[272,896]{1,0:T(8,128)(2,1)S(1)}, u32[]{:S(2)}, u32[]{:S(2)}) collective-permute-start(bf16[272,896]{1,0:T(8,128)(2,1)S(1)} %shard_map.125.refs_4_.refs_0_), channel_id=1, source_target_pairs={{0,12},{4,8},{8,4},{12,0},{1,13},{5,9},{9,5},{13,1},{2,14},{6,10},... | collective-permute-start | bytes 1462280 | tf_op jit(solution)/shard_map/ppermute | solution.py:31
  65.2 18.6 %collective-permute-start.15 = (bf16[272,896]{1,0:T(8,128)(2,1)S(1)}, bf16[272,896]{1,0:T(8,128)(2,1)S(1)}, u32[]{:S(2)}, u32[]{:S(2)}) collective-permute-start(bf16[272,896]{1,0:T(8,128)(2,1)S(1)} %shard_map.125.refs_4_.refs_0_), channel_id=1, source_target_pairs={{0,8},{4,12},{8,0},{12,4},{1,9},{5,13},{9,1},{13,5},{2,10},{6,14},... | collective-permute-start | bytes 1462280 | tf_op jit(solution)/shard_map/ppermute | solution.py:31
  66.5 17.3 %collective-permute-start.14 = (bf16[272,896]{1,0:T(8,128)(2,1)S(1)}, bf16[272,896]{1,0:T(8,128)(2,1)S(1)}, u32[]{:S(2)}, u32[]{:S(2)}) collective-permute-start(bf16[272,896]{1,0:T(8,128)(2,1)S(1)} %shard_map.125.refs_4_.refs_0_), channel_id=1, source_target_pairs={{0,4},{4,0},{8,12},{12,8},{1,5},{5,1},{9,13},{13,9},{2,6},{6,2},{1... | collective-permute-start | bytes 1462280 | tf_op jit(solution)/shard_map/ppermute | solution.py:31
  86.5 20.9 %collective-permute-start.33 = (bf16[272,896]{1,0:T(8,128)(2,1)}, bf16[272,896]{1,0:T(8,128)(2,1)}, u32[]{:S(2)}, u32[]{:S(2)}) collective-permute-start(bf16[272,896]{1,0:T(8,128)(2,1)} %shard_map.131.refs_0_), channel_id=1, source_target_pairs={{0,12},{4,8},{8,4},{12,0},{1,13},{5,9},{9,5},{13,1},{2,14},{6,10},... | collective-permute-start | bytes 1462280 | tf_op jit(solution)/shard_map/ppermute | solution.py:31
  88.3 22.4 %collective-permute-start.32 = (bf16[272,896]{1,0:T(8,128)(2,1)}, bf16[272,896]{1,0:T(8,128)(2,1)}, u32[]{:S(2)}, u32[]{:S(2)}) collective-permute-start(bf16[272,896]{1,0:T(8,128)(2,1)} %shard_map.131.refs_0_), channel_id=1, source_target_pairs={{0,8},{4,12},{8,0},{12,4},{1,9},{5,13},{9,1},{13,5},{2,10},{6,14},... | collective-permute-start | bytes 1462280 | tf_op jit(solution)/shard_map/ppermute | solution.py:31
  89.6 21.1 %collective-permute-start.31 = (bf16[272,896]{1,0:T(8,128)(2,1)}, bf16[272,896]{1,0:T(8,128)(2,1)}, u32[]{:S(2)}, u32[]{:S(2)}) collective-permute-start(bf16[272,896]{1,0:T(8,128)(2,1)} %shard_map.131.refs_0_), channel_id=1, source_target_pairs={{0,4},{4,0},{8,12},{12,8},{1,5},{5,1},{9,13},{13,9},{2,6},{6,2},{1... | collective-permute-start | bytes 1462280 | tf_op jit(solution)/shard_map/ppermute | solution.py:31
  113.1 22.5 %collective-permute-start.25 = (bf16[256,896]{1,0:T(8,128)(2,1)}, bf16[256,896]{1,0:T(8,128)(2,1)}, u32[]{:S(2)}, u32[]{:S(2)}) collective-permute-start(bf16[256,896]{1,0:T(8,128)(2,1)} %get-tuple-element.46), channel_id=1, source_target_pairs={{0,4},{4,0},{8,12},{12,8},{1,5},{5,1},{9,13},{13,9},{2,6},{6,2},{1... | collective-permute-start | bytes 1376264 | tf_op jit(solution)/shard_map/ppermute | solution.py:31
  114.6 22.8 %collective-permute-start.26 = (bf16[256,896]{1,0:T(8,128)(2,1)}, bf16[256,896]{1,0:T(8,128)(2,1)}, u32[]{:S(2)}, u32[]{:S(2)}) collective-permute-start(bf16[256,896]{1,0:T(8,128)(2,1)} %get-tuple-element.47), channel_id=1, source_target_pairs={{0,8},{4,12},{8,0},{12,4},{1,9},{5,13},{9,1},{13,5},{2,10},{6,14},... | collective-permute-start | bytes 1376264 | tf_op jit(solution)/shard_map/ppermute | solution.py:31
  115.4 22.1 %collective-permute-start.27 = (bf16[256,896]{1,0:T(8,128)(2,1)}, bf16[256,896]{1,0:T(8,128)(2,1)}, u32[]{:S(2)}, u32[]{:S(2)}) collective-permute-start(bf16[256,896]{1,0:T(8,128)(2,1)} %get-tuple-element.48), channel_id=1, source_target_pairs={{0,12},{4,8},{8,4},{12,0},{1,13},{5,9},{9,5},{13,1},{2,14},{6,10},... | collective-permute-start | bytes 1376264 | tf_op jit(solution)/shard_map/ppermute | solution.py:31
  133.3 13.4 %collective-permute-start.39 = (bf16[256,896]{1,0:T(8,128)(2,1)S(1)}, bf16[256,896]{1,0:T(8,128)(2,1)S(1)}, u32[]{:S(2)}, u32[]{:S(2)}) collective-permute-start(bf16[256,896]{1,0:T(8,128)(2,1)S(1)} %get-tuple-element.56), channel_id=1, source_target_pairs={{0,4},{4,0},{8,12},{12,8},{1,5},{5,1},{9,13},{13,9},{2,6},{6,2},{1... | collective-permute-start | bytes 1376264 | tf_op jit(solution)/shard_map/ppermute | solution.py:31
  134.9 22.1 %collective-permute-start.40 = (bf16[256,896]{1,0:T(8,128)(2,1)S(1)}, bf16[256,896]{1,0:T(8,128)(2,1)S(1)}, u32[]{:S(2)}, u32[]{:S(2)}) collective-permute-start(bf16[256,896]{1,0:T(8,128)(2,1)S(1)} %get-tuple-element.57), channel_id=1, source_target_pairs={{0,8},{4,12},{8,0},{12,4},{1,9},{5,13},{9,1},{13,5},{2,10},{6,14},... | collective-permute-start | bytes 1376264 | tf_op jit(solution)/shard_map/ppermute | solution.py:31
  135.6 21.4 %collective-permute-start.41 = (bf16[256,896]{1,0:T(8,128)(2,1)S(1)}, bf16[256,896]{1,0:T(8,128)(2,1)S(1)}, u32[]{:S(2)}, u32[]{:S(2)}) collective-permute-start(bf16[256,896]{1,0:T(8,128)(2,1)S(1)} %get-tuple-element.58), channel_id=1, source_target_pairs={{0,12},{4,8},{8,4},{12,0},{1,13},{5,9},{9,5},{13,1},{2,14},{6,10},... | collective-permute-start | bytes 1376264 | tf_op jit(solution)/shard_map/ppermute | solution.py:31
  139.0 21.3 %collective-permute-start.36 = (bf16[64,896]{1,0:T(8,128)(2,1)S(1)}, bf16[64,896]{1,0:T(8,128)(2,1)S(1)}, u32[]{:S(2)}, u32[]{:S(2)}) collective-permute-start(bf16[64,896]{1,0:T(8,128)(2,1)S(1)} %get-tuple-element.52), channel_id=1, source_target_pairs={{0,1},{1,0},{2,3},{3,2},{4,5},{5,4},{6,7},{7,6},{8,9},{9,8},{10,11... | collective-permute-start | bytes 344072 | tf_op jit(solution)/shard_map/ppermute | solution.py:31
  139.8 21.9 %collective-permute-start.37 = (bf16[64,896]{1,0:T(8,128)(2,1)S(1)}, bf16[64,896]{1,0:T(8,128)(2,1)S(1)}, u32[]{:S(2)}, u32[]{:S(2)}) collective-permute-start(bf16[64,896]{1,0:T(8,128)(2,1)S(1)} %get-tuple-element.53), channel_id=1, source_target_pairs={{0,2},{1,3},{2,0},{3,1},{4,6},{5,7},{6,4},{7,5},{8,10},{9,11},{10,... | collective-permute-start | bytes 344072 | tf_op jit(solution)/shard_map/ppermute | solution.py:31
  146.7 14.9 %collective-permute-start.38 = (bf16[64,896]{1,0:T(8,128)(2,1)S(1)}, bf16[64,896]{1,0:T(8,128)(2,1)S(1)}, u32[]{:S(2)}, u32[]{:S(2)}) collective-permute-start(bf16[64,896]{1,0:T(8,128)(2,1)S(1)} %get-tuple-element.54), channel_id=1, source_target_pairs={{0,3},{1,2},{2,1},{3,0},{4,7},{5,6},{6,5},{7,4},{8,11},{9,10},{10,... | collective-permute-start | bytes 344072 | tf_op jit(solution)/shard_map/ppermute | solution.py:31
  (29 other events, 226.8 us)

commit v2 on v1

--- a/solution.py
+++ b/solution.py
@@ -201,36 +201,42 @@
     for ref in refs[:n_ref]:
         pieces += [ref] if len(ref.shape) == 2 else [ref.at[i] for i in range(ref.shape[0])]
     n = len(pieces)
-    wg_hbm, wu_hbm, weight_ref = refs[n_ref : n_ref + 3]
-    out_ref, x_ref, wg_ref, wu_ref, g_ref, u_ref, sq_ref, sems, wg_sems, wu_sems = refs[-10:]
+    wg_hbm, wu_hbm, weight_ref, gain_in = refs[n_ref : n_ref + 4]
+    out_ref, gain_ref, x_ref, wg_ref, wu_ref, g_ref, u_ref, sq_ref, sems, wg_sems, wu_sems = refs[-11:]
     width = pieces[0].shape[1]
     rows = out_ref.shape[0]
-
-    def load(i):
-        at = pl.ds(pl.multiple_of(idx_ref[i] * width, width), width)
+    group = n // x_ref.shape[0]
+
+    def load(i, j):
+        at = pl.ds(pl.multiple_of(idx_ref[i * group + j] * width, width), width)
+        to = pl.ds(j * width, width)
         return (
-            pltpu.make_async_copy(wg_hbm.at[at], wg_ref.at[i], wg_sems.at[i]),
-            pltpu.make_async_copy(wu_hbm.at[at], wu_ref.at[i], wu_sems.at[i]),
+            pltpu.make_async_copy(pieces[0], x_ref.at[i, :, to], sems.at[i * group + j]),
+            pltpu.make_async_copy(wg_hbm.at[at], wg_ref.at[i, to], wg_sems.at[i * group + j]),
+            pltpu.make_async_copy(wu_hbm.at[at], wu_ref.at[i, to], wu_sems.at[i * group + j]),
         )
 
     for i in range(n):
-        pltpu.make_async_copy(pieces[i], x_ref.at[i], sems.at[i]).start()
-        for copy in load(i):
+        to = x_ref.at[i // group, :, pl.ds(i % group * width, width)]
+        pltpu.make_async_copy(pieces[i], to, sems.at[i]).start()
+        for copy in load(i // group, i % group)[1:]:
             copy.start()
     g_ref[...] = jnp.zeros_like(g_ref)
     u_ref[...] = jnp.zeros_like(u_ref)
     sq_ref[...] = jnp.zeros_like(sq_ref)
-
-    @pl.loop(0, n)
+    gain_ref[...] = gain_in[...]
+
+    @pl.loop(0, n // group)
     def _(i):
-        pltpu.make_async_copy(pieces[0], x_ref.at[i], sems.at[i]).wait()
+        for j in range(group):
+            for copy in load(i, j):
+                copy.wait()
         x = x_ref[i, :rows, :]
-        inverse_gain = 1.0 / x_ref[i, rows:, :][0:1].astype(jnp.float32)
-        for copy in load(i):
-            copy.wait()
+        if x_ref.shape[1] > rows:
+            gain_ref[pl.ds(i, 1), :] = 1.0 / x_ref[i, rows:, :][0:1].astype(jnp.float32)
         g_ref[...] += jnp.dot(x, wg_ref[i], preferred_element_type=jnp.float32)
         u_ref[...] += jnp.dot(x, wu_ref[i], preferred_element_type=jnp.float32)
-        hidden = x.astype(jnp.float32) * inverse_gain
+        hidden = x.astype(jnp.float32) * gain_ref[pl.ds(i, 1), :]
         sq_ref[...] += jnp.sum(hidden * hidden, axis=1, keepdims=True)
 
     inv = lax.rsqrt(sq_ref[...] / (n * width) + EPS)
@@ -239,20 +245,25 @@
     out_ref[...] = (g / (1.0 + jnp.exp(-g)) * u * weight_ref[...]).astype(jnp.bfloat16)
 
 
-def gate_up(pieces, owners, w_gate, w_up, weight):
+def gate_up(pieces, owners, w_gate, w_up, weight, gain):
     n = owners.shape[0]
     held, width = pieces[0].shape[-2:]
-    rows = held - EXTRA
+    rows = weight.shape[0]
     full, units = w_gate.shape
+    group = 2 if width % 128 == 0 else 1
+    groups, wide = n // group, group * width
     return pl.pallas_call(
         functools.partial(gate_up_kernel, len(pieces)),
-        in_specs=[SMEM] + [ANY] * (len(pieces) + 2) + [VMEM],
-        out_specs=VMEM,
-        out_shape=jax.ShapeDtypeStruct((rows, units), jnp.bfloat16),
+        in_specs=[SMEM] + [ANY] * (len(pieces) + 2) + [VMEM] * 2,
+        out_specs=[VMEM] * 2,
+        out_shape=[
+            jax.ShapeDtypeStruct((rows, units), jnp.bfloat16),
+            jax.ShapeDtypeStruct((groups, wide), jnp.float32),
+        ],
         scratch_shapes=[
-            pltpu.VMEM((n, held, width), jnp.bfloat16),
-            pltpu.VMEM((n, width, units), jnp.bfloat16),
-            pltpu.VMEM((n, width, units), jnp.bfloat16),
+            pltpu.VMEM((groups, held, wide), jnp.bfloat16),
+            pltpu.VMEM((groups, wide, units), jnp.bfloat16),
+            pltpu.VMEM((groups, wide, units), jnp.bfloat16),
             pltpu.VMEM((rows, units), jnp.float32),
             pltpu.VMEM((rows, units), jnp.float32),
             pltpu.VMEM((rows, 1), jnp.float32),
@@ -262,24 +273,26 @@
         ],
         compiler_params=pltpu.CompilerParams(vmem_limit_bytes=30 * MIB),
         cost_estimate=HEAVY,
-    )(owners, *pieces, in_hbm(w_gate), in_hbm(w_up), weight)
+    )(owners, *pieces, in_hbm(w_gate), in_hbm(w_up), weight, gain.reshape(groups, wide))
 
 
 def down_kernel(idx_ref, act_ref, w_ref, out_ref):
     m, _, width = out_ref.shape
 
-    @pl.loop(0, m)
+    @pl.loop(0, m // 2)
     def _(j):
-        at = pl.ds(pl.multiple_of(idx_ref[j] * width, 128), width)
-        out_ref[j] = jnp.dot(
-            act_ref[...], w_ref[:, at], preferred_element_type=jnp.float32
-        ).astype(jnp.bfloat16)
+        even = idx_ref[2 * j] // 2 * 2
+        swapped = idx_ref[2 * j] - even
+        at = pl.ds(pl.multiple_of(even * width, 128), 2 * width)
+        both = jnp.dot(act_ref[...], w_ref[:, at], preferred_element_type=jnp.float32)
+        out_ref[2 * j + swapped] = both[:, :width].astype(jnp.bfloat16)
+        out_ref[2 * j + 1 - swapped] = both[:, width:].astype(jnp.bfloat16)
 
 
 def down(act, owners, w_down, width):
     rows, units = act.shape
     m = owners.shape[0]
-    if width % 128:
+    if width % 128 or m % 2:
         cut = [
             lax.dynamic_slice_in_dim(w_down, owners[j] * width, width, axis=1) for j in range(m)
         ]
@@ -296,26 +309,30 @@
     )(owners, act, w_down)
 
 
-def combine_kernel(n, near_ref, got_ref, *refs):
-    outs = refs
-    for d in range(n):
-        both = near_ref[d].astype(jnp.float32) + got_ref[d].astype(jnp.float32)
-        outs[d][...] = both.astype(outs[d].dtype)
-
-
-def combine(near, got):
+def combine_kernel(n, parts, near_ref, got_ref, *outs):
+    size = near_ref.shape[1] // parts
+    for p in range(parts):
+        at = slice(p * size, (p + 1) * size)
+        for d in range(n):
+            both = near_ref[d, at, :].astype(jnp.float32) + got_ref[d, at, :].astype(jnp.float32)
+            outs[p * n + d][...] = both.astype(outs[p * n + d].dtype)
+
+
+def combine(near, got, parts):
     n, rows, width = near.shape
-    return pl.pallas_call(
-        functools.partial(combine_kernel, n),
+    outs = pl.pallas_call(
+        functools.partial(combine_kernel, n, parts),
         in_specs=[VMEM] * 2,
-        out_specs=[VMEM] * n,
+        out_specs=[VMEM] * (n * parts),
         out_shape=[
-            jax.ShapeDtypeStruct((rows, width), jnp.bfloat16 if d else jnp.float32)
+            jax.ShapeDtypeStruct((rows // parts, width), jnp.bfloat16 if d else jnp.float32)
             for d in range(n)
-        ],
+        ]
+        * parts,
         compiler_params=pltpu.CompilerParams(vmem_limit_bytes=12 * MIB),
         cost_estimate=HEAVY,
     )(near, got)
+    return [outs[p * n : (p + 1) * n] for p in range(parts)]
 
 
 def reduce_kernel(n, blocks, *refs):
@@ -329,7 +346,7 @@
         outs[b][...] = total.astype(outs[b].dtype)
 
 
-def reduce(pieces, blocks, after):
+def reduce(pieces, blocks, own, after):
     n = len(pieces)
     rows, width = pieces[0].shape
     return pl.pallas_call(
@@ -337,7 +354,7 @@
         in_specs=[VMEM] * n + [ANY] * len(after),
         out_specs=[VMEM] * blocks,
         out_shape=[
-            jax.ShapeDtypeStruct((rows // blocks, width), jnp.bfloat16 if b else jnp.float32)
+            jax.ShapeDtypeStruct((rows // blocks, width), jnp.bfloat16 if b or not own else jnp.float32)
             for b in range(blocks)
         ],
         compiler_params=pltpu.CompilerParams(vmem_limit_bytes=8 * MIB),
@@ -345,11 +362,12 @@
     )(*pieces, *after)
 
 
-def finish_kernel(chunks, per, n, *refs):
+def finish_kernel(counts, per, *refs):
     out_ref = refs[-1]
+    chunks = len(counts)
     part = out_ref.shape[0] // (chunks * per)
     for c in range(chunks):
-        pieces = refs[c * n : (c + 1) * n]
+        pieces = refs[sum(counts[:c]) : sum(counts[: c + 1])]
         for p in range(per):
             at = slice(p * part, (p + 1) * part)
             total = pieces[0][at, :]
@@ -360,13 +378,13 @@
 
 
 def finish(terms, per):
-    chunks, n = len(terms), len(terms[0])
+    counts = [len(chunk) for chunk in terms]
     rows, width = terms[0][0].shape
     return pl.pallas_call(
-        functools.partial(finish_kernel, chunks, per, n),
-        in_specs=[VMEM] * (chunks * n),
+        functools.partial(finish_kernel, counts, per),
+        in_specs=[VMEM] * sum(counts),
         out_specs=VMEM,
-        out_shape=jax.ShapeDtypeStruct((chunks * rows, width), jnp.bfloat16),
+        out_shape=jax.ShapeDtypeStruct((len(counts) * rows, width), jnp.bfloat16),
         compiler_params=pltpu.CompilerParams(vmem_limit_bytes=8 * MIB),
         cost_estimate=HEAVY,
     )(*[x for chunk in terms for x in chunk])
@@ -499,12 +517,14 @@
     def other_core(x):
         return swap(x, "side", 2, 1)
 
-    def experts(near, held):
+    def experts(near, held, inverse_gain, parts):
         far = [other_core(piece) for piece in near]
-        act = gate_up(near + far, owners, gate_dev, up_dev, held)
+        act, inverse_gain = gate_up(
+            near + far, owners, gate_dev, up_dev, held, inverse_gain
+        )
         far_rows = down(act, owners[n_row:], down_dev, width)
         near_rows = down(act, owners[:n_row], down_dev, width)
-        return combine(near_rows, other_core(far_rows))
+        return combine(near_rows, other_core(far_rows), parts), inverse_gain
 
     def stack_rows(x, after, estimate=HEAVY):
         return stack(over_row([x] * n_row), after, estimate).reshape(n_row, *x.shape)
@@ -521,14 +541,20 @@
     weight = gates.reshape(n_col, per, chunks, part)
     weight = [weight[:, :, c].reshape(-1, 1) for c in range(chunks)]
     near_0 = over_row([rows_0] * n_row)
-    both_0 = experts(near_0, weight[0])
-    rows_1 = stack(over_col([scaled_1] * n_col) + [gain], near_0[1:])
+    no_gain = jnp.zeros((2 * n_row, width), jnp.float32)
+    [both_0], inverse_gain = experts(near_0, weight[0], no_gain, 1)
+    rows_1 = stack(over_col([scaled_1] * n_col), near_0[1:])
     near_1 = stack_rows(rows_1, both_0[:1])
-    both_1 = experts([near_1], hand_on(weight[1], [near_1]))
-    total_0 = reduce(over_row(both_0), n_col, both_1[:1])
-    total_1 = reduce(over_row(both_1), n_col, [])
-    terms = [[hidden_0, *over_col(total_0)], [hidden_1, *over_col(total_1)]]
-    return finish(terms, per)
+    both_1, _ = experts([near_1], hand_on(weight[1], [near_1]), inverse_gain, 2)
+    total_0 = reduce(over_row(both_0), n_col, True, both_1[0][:1])
+    terms_0 = [hidden_0, *over_col(total_0)]
+    half = n_col // 2
+    far_1 = reduce(over_row(both_1[1]), half, False, total_0[:1])
+    last = [swap(far_1[d], "col", n_col, half + d) for d in range(half)]
+    total_1 = reduce(over_row(both_1[0]), half, True, [far_1[0], *terms_0[2:]])
+    first = [total_1[0]] + [swap(total_1[d], "col", n_col, d) for d in range(1, half)]
+    [hidden_1] = reduce([hidden_1, *last], 1, True, total_1[:1])
+    return finish([terms_0, [hidden_1, *first]], per)
 
 
 def solution(mesh):

time: 170 us -> 164 us (0.965)
  Pallas kernels: 65.4 us -> 59.8 us
  waiting for transfers between devices: 48.2 us -> 42.8 us
  starting transfers between devices: 54.5 us -> 59.5 us
    ppermute x45 -> x48, waiting for transfers between devices: 48.2 us -> 42.8 us  [swap(): return lax.ppermute(x, axis, [(i, i ^ d) for i in range(count)])]
    ppermute x45 -> x48, starting transfers between devices: 54.5 us -> 59.5 us  [swap(): return lax.ppermute(x, axis, [(i, i ^ d) for i in range(count)])]
    pallas_call x2, Pallas kernels: 19.4 us -> 15.9 us  [gate_up(): pl.pallas_call(functools.partial(gate_up_kernel, len(pieces)), in_specs=[...]
    pallas_call x4, Pallas kernels: 9.52 us -> 7.5 us  [down(): pl.pallas_call(down_kernel, in_specs=[SMEM, VMEM, VMEM], out_specs=VMEM,...]
  transfers between devices with their start and end apart: 45 -> 48, of which waited for: 18 -> 18; matrix products, arithmetic and copies ran while one was open for 0% -> 0% of each run, Pallas kernels for 32% -> 30%
where the time goes in v2:
time: 164 us
  Pallas kernels  59.8 us (36%)
  starting transfers between devices  59.5 us (36%)
  waiting for transfers between devices  42.8 us (26%)
    ppermute x48, starting transfers between devices, swap(): return lax.ppermute(x, axis, [(i, i ^ d) for i in range(count)])  59.5 us
    ppermute x48, waiting for transfers between devices, swap(): return lax.ppermute(x, axis, [(i, i ^ d) for i in range(count)])  42.8 us
    pallas_call x2, Pallas kernels, gate_up(): pl.pallas_call(functools.partial(gate_up_kernel, len(pieces)), in_specs=[...  15.9 us
    pallas_call x2, Pallas kernels, attend(): pl.pallas_call(functools.partial(attend_kernel, (size + ROPE) ** (-0.5),...  15.4 us
    pallas_call x2, Pallas kernels, project(): pl.pallas_call(functools.partial(project_kernel, blocks, len(gate)), in_s...  11.2 us
    pallas_call x4, Pallas kernels, down(): pl.pallas_call(down_kernel, in_specs=[SMEM, VMEM, VMEM], out_specs=VMEM,...  7.5 us
    pallas_call x5, Pallas kernels, stack(): pl.pallas_call(functools.partial(stack_kernel, n), in_specs=[ANY] * (n +...  5.38 us
  transfers between devices with their start and end apart: 48, of which 18 were waited for; matrix products, arithmetic and copies ran while one was open for 0% of the time, Pallas kernels for 30%

profile of v2, /device:TPU:0, one launch (start us, length us, event | category | flops | bytes accessed | tf_op | source)
XLA Modules:
  0.0 163.8 jit_solution(12720810310625463501)
XLA Ops:
  0.7 7.7 %shard_map.118.refs_0_ = bf16[32,4096]{1,0:T(8,128)(2,1)S(1)} custom-call(s32[64]{0:T(128)S(1)} %copy-done.3, bf16[64,32,576]{2,1,0:T(8,128)(2,1)} %q_ref.3, bf16[64,576,128]{2,1,0:T(8,128)(2,1)} %bitcast.36, bf16[32,512,128]{2,1,0:T(8,128)(2,1)} %w_hbm.5), custom_call_target="tpu_custom_call" | custom-call | flops 99999997952 | bytes 1024 | tf_op jit(solution)/shard_map/pallas_call | solution.py:444
  8.3 4.0 %collective-permute-start.2 = (bf16[32,4096]{1,0:T(8,128)(2,1)S(1)}, bf16[32,4096]{1,0:T(8,128)(2,1)S(1)}, u32[]{:S(2)}, u32[]{:S(2)}) collective-permute-start(bf16[32,4096]{1,0:T(8,128)(2,1)S(1)} %shard_map.118.refs_0_), channel_id=1, source_target_pairs={{0,12},{4,8},{8,4},{12,0},{1,13},{5,9},{9,5},{13,1},{2,14},{6,10},... | collective-permute-start | bytes 786440 | tf_op jit(solution)/shard_map/ppermute | solution.py:31
  12.9 7.7 %shard_map.119.refs_4_.refs_0_ = bf16[32,4096]{1,0:T(8,128)(2,1)S(1)} custom-call(s32[64]{0:T(128)S(1)} %copy-done.3, bf16[64,32,576]{2,1,0:T(8,128)(2,1)} %q_ref.3, bf16[64,576,128]{2,1,0:T(8,128)(2,1)} %bitcast.37, bf16[32,512,128]{2,1,0:T(8,128)(2,1)} %w_hbm.5, bf16[32,4096]{1,0:T(8,128)(2,1)S(1)} %shard_map.118.refs_0_), custom_call_target="tpu_custom_call" | custom-call | flops 99999997952 | bytes 1024 | tf_op jit(solution)/shard_map/pallas_call | solution.py:444
  20.6 3.6 %collective-permute-done.1.refs_2_ = bf16[32,4096]{1,0:T(8,128)(2,1)S(1)} collective-permute-done((bf16[32,4096]{1,0:T(8,128)(2,1)S(1)}, bf16[32,4096]{1,0:T(8,128)(2,1)S(1)}, u32[]{:S(2)}, u32[]{:S(2)}) %collective-permute-start.1) | collective-permute-done | bytes 262176 | tf_op jit(solution)/shard_map/ppermute | solution.py:31
  28.5 5.6 %shard_map.121 = (bf16[64,896]{1,0:T(8,128)(2,1)S(1)}, bf16[64,896]{1,0:T(8,128)(2,1)S(1)}, bf16[64,896]{1,0:T(8,128)(2,1)S(1)}, bf16[64,896]{1,0:T(8,128)(2,1)S(1)}) custom-call(s32[8]{0:T(128)S(1)} %fusion.pos_ref, bf16[4,32,4096]{2,1,0:T(8,128)(2,1)S(1)} %bitcast.23, bf16[4,32,4096]{2,1,0:T(8,128)(2,1)S(1)} %collective-permute-done.3.far_ref, ...), custom_call_target="tpu_custom_call" | custom-call | flops 99999997952 | bytes 1024 | tf_op jit(solution)/shard_map/pallas_call | solution.py:144
  35.8 2.6 %collective-permute-start.5 = (bf16[64,896]{1,0:T(8,128)(2,1)S(1)}, bf16[64,896]{1,0:T(8,128)(2,1)S(1)}, u32[]{:S(2)}, u32[]{:S(2)}) collective-permute-start(bf16[64,896]{1,0:T(8,128)(2,1)S(1)} %get-tuple-element.43), channel_id=1, source_target_pairs={{0,2},{1,3},{2,0},{3,1},{4,6},{5,7},{6,4},{7,5},{8,10},{9,11},{10,... | collective-permute-start | bytes 344072 | tf_op jit(solution)/shard_map/ppermute | solution.py:31
  40.4 6.8 %collective-permute-done.5.refs_2_ = bf16[64,896]{1,0:T(8,128)(2,1)S(1)} collective-permute-done((bf16[64,896]{1,0:T(8,128)(2,1)S(1)}, bf16[64,896]{1,0:T(8,128)(2,1)S(1)}, u32[]{:S(2)}, u32[]{:S(2)}) %collective-permute-start.5) | collective-permute-done | bytes 114720 | tf_op jit(solution)/shard_map/ppermute | solution.py:31
  47.4 2.5 %collective-permute-start.9 = (bf16[64,896]{1,0:T(8,128)(2,1)S(1)}, bf16[64,896]{1,0:T(8,128)(2,1)S(1)}, u32[]{:S(2)}, u32[]{:S(2)}) collective-permute-start(bf16[64,896]{1,0:T(8,128)(2,1)S(1)} %get-tuple-element.46.refs_1_.refs_0_), channel_id=1, source_target_pairs={{0,3},{1,2},{2,1},{3,0},{4,7},{5,6},{6,5},{7,4},{8,11},{9,10},{10,... | collective-permute-start | bytes 344072 | tf_op jit(solution)/shard_map/ppermute | solution.py:31
  52.0 5.6 %shard_map.124 = (bf16[80,896]{1,0:T(8,128)(2,1)S(1)}, bf16[80,896]{1,0:T(8,128)(2,1)S(1)}, bf16[80,896]{1,0:T(8,128)(2,1)S(1)}, bf16[80,896]{1,0:T(8,128)(2,1)S(1)}) custom-call(s32[8]{0:T(128)S(1)} %fusion.pos_ref, bf16[4,32,4096]{2,1,0:T(8,128)(2,1)S(1)} %bitcast.25, bf16[4,32,4096]{2,1,0:T(8,128)(2,1)S(1)} %collective-permute-done.13.far_ref, ...), custom_call_target="tpu_custom_call" | custom-call | flops 99999997952 | bytes 1024 | tf_op jit(solution)/shard_map/pallas_call | solution.py:144
  67.1 4.2 %collective-permute-done.22.refs_2_ = bf16[80,896]{1,0:T(8,128)(2,1)S(1)} collective-permute-done((bf16[80,896]{1,0:T(8,128)(2,1)S(1)}, bf16[80,896]{1,0:T(8,128)(2,1)S(1)}, u32[]{:S(2)}, u32[]{:S(2)}) %collective-permute-start.22) | collective-permute-done | bytes 143392 | tf_op jit(solution)/shard_map/ppermute | solution.py:31
  71.4 2.5 %collective-permute-start.30 = (bf16[64,896]{1,0:T(8,128)(2,1)S(1)}, bf16[64,896]{1,0:T(8,128)(2,1)S(1)}, u32[]{:S(2)}, u32[]{:S(2)}) collective-permute-start(bf16[64,896]{1,0:T(8,128)(2,1)S(1)} %get-tuple-element.57.refs_0_), channel_id=1, source_target_pairs={{0,3},{1,2},{2,1},{3,0},{4,7},{5,6},{6,5},{7,4},{8,11},{9,10},{10,... | collective-permute-start | bytes 344072 | tf_op jit(solution)/shard_map/ppermute | solution.py:31
  75.3 3.6 %collective-permute-done.30.refs_3_ = bf16[64,896]{1,0:T(8,128)(2,1)S(1)} collective-permute-done((bf16[64,896]{1,0:T(8,128)(2,1)S(1)}, bf16[64,896]{1,0:T(8,128)(2,1)S(1)}, u32[]{:S(2)}, u32[]{:S(2)}) %collective-permute-start.30) | collective-permute-done | bytes 114720 | tf_op jit(solution)/shard_map/ppermute | solution.py:31
  78.9 3.4 %collective-permute-start.28 = (bf16[64,896]{1,0:T(8,128)(2,1)S(1)}, bf16[64,896]{1,0:T(8,128)(2,1)S(1)}, u32[]{:S(2)}, u32[]{:S(2)}) collective-permute-start(bf16[64,896]{1,0:T(8,128)(2,1)S(1)} %get-tuple-element.57.refs_0_), channel_id=1, source_target_pairs={{0,1},{1,0},{2,3},{3,2},{4,5},{5,4},{6,7},{7,6},{8,9},{9,8},{10,11... | collective-permute-start | bytes 344072 | tf_op jit(solution)/shard_map/ppermute | solution.py:31
  90.0 8.1 %shard_map.127 = (bf16[256,512]{1,0:T(8,128)(2,1)S(1)}, f32[4,1792]{1,0:T(4,128)S(1)}) custom-call(s32[8]{0:T(128)S(1)} %stack.39.idx_ref, bf16[272,896]{1,0:T(8,128)(2,1)S(1)} %shard_map.125.refs_4_.refs_0_, bf16[272,896]{1,0:T(8,128)(2,1)S(1)} %collective-permute-done.14.refs_1_.refs_4_, bf16[272,896]{1,0:T(8,128)(2,1)S(1)} %collective-permute-done.15.refs_2_.refs_5_, ...), custom_call_target="tpu_custom_call" | custom-call | flops 99999997952 | bytes 1024 | tf_op jit(solution)/shard_map/pallas_call | solution.py:255
  105.2 4.2 %collective-permute-done.32.refs_2_ = bf16[256,896]{1,0:T(8,128)(2,1)} collective-permute-done((bf16[256,896]{1,0:T(8,128)(2,1)}, bf16[256,896]{1,0:T(8,128)(2,1)}, u32[]{:S(2)}, u32[]{:S(2)}) %collective-permute-start.32) | collective-permute-done | bytes 458784 | tf_op jit(solution)/shard_map/ppermute | solution.py:31
  109.3 2.2 %shard_map.132 = bf16[1024,896]{1,0:T(8,128)(2,1)S(1)} custom-call(bf16[256,896]{1,0:T(8,128)(2,1)} %shard_map.131.refs_0_, bf16[256,896]{1,0:T(8,128)(2,1)} %collective-permute-done.31.refs_1_, bf16[256,896]{1,0:T(8,128)(2,1)} %collective-permute-done.32.refs_2_, bf16[256,896]{1,0:T(8,128)(2,1)} %collective-permute-done.33.refs_3_, ...), custom_call_target="tpu_custom_call" | custom-call | flops 99999997952 | bytes 1024 | tf_op jit(solution)/shard_map/pallas_call | solution.py:57
  115.4 7.8 %shard_map.134 = (bf16[256,512]{1,0:T(8,128)(2,1)S(1)}, f32[4,1792]{1,0:T(4,128)}) custom-call(s32[8]{0:T(128)S(1)} %stack.39.idx_ref, bf16[4,256,896]{2,1,0:T(8,128)(2,1)S(1)} %bitcast.33, bf16[4,256,896]{2,1,0:T(8,128)(2,1)S(1)} %collective-permute-done.34.refs_1_, bf16[7168,512]{1,0:T(8,128)(2,1)} %bitcast.39, bf16[7168,512]{1,0:T(8,128)(2,1)} %bitcast.41, ...), custom_call_target="tpu_custom_call" | custom-call | flops 99999997952 | bytes 1024 | tf_op jit(solution)/shard_map/pallas_call | solution.py:255
  132.9 3.3 %collective-permute-done.26.refs_2_ = bf16[256,896]{1,0:T(8,128)(2,1)} collective-permute-done((bf16[256,896]{1,0:T(8,128)(2,1)}, bf16[256,896]{1,0:T(8,128)(2,1)}, u32[]{:S(2)}, u32[]{:S(2)}) %collective-permute-start.26) | collective-permute-done | bytes 458784 | tf_op jit(solution)/shard_map/ppermute | solution.py:31
  138.5 2.3 %collective-permute-start.37 = (bf16[64,896]{1,0:T(8,128)(2,1)S(1)}, bf16[64,896]{1,0:T(8,128)(2,1)S(1)}, u32[]{:S(2)}, u32[]{:S(2)}) collective-permute-start(bf16[64,896]{1,0:T(8,128)(2,1)S(1)} %get-tuple-element.63), channel_id=1, source_target_pairs={{0,2},{1,3},{2,0},{3,1},{4,6},{5,7},{6,4},{7,5},{8,10},{9,11},{10,... | collective-permute-start | bytes 344072 | tf_op jit(solution)/shard_map/ppermute | solution.py:31
  140.8 3.0 %collective-permute-done.36.refs_5_.refs_2_ = bf16[64,896]{1,0:T(8,128)(2,1)S(1)} collective-permute-done((bf16[64,896]{1,0:T(8,128)(2,1)S(1)}, bf16[64,896]{1,0:T(8,128)(2,1)S(1)}, u32[]{:S(2)}, u32[]{:S(2)}) %collective-permute-start.36) | collective-permute-done | bytes 114720 | tf_op jit(solution)/shard_map/ppermute | solution.py:31
  143.8 2.4 %collective-permute-start.38 = (bf16[64,896]{1,0:T(8,128)(2,1)S(1)}, bf16[64,896]{1,0:T(8,128)(2,1)S(1)}, u32[]{:S(2)}, u32[]{:S(2)}) collective-permute-start(bf16[64,896]{1,0:T(8,128)(2,1)S(1)} %get-tuple-element.64), channel_id=1, source_target_pairs={{0,3},{1,2},{2,1},{3,0},{4,7},{5,6},{6,5},{7,4},{8,11},{9,10},{10,... | collective-permute-start | bytes 344072 | tf_op jit(solution)/shard_map/ppermute | solution.py:31
  151.3 4.0 %collective-permute-start.42 = (bf16[64,896]{1,0:T(8,128)(2,1)S(1)}, bf16[64,896]{1,0:T(8,128)(2,1)S(1)}, u32[]{:S(2)}, u32[]{:S(2)}) collective-permute-start(bf16[64,896]{1,0:T(8,128)(2,1)S(1)} %get-tuple-element.70.refs_4_), channel_id=1, source_target_pairs={{0,2},{1,3},{2,0},{3,1},{4,6},{5,7},{6,4},{7,5},{8,10},{9,11},{10,... | collective-permute-start | bytes 344072 | tf_op jit(solution)/shard_map/ppermute | solution.py:31
  155.3 2.7 %collective-permute-done.45.refs_2_ = bf16[128,896]{1,0:T(8,128)(2,1)S(1)} collective-permute-done((bf16[128,896]{1,0:T(8,128)(2,1)S(1)}, bf16[128,896]{1,0:T(8,128)(2,1)S(1)}, u32[]{:S(2)}, u32[]{:S(2)}) %collective-permute-start.45) | collective-permute-done | bytes 229408 | tf_op jit(solution)/shard_map/ppermute | solution.py:31
  160.8 2.2 %collective-permute-done.47.refs_7_ = bf16[64,896]{1,0:T(8,128)(2,1)S(1)} collective-permute-done((bf16[64,896]{1,0:T(8,128)(2,1)S(1)}, bf16[64,896]{1,0:T(8,128)(2,1)S(1)}, u32[]{:S(2)}, u32[]{:S(2)}) %collective-permute-start.47) | collective-permute-done | bytes 114720 | tf_op jit(solution)/shard_map/ppermute | solution.py:31
  (129 shorter events, 61.4 us)
Async XLA Ops:
  8.3 12.3 %collective-permute-start.2 = (bf16[32,4096]{1,0:T(8,128)(2,1)S(1)}, bf16[32,4096]{1,0:T(8,128)(2,1)S(1)}, u32[]{:S(2)}, u32[]{:S(2)}) collective-permute-start(bf16[32,4096]{1,0:T(8,128)(2,1)S(1)} %shard_map.118.refs_0_), channel_id=1, source_target_pairs={{0,12},{4,8},{8,4},{12,0},{1,13},{5,9},{9,5},{13,1},{2,14},{6,10},... | collective-permute-start | bytes 786440 | tf_op jit(solution)/shard_map/ppermute | solution.py:31
  12.3 11.9 %collective-permute-start.1 = (bf16[32,4096]{1,0:T(8,128)(2,1)S(1)}, bf16[32,4096]{1,0:T(8,128)(2,1)S(1)}, u32[]{:S(2)}, u32[]{:S(2)}) collective-permute-start(bf16[32,4096]{1,0:T(8,128)(2,1)S(1)} %shard_map.118.refs_0_), channel_id=1, source_target_pairs={{0,8},{4,12},{8,0},{12,4},{1,9},{5,13},{9,1},{13,5},{2,10},{6,14},... | collective-permute-start | bytes 786440 | tf_op jit(solution)/shard_map/ppermute | solution.py:31
  12.8 11.7 %collective-permute-start = (bf16[32,4096]{1,0:T(8,128)(2,1)S(1)}, bf16[32,4096]{1,0:T(8,128)(2,1)S(1)}, u32[]{:S(2)}, u32[]{:S(2)}) collective-permute-start(bf16[32,4096]{1,0:T(8,128)(2,1)S(1)} %shard_map.118.refs_0_), channel_id=1, source_target_pairs={{0,4},{4,0},{8,12},{12,8},{1,5},{5,1},{9,13},{13,9},{2,6},{6,2},{1... | collective-permute-start | bytes 786440 | tf_op jit(solution)/shard_map/ppermute | solution.py:31
  24.8 13.6 %collective-permute-start.12 = (bf16[32,4096]{1,0:T(8,128)(2,1)S(1)}, bf16[32,4096]{1,0:T(8,128)(2,1)S(1)}, u32[]{:S(2)}, u32[]{:S(2)}) collective-permute-start(bf16[32,4096]{1,0:T(8,128)(2,1)S(1)} %shard_map.119.refs_4_.refs_0_), channel_id=1, source_target_pairs={{0,12},{4,8},{8,4},{12,0},{1,13},{5,9},{9,5},{13,1},{2,14},{6,10},... | collective-permute-start | bytes 786440 | tf_op jit(solution)/shard_map/ppermute | solution.py:31
  26.4 13.6 %collective-permute-start.11 = (bf16[32,4096]{1,0:T(8,128)(2,1)S(1)}, bf16[32,4096]{1,0:T(8,128)(2,1)S(1)}, u32[]{:S(2)}, u32[]{:S(2)}) collective-permute-start(bf16[32,4096]{1,0:T(8,128)(2,1)S(1)} %shard_map.119.refs_4_.refs_0_), channel_id=1, source_target_pairs={{0,8},{4,12},{8,0},{12,4},{1,9},{5,13},{9,1},{13,5},{2,10},{6,14},... | collective-permute-start | bytes 786440 | tf_op jit(solution)/shard_map/ppermute | solution.py:31
  27.9 12.2 %collective-permute-start.10 = (bf16[32,4096]{1,0:T(8,128)(2,1)S(1)}, bf16[32,4096]{1,0:T(8,128)(2,1)S(1)}, u32[]{:S(2)}, u32[]{:S(2)}) collective-permute-start(bf16[32,4096]{1,0:T(8,128)(2,1)S(1)} %shard_map.119.refs_4_.refs_0_), channel_id=1, source_target_pairs={{0,4},{4,0},{8,12},{12,8},{1,5},{5,1},{9,13},{13,9},{2,6},{6,2},{1... | collective-permute-start | bytes 786440 | tf_op jit(solution)/shard_map/ppermute | solution.py:31
  35.8 11.5 %collective-permute-start.5 = (bf16[64,896]{1,0:T(8,128)(2,1)S(1)}, bf16[64,896]{1,0:T(8,128)(2,1)S(1)}, u32[]{:S(2)}, u32[]{:S(2)}) collective-permute-start(bf16[64,896]{1,0:T(8,128)(2,1)S(1)} %get-tuple-element.43), channel_id=1, source_target_pairs={{0,2},{1,3},{2,0},{3,1},{4,6},{5,7},{6,4},{7,5},{8,10},{9,11},{10,... | collective-permute-start | bytes 344072 | tf_op jit(solution)/shard_map/ppermute | solution.py:31
  40.3 11.7 %collective-permute-start.13 = (bf16[4,32,4096]{2,1,0:T(8,128)(2,1)S(1)}, bf16[4,32,4096]{2,1,0:T(8,128)(2,1)S(1)}, u32[]{:S(2)}, u32[]{:S(2)}) collective-permute-start(bf16[4,32,4096]{2,1,0:T(8,128)(2,1)S(1)} %bitcast.24), channel_id=1, source_target_pairs={{0,16},{16,0},{1,17},{17,1},{2,18},{18,2},{3,19},{19,3},{4,20},{20... | collective-permute-start | bytes 3145736 | tf_op jit(solution)/shard_map/ppermute | solution.py:31
  47.4 13.4 %collective-permute-start.9 = (bf16[64,896]{1,0:T(8,128)(2,1)S(1)}, bf16[64,896]{1,0:T(8,128)(2,1)S(1)}, u32[]{:S(2)}, u32[]{:S(2)}) collective-permute-start(bf16[64,896]{1,0:T(8,128)(2,1)S(1)} %get-tuple-element.46.refs_1_.refs_0_), channel_id=1, source_target_pairs={{0,3},{1,2},{2,1},{3,0},{4,7},{5,6},{6,5},{7,4},{8,11},{9,10},{10,... | collective-permute-start | bytes 344072 | tf_op jit(solution)/shard_map/ppermute | solution.py:31
  49.9 12.2 %collective-permute-start.8 = (bf16[64,896]{1,0:T(8,128)(2,1)S(1)}, bf16[64,896]{1,0:T(8,128)(2,1)S(1)}, u32[]{:S(2)}, u32[]{:S(2)}) collective-permute-start(bf16[64,896]{1,0:T(8,128)(2,1)S(1)} %get-tuple-element.46.refs_1_.refs_0_), channel_id=1, source_target_pairs={{0,2},{1,3},{2,0},{3,1},{4,6},{5,7},{6,4},{7,5},{8,10},{9,11},{10,... | collective-permute-start | bytes 344072 | tf_op jit(solution)/shard_map/ppermute | solution.py:31
  59.3 12.0 %collective-permute-start.22 = (bf16[80,896]{1,0:T(8,128)(2,1)S(1)}, bf16[80,896]{1,0:T(8,128)(2,1)S(1)}, u32[]{:S(2)}, u32[]{:S(2)}) collective-permute-start(bf16[80,896]{1,0:T(8,128)(2,1)S(1)} %get-tuple-element.49), channel_id=1, source_target_pairs={{0,2},{1,3},{2,0},{3,1},{4,6},{5,7},{6,4},{7,5},{8,10},{9,11},{10,... | collective-permute-start | bytes 430088 | tf_op jit(solution)/shard_map/ppermute | solution.py:31
  63.5 19.4 %collective-permute-start.16 = (bf16[272,896]{1,0:T(8,128)(2,1)S(1)}, bf16[272,896]{1,0:T(8,128)(2,1)S(1)}, u32[]{:S(2)}, u32[]{:S(2)}) collective-permute-start(bf16[272,896]{1,0:T(8,128)(2,1)S(1)} %shard_map.125.refs_4_.refs_0_), channel_id=1, source_target_pairs={{0,12},{4,8},{8,4},{12,0},{1,13},{5,9},{9,5},{13,1},{2,14},{6,10},... | collective-permute-start | bytes 1462280 | tf_op jit(solution)/shard_map/ppermute | solution.py:31
  65.2 18.6 %collective-permute-start.15 = (bf16[272,896]{1,0:T(8,128)(2,1)S(1)}, bf16[272,896]{1,0:T(8,128)(2,1)S(1)}, u32[]{:S(2)}, u32[]{:S(2)}) collective-permute-start(bf16[272,896]{1,0:T(8,128)(2,1)S(1)} %shard_map.125.refs_4_.refs_0_), channel_id=1, source_target_pairs={{0,8},{4,12},{8,0},{12,4},{1,9},{5,13},{9,1},{13,5},{2,10},{6,14},... | collective-permute-start | bytes 1462280 | tf_op jit(solution)/shard_map/ppermute | solution.py:31
  66.5 17.3 %collective-permute-start.14 = (bf16[272,896]{1,0:T(8,128)(2,1)S(1)}, bf16[272,896]{1,0:T(8,128)(2,1)S(1)}, u32[]{:S(2)}, u32[]{:S(2)}) collective-permute-start(bf16[272,896]{1,0:T(8,128)(2,1)S(1)} %shard_map.125.refs_4_.refs_0_), channel_id=1, source_target_pairs={{0,4},{4,0},{8,12},{12,8},{1,5},{5,1},{9,13},{13,9},{2,6},{6,2},{1... | collective-permute-start | bytes 1462280 | tf_op jit(solution)/shard_map/ppermute | solution.py:31
  86.5 18.7 %collective-permute-start.33 = (bf16[256,896]{1,0:T(8,128)(2,1)}, bf16[256,896]{1,0:T(8,128)(2,1)}, u32[]{:S(2)}, u32[]{:S(2)}) collective-permute-start(bf16[256,896]{1,0:T(8,128)(2,1)} %shard_map.131.refs_0_), channel_id=1, source_target_pairs={{0,12},{4,8},{8,4},{12,0},{1,13},{5,9},{9,5},{13,1},{2,14},{6,10},... | collective-permute-start | bytes 1376264 | tf_op jit(solution)/shard_map/ppermute | solution.py:31
  88.2 21.2 %collective-permute-start.32 = (bf16[256,896]{1,0:T(8,128)(2,1)}, bf16[256,896]{1,0:T(8,128)(2,1)}, u32[]{:S(2)}, u32[]{:S(2)}) collective-permute-start(bf16[256,896]{1,0:T(8,128)(2,1)} %shard_map.131.refs_0_), channel_id=1, source_target_pairs={{0,8},{4,12},{8,0},{12,4},{1,9},{5,13},{9,1},{13,5},{2,10},{6,14},... | collective-permute-start | bytes 1376264 | tf_op jit(solution)/shard_map/ppermute | solution.py:31
  89.5 19.9 %collective-permute-start.31 = (bf16[256,896]{1,0:T(8,128)(2,1)}, bf16[256,896]{1,0:T(8,128)(2,1)}, u32[]{:S(2)}, u32[]{:S(2)}) collective-permute-start(bf16[256,896]{1,0:T(8,128)(2,1)} %shard_map.131.refs_0_), channel_id=1, source_target_pairs={{0,4},{4,0},{8,12},{12,8},{1,5},{5,1},{9,13},{13,9},{2,6},{6,2},{1... | collective-permute-start | bytes 1376264 | tf_op jit(solution)/shard_map/ppermute | solution.py:31
  111.6 20.0 %collective-permute-start.25 = (bf16[256,896]{1,0:T(8,128)(2,1)}, bf16[256,896]{1,0:T(8,128)(2,1)}, u32[]{:S(2)}, u32[]{:S(2)}) collective-permute-start(bf16[256,896]{1,0:T(8,128)(2,1)} %get-tuple-element.54), channel_id=1, source_target_pairs={{0,4},{4,0},{8,12},{12,8},{1,5},{5,1},{9,13},{13,9},{2,6},{6,2},{1... | collective-permute-start | bytes 1376264 | tf_op jit(solution)/shard_map/ppermute | solution.py:31
  113.2 23.0 %collective-permute-start.26 = (bf16[256,896]{1,0:T(8,128)(2,1)}, bf16[256,896]{1,0:T(8,128)(2,1)}, u32[]{:S(2)}, u32[]{:S(2)}) collective-permute-start(bf16[256,896]{1,0:T(8,128)(2,1)} %get-tuple-element.55), channel_id=1, source_target_pairs={{0,8},{4,12},{8,0},{12,4},{1,9},{5,13},{9,1},{13,5},{2,10},{6,14},... | collective-permute-start | bytes 1376264 | tf_op jit(solution)/shard_map/ppermute | solution.py:31
  113.9 22.3 %collective-permute-start.27 = (bf16[256,896]{1,0:T(8,128)(2,1)}, bf16[256,896]{1,0:T(8,128)(2,1)}, u32[]{:S(2)}, u32[]{:S(2)}) collective-permute-start(bf16[256,896]{1,0:T(8,128)(2,1)} %get-tuple-element.56), channel_id=1, source_target_pairs={{0,12},{4,8},{8,4},{12,0},{1,13},{5,9},{9,5},{13,1},{2,14},{6,10},... | collective-permute-start | bytes 1376264 | tf_op jit(solution)/shard_map/ppermute | solution.py:31
  129.3 16.9 %collective-permute-start.39 = (bf16[128,896]{1,0:T(8,128)(2,1)S(1)}, bf16[128,896]{1,0:T(8,128)(2,1)S(1)}, u32[]{:S(2)}, u32[]{:S(2)}) collective-permute-start(bf16[128,896]{1,0:T(8,128)(2,1)S(1)} %get-tuple-element.67), channel_id=1, source_target_pairs={{0,4},{4,0},{8,12},{12,8},{1,5},{5,1},{9,13},{13,9},{2,6},{6,2},{1... | collective-permute-start | bytes 688136 | tf_op jit(solution)/shard_map/ppermute | solution.py:31
  130.9 16.2 %collective-permute-start.40 = (bf16[128,896]{1,0:T(8,128)(2,1)S(1)}, bf16[128,896]{1,0:T(8,128)(2,1)S(1)}, u32[]{:S(2)}, u32[]{:S(2)}) collective-permute-start(bf16[128,896]{1,0:T(8,128)(2,1)S(1)} %get-tuple-element.68), channel_id=1, source_target_pairs={{0,8},{4,12},{8,0},{12,4},{1,9},{5,13},{9,1},{13,5},{2,10},{6,14},... | collective-permute-start | bytes 688136 | tf_op jit(solution)/shard_map/ppermute | solution.py:31
  131.6 16.8 %collective-permute-start.41 = (bf16[128,896]{1,0:T(8,128)(2,1)S(1)}, bf16[128,896]{1,0:T(8,128)(2,1)S(1)}, u32[]{:S(2)}, u32[]{:S(2)}) collective-permute-start(bf16[128,896]{1,0:T(8,128)(2,1)S(1)} %get-tuple-element.69), channel_id=1, source_target_pairs={{0,12},{4,8},{8,4},{12,0},{1,13},{5,9},{9,5},{13,1},{2,14},{6,10},... | collective-permute-start | bytes 688136 | tf_op jit(solution)/shard_map/ppermute | solution.py:31
  138.5 11.3 %collective-permute-start.37 = (bf16[64,896]{1,0:T(8,128)(2,1)S(1)}, bf16[64,896]{1,0:T(8,128)(2,1)S(1)}, u32[]{:S(2)}, u32[]{:S(2)}) collective-permute-start(bf16[64,896]{1,0:T(8,128)(2,1)S(1)} %get-tuple-element.63), channel_id=1, source_target_pairs={{0,2},{1,3},{2,0},{3,1},{4,6},{5,7},{6,4},{7,5},{8,10},{9,11},{10,... | collective-permute-start | bytes 344072 | tf_op jit(solution)/shard_map/ppermute | solution.py:31
  (34 other events, 257.2 us)

commit v3 on v2

--- a/solution.py
+++ b/solution.py
@@ -544,7 +544,7 @@
     no_gain = jnp.zeros((2 * n_row, width), jnp.float32)
     [both_0], inverse_gain = experts(near_0, weight[0], no_gain, 1)
     rows_1 = stack(over_col([scaled_1] * n_col), near_0[1:])
-    near_1 = stack_rows(rows_1, both_0[:1])
+    near_1 = stack_rows(rows_1, both_0[1:])
     both_1, _ = experts([near_1], hand_on(weight[1], [near_1]), inverse_gain, 2)
     total_0 = reduce(over_row(both_0), n_col, True, both_1[0][:1])
     terms_0 = [hidden_0, *over_col(total_0)]

time: 164 us -> 161 us (0.982)
  waiting for transfers between devices: 42.8 us -> 40.2 us
    ppermute x48, waiting for transfers between devices: 42.8 us -> 40.2 us  [swap(): return lax.ppermute(x, axis, [(i, i ^ d) for i in range(count)])]
  transfers between devices with their start and end apart: 48 -> 48, of which waited for: 18 -> 18; matrix products, arithmetic and copies ran while one was open for 0% -> 0% of each run, Pallas kernels for 30% -> 32%
where the time goes in v3:
time: 161 us
  Pallas kernels  59.8 us (37%)
  starting transfers between devices  59.3 us (37%)
  waiting for transfers between devices  40.2 us (25%)
    ppermute x48, starting transfers between devices, swap(): return lax.ppermute(x, axis, [(i, i ^ d) for i in range(count)])  59.3 us
    ppermute x48, waiting for transfers between devices, swap(): return lax.ppermute(x, axis, [(i, i ^ d) for i in range(count)])  40.2 us
    pallas_call x2, Pallas kernels, gate_up(): pl.pallas_call(functools.partial(gate_up_kernel, len(pieces)), in_specs=[...  15.9 us
    pallas_call x2, Pallas kernels, attend(): pl.pallas_call(functools.partial(attend_kernel, (size + ROPE) ** (-0.5),...  15.4 us
    pallas_call x2, Pallas kernels, project(): pl.pallas_call(functools.partial(project_kernel, blocks, len(gate)), in_s...  11.2 us
    pallas_call x4, Pallas kernels, down(): pl.pallas_call(down_kernel, in_specs=[SMEM, VMEM, VMEM], out_specs=VMEM,...  7.5 us
    pallas_call x5, Pallas kernels, stack(): pl.pallas_call(functools.partial(stack_kernel, n), in_specs=[ANY] * (n +...  5.38 us
  transfers between devices with their start and end apart: 48, of which 18 were waited for; matrix products, arithmetic and copies ran while one was open for 0% of the time, Pallas kernels for 32%

profile of v3, /device:TPU:0, one launch (start us, length us, event | category | flops | bytes accessed | tf_op | source)
XLA Modules:
  0.0 161.0 jit_solution(6500446376395991037)
XLA Ops:
  0.7 7.7 %shard_map.118.refs_0_ = bf16[32,4096]{1,0:T(8,128)(2,1)S(1)} custom-call(s32[64]{0:T(128)S(1)} %copy-done.3, bf16[64,32,576]{2,1,0:T(8,128)(2,1)} %q_ref.3, bf16[64,576,128]{2,1,0:T(8,128)(2,1)} %bitcast.36, bf16[32,512,128]{2,1,0:T(8,128)(2,1)} %w_hbm.5), custom_call_target="tpu_custom_call" | custom-call | flops 99999997952 | bytes 1024 | tf_op jit(solution)/shard_map/pallas_call | solution.py:444
  8.3 4.0 %collective-permute-start.2 = (bf16[32,4096]{1,0:T(8,128)(2,1)S(1)}, bf16[32,4096]{1,0:T(8,128)(2,1)S(1)}, u32[]{:S(2)}, u32[]{:S(2)}) collective-permute-start(bf16[32,4096]{1,0:T(8,128)(2,1)S(1)} %shard_map.118.refs_0_), channel_id=1, source_target_pairs={{0,12},{4,8},{8,4},{12,0},{1,13},{5,9},{9,5},{13,1},{2,14},{6,10},... | collective-permute-start | bytes 786440 | tf_op jit(solution)/shard_map/ppermute | solution.py:31
  12.9 7.7 %shard_map.119.refs_4_.refs_0_ = bf16[32,4096]{1,0:T(8,128)(2,1)S(1)} custom-call(s32[64]{0:T(128)S(1)} %copy-done.3, bf16[64,32,576]{2,1,0:T(8,128)(2,1)} %q_ref.3, bf16[64,576,128]{2,1,0:T(8,128)(2,1)} %bitcast.37, bf16[32,512,128]{2,1,0:T(8,128)(2,1)} %w_hbm.5, bf16[32,4096]{1,0:T(8,128)(2,1)S(1)} %shard_map.118.refs_0_), custom_call_target="tpu_custom_call" | custom-call | flops 99999997952 | bytes 1024 | tf_op jit(solution)/shard_map/pallas_call | solution.py:444
  20.6 3.6 %collective-permute-done.1.refs_2_ = bf16[32,4096]{1,0:T(8,128)(2,1)S(1)} collective-permute-done((bf16[32,4096]{1,0:T(8,128)(2,1)S(1)}, bf16[32,4096]{1,0:T(8,128)(2,1)S(1)}, u32[]{:S(2)}, u32[]{:S(2)}) %collective-permute-start.1) | collective-permute-done | bytes 262176 | tf_op jit(solution)/shard_map/ppermute | solution.py:31
  28.5 5.6 %shard_map.121 = (bf16[64,896]{1,0:T(8,128)(2,1)S(1)}, bf16[64,896]{1,0:T(8,128)(2,1)S(1)}, bf16[64,896]{1,0:T(8,128)(2,1)S(1)}, bf16[64,896]{1,0:T(8,128)(2,1)S(1)}) custom-call(s32[8]{0:T(128)S(1)} %fusion.pos_ref, bf16[4,32,4096]{2,1,0:T(8,128)(2,1)S(1)} %bitcast.23, bf16[4,32,4096]{2,1,0:T(8,128)(2,1)S(1)} %collective-permute-done.3.far_ref, ...), custom_call_target="tpu_custom_call" | custom-call | flops 99999997952 | bytes 1024 | tf_op jit(solution)/shard_map/pallas_call | solution.py:144
  35.8 2.6 %collective-permute-start.5 = (bf16[64,896]{1,0:T(8,128)(2,1)S(1)}, bf16[64,896]{1,0:T(8,128)(2,1)S(1)}, u32[]{:S(2)}, u32[]{:S(2)}) collective-permute-start(bf16[64,896]{1,0:T(8,128)(2,1)S(1)} %get-tuple-element.43), channel_id=1, source_target_pairs={{0,2},{1,3},{2,0},{3,1},{4,6},{5,7},{6,4},{7,5},{8,10},{9,11},{10,... | collective-permute-start | bytes 344072 | tf_op jit(solution)/shard_map/ppermute | solution.py:31
  40.4 6.8 %collective-permute-done.5.refs_2_ = bf16[64,896]{1,0:T(8,128)(2,1)S(1)} collective-permute-done((bf16[64,896]{1,0:T(8,128)(2,1)S(1)}, bf16[64,896]{1,0:T(8,128)(2,1)S(1)}, u32[]{:S(2)}, u32[]{:S(2)}) %collective-permute-start.5) | collective-permute-done | bytes 114720 | tf_op jit(solution)/shard_map/ppermute | solution.py:31
  47.4 2.5 %collective-permute-start.9 = (bf16[64,896]{1,0:T(8,128)(2,1)S(1)}, bf16[64,896]{1,0:T(8,128)(2,1)S(1)}, u32[]{:S(2)}, u32[]{:S(2)}) collective-permute-start(bf16[64,896]{1,0:T(8,128)(2,1)S(1)} %get-tuple-element.46.refs_1_.refs_0_), channel_id=1, source_target_pairs={{0,3},{1,2},{2,1},{3,0},{4,7},{5,6},{6,5},{7,4},{8,11},{9,10},{10,... | collective-permute-start | bytes 344072 | tf_op jit(solution)/shard_map/ppermute | solution.py:31
  52.0 5.6 %shard_map.124 = (bf16[80,896]{1,0:T(8,128)(2,1)S(1)}, bf16[80,896]{1,0:T(8,128)(2,1)S(1)}, bf16[80,896]{1,0:T(8,128)(2,1)S(1)}, bf16[80,896]{1,0:T(8,128)(2,1)S(1)}) custom-call(s32[8]{0:T(128)S(1)} %fusion.pos_ref, bf16[4,32,4096]{2,1,0:T(8,128)(2,1)S(1)} %bitcast.25, bf16[4,32,4096]{2,1,0:T(8,128)(2,1)S(1)} %collective-permute-done.13.far_ref, ...), custom_call_target="tpu_custom_call" | custom-call | flops 99999997952 | bytes 1024 | tf_op jit(solution)/shard_map/pallas_call | solution.py:144
  67.1 4.2 %collective-permute-done.22.refs_2_ = bf16[80,896]{1,0:T(8,128)(2,1)S(1)} collective-permute-done((bf16[80,896]{1,0:T(8,128)(2,1)S(1)}, bf16[80,896]{1,0:T(8,128)(2,1)S(1)}, u32[]{:S(2)}, u32[]{:S(2)}) %collective-permute-start.22) | collective-permute-done | bytes 143392 | tf_op jit(solution)/shard_map/ppermute | solution.py:31
  71.4 2.5 %collective-permute-start.30 = (bf16[64,896]{1,0:T(8,128)(2,1)S(1)}, bf16[64,896]{1,0:T(8,128)(2,1)S(1)}, u32[]{:S(2)}, u32[]{:S(2)}) collective-permute-start(bf16[64,896]{1,0:T(8,128)(2,1)S(1)} %get-tuple-element.57.refs_0_), channel_id=1, source_target_pairs={{0,3},{1,2},{2,1},{3,0},{4,7},{5,6},{6,5},{7,4},{8,11},{9,10},{10,... | collective-permute-start | bytes 344072 | tf_op jit(solution)/shard_map/ppermute | solution.py:31
  75.3 3.6 %collective-permute-done.30.refs_3_ = bf16[64,896]{1,0:T(8,128)(2,1)S(1)} collective-permute-done((bf16[64,896]{1,0:T(8,128)(2,1)S(1)}, bf16[64,896]{1,0:T(8,128)(2,1)S(1)}, u32[]{:S(2)}, u32[]{:S(2)}) %collective-permute-start.30) | collective-permute-done | bytes 114720 | tf_op jit(solution)/shard_map/ppermute | solution.py:31
  78.9 3.4 %collective-permute-start.28 = (bf16[64,896]{1,0:T(8,128)(2,1)S(1)}, bf16[64,896]{1,0:T(8,128)(2,1)S(1)}, u32[]{:S(2)}, u32[]{:S(2)}) collective-permute-start(bf16[64,896]{1,0:T(8,128)(2,1)S(1)} %get-tuple-element.57.refs_0_), channel_id=1, source_target_pairs={{0,1},{1,0},{2,3},{3,2},{4,5},{5,4},{6,7},{7,6},{8,9},{9,8},{10,11... | collective-permute-start | bytes 344072 | tf_op jit(solution)/shard_map/ppermute | solution.py:31
  90.0 8.1 %shard_map.127 = (bf16[256,512]{1,0:T(8,128)(2,1)S(1)}, f32[4,1792]{1,0:T(4,128)S(1)}) custom-call(s32[8]{0:T(128)S(1)} %stack.39.idx_ref, bf16[272,896]{1,0:T(8,128)(2,1)S(1)} %shard_map.125.refs_4_.refs_0_, bf16[272,896]{1,0:T(8,128)(2,1)S(1)} %collective-permute-done.14.refs_1_.refs_4_, bf16[272,896]{1,0:T(8,128)(2,1)S(1)} %collective-permute-done.15.refs_2_.refs_5_, ...), custom_call_target="tpu_custom_call" | custom-call | flops 99999997952 | bytes 1024 | tf_op jit(solution)/shard_map/pallas_call | solution.py:255
  102.0 1.9 %collective-permute-done.24.got_ref = bf16[4,256,896]{2,1,0:T(8,128)(2,1)S(1)} collective-permute-done((bf16[4,256,896]{2,1,0:T(8,128)(2,1)S(1)}, bf16[4,256,896]{2,1,0:T(8,128)(2,1)S(1)}, u32[]{:S(2)}, u32[]{:S(2)}) %collective-permute-start.24) | collective-permute-done | bytes 1835040 | tf_op jit(solution)/shard_map/ppermute | solution.py:31
  110.4 2.2 %shard_map.132 = bf16[1024,896]{1,0:T(8,128)(2,1)S(1)} custom-call(bf16[256,896]{1,0:T(8,128)(2,1)} %shard_map.131.refs_0_, bf16[256,896]{1,0:T(8,128)(2,1)} %collective-permute-done.31.refs_1_, bf16[256,896]{1,0:T(8,128)(2,1)} %collective-permute-done.32.refs_2_, bf16[256,896]{1,0:T(8,128)(2,1)} %collective-permute-done.33.refs_3_, ...), custom_call_target="tpu_custom_call" | custom-call | flops 99999997952 | bytes 1024 | tf_op jit(solution)/shard_map/pallas_call | solution.py:57
  112.7 3.8 %collective-permute-done.34.refs_1_ = bf16[4,256,896]{2,1,0:T(8,128)(2,1)S(1)} collective-permute-done((bf16[4,256,896]{2,1,0:T(8,128)(2,1)S(1)}, bf16[4,256,896]{2,1,0:T(8,128)(2,1)S(1)}, u32[]{:S(2)}, u32[]{:S(2)}) %collective-permute-start.34) | collective-permute-done | bytes 1835040 | tf_op jit(solution)/shard_map/ppermute | solution.py:31
  116.4 7.8 %shard_map.134 = (bf16[256,512]{1,0:T(8,128)(2,1)S(1)}, f32[4,1792]{1,0:T(4,128)}) custom-call(s32[8]{0:T(128)S(1)} %stack.39.idx_ref, bf16[4,256,896]{2,1,0:T(8,128)(2,1)S(1)} %bitcast.33, bf16[4,256,896]{2,1,0:T(8,128)(2,1)S(1)} %collective-permute-done.34.refs_1_, bf16[7168,512]{1,0:T(8,128)(2,1)} %bitcast.39, bf16[7168,512]{1,0:T(8,128)(2,1)} %bitcast.41, ...), custom_call_target="tpu_custom_call" | custom-call | flops 99999997952 | bytes 1024 | tf_op jit(solution)/shard_map/pallas_call | solution.py:255
  135.8 3.0 %collective-permute-start.37 = (bf16[64,896]{1,0:T(8,128)(2,1)S(1)}, bf16[64,896]{1,0:T(8,128)(2,1)S(1)}, u32[]{:S(2)}, u32[]{:S(2)}) collective-permute-start(bf16[64,896]{1,0:T(8,128)(2,1)S(1)} %get-tuple-element.63), channel_id=1, source_target_pairs={{0,2},{1,3},{2,0},{3,1},{4,6},{5,7},{6,4},{7,5},{8,10},{9,11},{10,... | collective-permute-start | bytes 344072 | tf_op jit(solution)/shard_map/ppermute | solution.py:31
  138.8 2.8 %collective-permute-done.36.refs_5_.refs_2_ = bf16[64,896]{1,0:T(8,128)(2,1)S(1)} collective-permute-done((bf16[64,896]{1,0:T(8,128)(2,1)S(1)}, bf16[64,896]{1,0:T(8,128)(2,1)S(1)}, u32[]{:S(2)}, u32[]{:S(2)}) %collective-permute-start.36) | collective-permute-done | bytes 114720 | tf_op jit(solution)/shard_map/ppermute | solution.py:31
  141.6 2.6 %collective-permute-start.38 = (bf16[64,896]{1,0:T(8,128)(2,1)S(1)}, bf16[64,896]{1,0:T(8,128)(2,1)S(1)}, u32[]{:S(2)}, u32[]{:S(2)}) collective-permute-start(bf16[64,896]{1,0:T(8,128)(2,1)S(1)} %get-tuple-element.64), channel_id=1, source_target_pairs={{0,3},{1,2},{2,1},{3,0},{4,7},{5,6},{6,5},{7,4},{8,11},{9,10},{10,... | collective-permute-start | bytes 344072 | tf_op jit(solution)/shard_map/ppermute | solution.py:31
  149.2 4.1 %collective-permute-start.42 = (bf16[64,896]{1,0:T(8,128)(2,1)S(1)}, bf16[64,896]{1,0:T(8,128)(2,1)S(1)}, u32[]{:S(2)}, u32[]{:S(2)}) collective-permute-start(bf16[64,896]{1,0:T(8,128)(2,1)S(1)} %get-tuple-element.70.refs_4_), channel_id=1, source_target_pairs={{0,2},{1,3},{2,0},{3,1},{4,6},{5,7},{6,4},{7,5},{8,10},{9,11},{10,... | collective-permute-start | bytes 344072 | tf_op jit(solution)/shard_map/ppermute | solution.py:31
  153.2 2.0 %collective-permute-done.45.refs_2_ = bf16[128,896]{1,0:T(8,128)(2,1)S(1)} collective-permute-done((bf16[128,896]{1,0:T(8,128)(2,1)S(1)}, bf16[128,896]{1,0:T(8,128)(2,1)S(1)}, u32[]{:S(2)}, u32[]{:S(2)}) %collective-permute-start.45) | collective-permute-done | bytes 229408 | tf_op jit(solution)/shard_map/ppermute | solution.py:31
  155.4 2.9 %collective-permute-done.42.refs_1_ = bf16[64,896]{1,0:T(8,128)(2,1)S(1)} collective-permute-done((bf16[64,896]{1,0:T(8,128)(2,1)S(1)}, bf16[64,896]{1,0:T(8,128)(2,1)S(1)}, u32[]{:S(2)}, u32[]{:S(2)}) %collective-permute-start.42) | collective-permute-done | bytes 114720 | tf_op jit(solution)/shard_map/ppermute | solution.py:31
  (129 shorter events, 59.7 us)
Async XLA Ops:
  8.3 12.3 %collective-permute-start.2 = (bf16[32,4096]{1,0:T(8,128)(2,1)S(1)}, bf16[32,4096]{1,0:T(8,128)(2,1)S(1)}, u32[]{:S(2)}, u32[]{:S(2)}) collective-permute-start(bf16[32,4096]{1,0:T(8,128)(2,1)S(1)} %shard_map.118.refs_0_), channel_id=1, source_target_pairs={{0,12},{4,8},{8,4},{12,0},{1,13},{5,9},{9,5},{13,1},{2,14},{6,10},... | collective-permute-start | bytes 786440 | tf_op jit(solution)/shard_map/ppermute | solution.py:31
  12.3 11.9 %collective-permute-start.1 = (bf16[32,4096]{1,0:T(8,128)(2,1)S(1)}, bf16[32,4096]{1,0:T(8,128)(2,1)S(1)}, u32[]{:S(2)}, u32[]{:S(2)}) collective-permute-start(bf16[32,4096]{1,0:T(8,128)(2,1)S(1)} %shard_map.118.refs_0_), channel_id=1, source_target_pairs={{0,8},{4,12},{8,0},{12,4},{1,9},{5,13},{9,1},{13,5},{2,10},{6,14},... | collective-permute-start | bytes 786440 | tf_op jit(solution)/shard_map/ppermute | solution.py:31
  12.8 11.7 %collective-permute-start = (bf16[32,4096]{1,0:T(8,128)(2,1)S(1)}, bf16[32,4096]{1,0:T(8,128)(2,1)S(1)}, u32[]{:S(2)}, u32[]{:S(2)}) collective-permute-start(bf16[32,4096]{1,0:T(8,128)(2,1)S(1)} %shard_map.118.refs_0_), channel_id=1, source_target_pairs={{0,4},{4,0},{8,12},{12,8},{1,5},{5,1},{9,13},{13,9},{2,6},{6,2},{1... | collective-permute-start | bytes 786440 | tf_op jit(solution)/shard_map/ppermute | solution.py:31
  24.8 13.6 %collective-permute-start.12 = (bf16[32,4096]{1,0:T(8,128)(2,1)S(1)}, bf16[32,4096]{1,0:T(8,128)(2,1)S(1)}, u32[]{:S(2)}, u32[]{:S(2)}) collective-permute-start(bf16[32,4096]{1,0:T(8,128)(2,1)S(1)} %shard_map.119.refs_4_.refs_0_), channel_id=1, source_target_pairs={{0,12},{4,8},{8,4},{12,0},{1,13},{5,9},{9,5},{13,1},{2,14},{6,10},... | collective-permute-start | bytes 786440 | tf_op jit(solution)/shard_map/ppermute | solution.py:31
  26.4 13.6 %collective-permute-start.11 = (bf16[32,4096]{1,0:T(8,128)(2,1)S(1)}, bf16[32,4096]{1,0:T(8,128)(2,1)S(1)}, u32[]{:S(2)}, u32[]{:S(2)}) collective-permute-start(bf16[32,4096]{1,0:T(8,128)(2,1)S(1)} %shard_map.119.refs_4_.refs_0_), channel_id=1, source_target_pairs={{0,8},{4,12},{8,0},{12,4},{1,9},{5,13},{9,1},{13,5},{2,10},{6,14},... | collective-permute-start | bytes 786440 | tf_op jit(solution)/shard_map/ppermute | solution.py:31
  27.9 12.2 %collective-permute-start.10 = (bf16[32,4096]{1,0:T(8,128)(2,1)S(1)}, bf16[32,4096]{1,0:T(8,128)(2,1)S(1)}, u32[]{:S(2)}, u32[]{:S(2)}) collective-permute-start(bf16[32,4096]{1,0:T(8,128)(2,1)S(1)} %shard_map.119.refs_4_.refs_0_), channel_id=1, source_target_pairs={{0,4},{4,0},{8,12},{12,8},{1,5},{5,1},{9,13},{13,9},{2,6},{6,2},{1... | collective-permute-start | bytes 786440 | tf_op jit(solution)/shard_map/ppermute | solution.py:31
  35.8 11.5 %collective-permute-start.5 = (bf16[64,896]{1,0:T(8,128)(2,1)S(1)}, bf16[64,896]{1,0:T(8,128)(2,1)S(1)}, u32[]{:S(2)}, u32[]{:S(2)}) collective-permute-start(bf16[64,896]{1,0:T(8,128)(2,1)S(1)} %get-tuple-element.43), channel_id=1, source_target_pairs={{0,2},{1,3},{2,0},{3,1},{4,6},{5,7},{6,4},{7,5},{8,10},{9,11},{10,... | collective-permute-start | bytes 344072 | tf_op jit(solution)/shard_map/ppermute | solution.py:31
  40.3 11.7 %collective-permute-start.13 = (bf16[4,32,4096]{2,1,0:T(8,128)(2,1)S(1)}, bf16[4,32,4096]{2,1,0:T(8,128)(2,1)S(1)}, u32[]{:S(2)}, u32[]{:S(2)}) collective-permute-start(bf16[4,32,4096]{2,1,0:T(8,128)(2,1)S(1)} %bitcast.24), channel_id=1, source_target_pairs={{0,16},{16,0},{1,17},{17,1},{2,18},{18,2},{3,19},{19,3},{4,20},{20... | collective-permute-start | bytes 3145736 | tf_op jit(solution)/shard_map/ppermute | solution.py:31
  47.4 13.4 %collective-permute-start.9 = (bf16[64,896]{1,0:T(8,128)(2,1)S(1)}, bf16[64,896]{1,0:T(8,128)(2,1)S(1)}, u32[]{:S(2)}, u32[]{:S(2)}) collective-permute-start(bf16[64,896]{1,0:T(8,128)(2,1)S(1)} %get-tuple-element.46.refs_1_.refs_0_), channel_id=1, source_target_pairs={{0,3},{1,2},{2,1},{3,0},{4,7},{5,6},{6,5},{7,4},{8,11},{9,10},{10,... | collective-permute-start | bytes 344072 | tf_op jit(solution)/shard_map/ppermute | solution.py:31
  49.9 12.2 %collective-permute-start.8 = (bf16[64,896]{1,0:T(8,128)(2,1)S(1)}, bf16[64,896]{1,0:T(8,128)(2,1)S(1)}, u32[]{:S(2)}, u32[]{:S(2)}) collective-permute-start(bf16[64,896]{1,0:T(8,128)(2,1)S(1)} %get-tuple-element.46.refs_1_.refs_0_), channel_id=1, source_target_pairs={{0,2},{1,3},{2,0},{3,1},{4,6},{5,7},{6,4},{7,5},{8,10},{9,11},{10,... | collective-permute-start | bytes 344072 | tf_op jit(solution)/shard_map/ppermute | solution.py:31
  59.3 12.0 %collective-permute-start.22 = (bf16[80,896]{1,0:T(8,128)(2,1)S(1)}, bf16[80,896]{1,0:T(8,128)(2,1)S(1)}, u32[]{:S(2)}, u32[]{:S(2)}) collective-permute-start(bf16[80,896]{1,0:T(8,128)(2,1)S(1)} %get-tuple-element.49), channel_id=1, source_target_pairs={{0,2},{1,3},{2,0},{3,1},{4,6},{5,7},{6,4},{7,5},{8,10},{9,11},{10,... | collective-permute-start | bytes 430088 | tf_op jit(solution)/shard_map/ppermute | solution.py:31
  63.5 19.4 %collective-permute-start.16 = (bf16[272,896]{1,0:T(8,128)(2,1)S(1)}, bf16[272,896]{1,0:T(8,128)(2,1)S(1)}, u32[]{:S(2)}, u32[]{:S(2)}) collective-permute-start(bf16[272,896]{1,0:T(8,128)(2,1)S(1)} %shard_map.125.refs_4_.refs_0_), channel_id=1, source_target_pairs={{0,12},{4,8},{8,4},{12,0},{1,13},{5,9},{9,5},{13,1},{2,14},{6,10},... | collective-permute-start | bytes 1462280 | tf_op jit(solution)/shard_map/ppermute | solution.py:31
  65.2 18.6 %collective-permute-start.15 = (bf16[272,896]{1,0:T(8,128)(2,1)S(1)}, bf16[272,896]{1,0:T(8,128)(2,1)S(1)}, u32[]{:S(2)}, u32[]{:S(2)}) collective-permute-start(bf16[272,896]{1,0:T(8,128)(2,1)S(1)} %shard_map.125.refs_4_.refs_0_), channel_id=1, source_target_pairs={{0,8},{4,12},{8,0},{12,4},{1,9},{5,13},{9,1},{13,5},{2,10},{6,14},... | collective-permute-start | bytes 1462280 | tf_op jit(solution)/shard_map/ppermute | solution.py:31
  66.5 17.3 %collective-permute-start.14 = (bf16[272,896]{1,0:T(8,128)(2,1)S(1)}, bf16[272,896]{1,0:T(8,128)(2,1)S(1)}, u32[]{:S(2)}, u32[]{:S(2)}) collective-permute-start(bf16[272,896]{1,0:T(8,128)(2,1)S(1)} %shard_map.125.refs_4_.refs_0_), channel_id=1, source_target_pairs={{0,4},{4,0},{8,12},{12,8},{1,5},{5,1},{9,13},{13,9},{2,6},{6,2},{1... | collective-permute-start | bytes 1462280 | tf_op jit(solution)/shard_map/ppermute | solution.py:31
  86.5 20.9 %collective-permute-start.33 = (bf16[256,896]{1,0:T(8,128)(2,1)}, bf16[256,896]{1,0:T(8,128)(2,1)}, u32[]{:S(2)}, u32[]{:S(2)}) collective-permute-start(bf16[256,896]{1,0:T(8,128)(2,1)} %shard_map.131.refs_0_), channel_id=1, source_target_pairs={{0,12},{4,8},{8,4},{12,0},{1,13},{5,9},{9,5},{13,1},{2,14},{6,10},... | collective-permute-start | bytes 1376264 | tf_op jit(solution)/shard_map/ppermute | solution.py:31
  88.2 21.2 %collective-permute-start.32 = (bf16[256,896]{1,0:T(8,128)(2,1)}, bf16[256,896]{1,0:T(8,128)(2,1)}, u32[]{:S(2)}, u32[]{:S(2)}) collective-permute-start(bf16[256,896]{1,0:T(8,128)(2,1)} %shard_map.131.refs_0_), channel_id=1, source_target_pairs={{0,8},{4,12},{8,0},{12,4},{1,9},{5,13},{9,1},{13,5},{2,10},{6,14},... | collective-permute-start | bytes 1376264 | tf_op jit(solution)/shard_map/ppermute | solution.py:31
  89.5 20.9 %collective-permute-start.31 = (bf16[256,896]{1,0:T(8,128)(2,1)}, bf16[256,896]{1,0:T(8,128)(2,1)}, u32[]{:S(2)}, u32[]{:S(2)}) collective-permute-start(bf16[256,896]{1,0:T(8,128)(2,1)} %shard_map.131.refs_0_), channel_id=1, source_target_pairs={{0,4},{4,0},{8,12},{12,8},{1,5},{5,1},{9,13},{13,9},{2,6},{6,2},{1... | collective-permute-start | bytes 1376264 | tf_op jit(solution)/shard_map/ppermute | solution.py:31
  105.2 27.3 %collective-permute-start.25 = (bf16[256,896]{1,0:T(8,128)(2,1)}, bf16[256,896]{1,0:T(8,128)(2,1)}, u32[]{:S(2)}, u32[]{:S(2)}) collective-permute-start(bf16[256,896]{1,0:T(8,128)(2,1)} %get-tuple-element.54.refs_4_), channel_id=1, source_target_pairs={{0,4},{4,0},{8,12},{12,8},{1,5},{5,1},{9,13},{13,9},{2,6},{6,2},{1... | collective-permute-start | bytes 1376264 | tf_op jit(solution)/shard_map/ppermute | solution.py:31
  106.6 27.3 %collective-permute-start.26 = (bf16[256,896]{1,0:T(8,128)(2,1)}, bf16[256,896]{1,0:T(8,128)(2,1)}, u32[]{:S(2)}, u32[]{:S(2)}) collective-permute-start(bf16[256,896]{1,0:T(8,128)(2,1)} %get-tuple-element.55.refs_5_), channel_id=1, source_target_pairs={{0,8},{4,12},{8,0},{12,4},{1,9},{5,13},{9,1},{13,5},{2,10},{6,14},... | collective-permute-start | bytes 1376264 | tf_op jit(solution)/shard_map/ppermute | solution.py:31
  107.4 26.6 %collective-permute-start.27 = (bf16[256,896]{1,0:T(8,128)(2,1)}, bf16[256,896]{1,0:T(8,128)(2,1)}, u32[]{:S(2)}, u32[]{:S(2)}) collective-permute-start(bf16[256,896]{1,0:T(8,128)(2,1)} %get-tuple-element.56.refs_6_), channel_id=1, source_target_pairs={{0,12},{4,8},{8,4},{12,0},{1,13},{5,9},{9,5},{13,1},{2,14},{6,10},... | collective-permute-start | bytes 1376264 | tf_op jit(solution)/shard_map/ppermute | solution.py:31
  130.4 13.8 %collective-permute-start.39 = (bf16[128,896]{1,0:T(8,128)(2,1)S(1)}, bf16[128,896]{1,0:T(8,128)(2,1)S(1)}, u32[]{:S(2)}, u32[]{:S(2)}) collective-permute-start(bf16[128,896]{1,0:T(8,128)(2,1)S(1)} %get-tuple-element.67), channel_id=1, source_target_pairs={{0,4},{4,0},{8,12},{12,8},{1,5},{5,1},{9,13},{13,9},{2,6},{6,2},{1... | collective-permute-start | bytes 688136 | tf_op jit(solution)/shard_map/ppermute | solution.py:31
  131.0 13.9 %collective-permute-start.40 = (bf16[128,896]{1,0:T(8,128)(2,1)S(1)}, bf16[128,896]{1,0:T(8,128)(2,1)S(1)}, u32[]{:S(2)}, u32[]{:S(2)}) collective-permute-start(bf16[128,896]{1,0:T(8,128)(2,1)S(1)} %get-tuple-element.68), channel_id=1, source_target_pairs={{0,8},{4,12},{8,0},{12,4},{1,9},{5,13},{9,1},{13,5},{2,10},{6,14},... | collective-permute-start | bytes 688136 | tf_op jit(solution)/shard_map/ppermute | solution.py:31
  132.4 13.6 %collective-permute-start.41 = (bf16[128,896]{1,0:T(8,128)(2,1)S(1)}, bf16[128,896]{1,0:T(8,128)(2,1)S(1)}, u32[]{:S(2)}, u32[]{:S(2)}) collective-permute-start(bf16[128,896]{1,0:T(8,128)(2,1)S(1)} %get-tuple-element.69), channel_id=1, source_target_pairs={{0,12},{4,8},{8,4},{12,0},{1,13},{5,9},{9,5},{13,1},{2,14},{6,10},... | collective-permute-start | bytes 688136 | tf_op jit(solution)/shard_map/ppermute | solution.py:31
  135.8 12.0 %collective-permute-start.37 = (bf16[64,896]{1,0:T(8,128)(2,1)S(1)}, bf16[64,896]{1,0:T(8,128)(2,1)S(1)}, u32[]{:S(2)}, u32[]{:S(2)}) collective-permute-start(bf16[64,896]{1,0:T(8,128)(2,1)S(1)} %get-tuple-element.63), channel_id=1, source_target_pairs={{0,2},{1,3},{2,0},{3,1},{4,6},{5,7},{6,4},{7,5},{8,10},{9,11},{10,... | collective-permute-start | bytes 344072 | tf_op jit(solution)/shard_map/ppermute | solution.py:31
  (34 other events, 254.3 us)

commit v4 on v3

--- a/solution.py
+++ b/solution.py
@@ -276,7 +276,8 @@
     )(owners, *pieces, in_hbm(w_gate), in_hbm(w_up), weight, gain.reshape(groups, wide))
 
 
-def down_kernel(idx_ref, act_ref, w_ref, out_ref):
+def down_kernel(idx_ref, act_ref, w_ref, *refs):
+    out_ref = refs[-1]
     m, _, width = out_ref.shape
 
     @pl.loop(0, m // 2)
@@ -289,7 +290,7 @@
         out_ref[2 * j + 1 - swapped] = both[:, width:].astype(jnp.bfloat16)
 
 
-def down(act, owners, w_down, width):
+def down(act, owners, w_down, width, after):
     rows, units = act.shape
     m = owners.shape[0]
     if width % 128 or m % 2:
@@ -301,12 +302,12 @@
         )
     return pl.pallas_call(
         down_kernel,
-        in_specs=[SMEM, VMEM, VMEM],
+        in_specs=[SMEM, VMEM, VMEM] + [ANY] * len(after),
         out_specs=VMEM,
         out_shape=jax.ShapeDtypeStruct((m, rows, width), jnp.bfloat16),
         compiler_params=pltpu.CompilerParams(vmem_limit_bytes=8 * MIB),
         cost_estimate=HEAVY,
-    )(owners, act, w_down)
+    )(owners, act, w_down, *after)
 
 
 def combine_kernel(n, parts, near_ref, got_ref, *outs):
@@ -517,13 +518,10 @@
     def other_core(x):
         return swap(x, "side", 2, 1)
 
-    def experts(near, held, inverse_gain, parts):
-        far = [other_core(piece) for piece in near]
-        act, inverse_gain = gate_up(
-            near + far, owners, gate_dev, up_dev, held, inverse_gain
-        )
-        far_rows = down(act, owners[n_row:], down_dev, width)
-        near_rows = down(act, owners[:n_row], down_dev, width)
+    def experts(pieces, held, inverse_gain, parts, after):
+        act, inverse_gain = gate_up(pieces, owners, gate_dev, up_dev, held, inverse_gain)
+        far_rows = down(act, owners[n_row:], down_dev, width, [])
+        near_rows = down(act, owners[:n_row], down_dev, width, after)
         return combine(near_rows, other_core(far_rows), parts), inverse_gain
 
     def stack_rows(x, after, estimate=HEAVY):
@@ -541,11 +539,15 @@
     weight = gates.reshape(n_col, per, chunks, part)
     weight = [weight[:, :, c].reshape(-1, 1) for c in range(chunks)]
     near_0 = over_row([rows_0] * n_row)
+    far_0 = [other_core(piece) for piece in near_0]
     no_gain = jnp.zeros((2 * n_row, width), jnp.float32)
-    [both_0], inverse_gain = experts(near_0, weight[0], no_gain, 1)
     rows_1 = stack(over_col([scaled_1] * n_col), near_0[1:])
-    near_1 = stack_rows(rows_1, both_0[1:])
-    both_1, _ = experts([near_1], hand_on(weight[1], [near_1]), inverse_gain, 2)
+    far_own = other_core(rows_1)
+    [both_0], inverse_gain = experts(near_0 + far_0, weight[0], no_gain, 1, [far_own])
+    near_1 = stack(over_row([rows_1] * n_row)[1:], both_0[1:])
+    near_1 = near_1.reshape(n_row - 1, *rows_1.shape)
+    pieces = [rows_1, near_1, far_own, other_core(near_1)]
+    both_1, _ = experts(pieces, hand_on(weight[1], [near_1]), inverse_gain, 2, [])
     total_0 = reduce(over_row(both_0), n_col, True, both_1[0][:1])
     terms_0 = [hidden_0, *over_col(total_0)]
     half = n_col // 2

time: 161 us -> 161 us (level)
  starting transfers between devices: 59.3 us -> 54.4 us
  waiting for transfers between devices: 40.2 us -> 45 us
    ppermute x48 -> x49, starting transfers between devices: 59.3 us -> 54.4 us  [swap(): return lax.ppermute(x, axis, [(i, i ^ d) for i in range(count)])]
    ppermute x48 -> x49, waiting for transfers between devices: 40.2 us -> 45 us  [swap(): return lax.ppermute(x, axis, [(i, i ^ d) for i in range(count)])]
  transfers between devices with their start and end apart: 48 -> 49, of which waited for: 18 -> 15; matrix products, arithmetic and copies ran while one was open for 0% -> 0% of each run, Pallas kernels for 32% -> 32%
where the time goes in v4:
time: 161 us; the launch traced here: 160 us
  Pallas kernels  59.3 us (37%)
  starting transfers between devices  54.4 us (34%)
  waiting for transfers between devices  45 us (28%)
    ppermute x49, starting transfers between devices, swap(): return lax.ppermute(x, axis, [(i, i ^ d) for i in range(count)])  54.4 us
    ppermute x49, waiting for transfers between devices, swap(): return lax.ppermute(x, axis, [(i, i ^ d) for i in range(count)])  45 us
    pallas_call x2, Pallas kernels, gate_up(): pl.pallas_call(functools.partial(gate_up_kernel, len(pieces)), in_specs=[...  15.8 us
    pallas_call x2, Pallas kernels, attend(): pl.pallas_call(functools.partial(attend_kernel, (size + ROPE) ** (-0.5),...  15.3 us
    pallas_call x2, Pallas kernels, project(): pl.pallas_call(functools.partial(project_kernel, blocks, len(gate)), in_s...  11.2 us
    pallas_call x4, Pallas kernels, down(): pl.pallas_call(down_kernel, in_specs=[SMEM, VMEM, VMEM] + [ANY] * len(aft...  7.51 us
    pallas_call x5, Pallas kernels, stack(): pl.pallas_call(functools.partial(stack_kernel, n), in_specs=[ANY] * (n +...  5.12 us
  transfers between devices with their start and end apart: 49, of which 15 were waited for; matrix products, arithmetic and copies ran while one was open for 0% of the time, Pallas kernels for 32%

profile of v4, /device:TPU:0, one launch (start us, length us, event | category | flops | bytes accessed | tf_op | source)
XLA Modules:
  0.0 160.4 jit_solution(10113626879342987535)
XLA Ops:
  0.7 7.7 %shard_map.118.refs_0_ = bf16[32,4096]{1,0:T(8,128)(2,1)S(1)} custom-call(s32[64]{0:T(128)S(1)} %copy-done.3, bf16[64,32,576]{2,1,0:T(8,128)(2,1)} %q_ref.3, bf16[64,576,128]{2,1,0:T(8,128)(2,1)} %bitcast.36, bf16[32,512,128]{2,1,0:T(8,128)(2,1)} %w_hbm.5), custom_call_target="tpu_custom_call" | custom-call | flops 99999997952 | bytes 1024 | tf_op jit(solution)/shard_map/pallas_call | solution.py:445
  8.3 3.0 %collective-permute-start = (bf16[32,4096]{1,0:T(8,128)(2,1)S(1)}, bf16[32,4096]{1,0:T(8,128)(2,1)S(1)}, u32[]{:S(2)}, u32[]{:S(2)}) collective-permute-start(bf16[32,4096]{1,0:T(8,128)(2,1)S(1)} %shard_map.118.refs_0_), channel_id=1, source_target_pairs={{0,4},{4,0},{8,12},{12,8},{1,5},{5,1},{9,13},{13,9},{2,6},{6,2},{1... | collective-permute-start | bytes 786440 | tf_op jit(solution)/shard_map/ppermute | solution.py:31
  12.9 7.7 %shard_map.119.refs_4_.refs_0_ = bf16[32,4096]{1,0:T(8,128)(2,1)S(1)} custom-call(s32[64]{0:T(128)S(1)} %copy-done.3, bf16[64,32,576]{2,1,0:T(8,128)(2,1)} %q_ref.3, bf16[64,576,128]{2,1,0:T(8,128)(2,1)} %bitcast.37, bf16[32,512,128]{2,1,0:T(8,128)(2,1)} %w_hbm.5, bf16[32,4096]{1,0:T(8,128)(2,1)S(1)} %shard_map.118.refs_0_), custom_call_target="tpu_custom_call" | custom-call | flops 99999997952 | bytes 1024 | tf_op jit(solution)/shard_map/pallas_call | solution.py:445
  20.6 4.1 %collective-permute-done.1.refs_2_ = bf16[32,4096]{1,0:T(8,128)(2,1)S(1)} collective-permute-done((bf16[32,4096]{1,0:T(8,128)(2,1)S(1)}, bf16[32,4096]{1,0:T(8,128)(2,1)S(1)}, u32[]{:S(2)}, u32[]{:S(2)}) %collective-permute-start.1) | collective-permute-done | bytes 262176 | tf_op jit(solution)/shard_map/ppermute | solution.py:31
  28.7 5.6 %shard_map.121 = (bf16[64,896]{1,0:T(8,128)(2,1)S(1)}, bf16[64,896]{1,0:T(8,128)(2,1)S(1)}, bf16[64,896]{1,0:T(8,128)(2,1)S(1)}, bf16[64,896]{1,0:T(8,128)(2,1)S(1)}) custom-call(s32[8]{0:T(128)S(1)} %fusion.pos_ref, bf16[4,32,4096]{2,1,0:T(8,128)(2,1)S(1)} %bitcast.23, bf16[4,32,4096]{2,1,0:T(8,128)(2,1)S(1)} %collective-permute-done.3.far_ref, ...), custom_call_target="tpu_custom_call" | custom-call | flops 99999997952 | bytes 1024 | tf_op jit(solution)/shard_map/pallas_call | solution.py:144
  36.0 2.6 %collective-permute-start.5 = (bf16[64,896]{1,0:T(8,128)(2,1)S(1)}, bf16[64,896]{1,0:T(8,128)(2,1)S(1)}, u32[]{:S(2)}, u32[]{:S(2)}) collective-permute-start(bf16[64,896]{1,0:T(8,128)(2,1)S(1)} %get-tuple-element.43), channel_id=1, source_target_pairs={{0,2},{1,3},{2,0},{3,1},{4,6},{5,7},{6,4},{7,5},{8,10},{9,11},{10,... | collective-permute-start | bytes 344072 | tf_op jit(solution)/shard_map/ppermute | solution.py:31
  40.7 6.8 %collective-permute-done.5.refs_2_ = bf16[64,896]{1,0:T(8,128)(2,1)S(1)} collective-permute-done((bf16[64,896]{1,0:T(8,128)(2,1)S(1)}, bf16[64,896]{1,0:T(8,128)(2,1)S(1)}, u32[]{:S(2)}, u32[]{:S(2)}) %collective-permute-start.5) | collective-permute-done | bytes 114720 | tf_op jit(solution)/shard_map/ppermute | solution.py:31
  52.0 5.6 %shard_map.124 = (bf16[80,896]{1,0:T(8,128)(2,1)S(1)}, bf16[80,896]{1,0:T(8,128)(2,1)S(1)}, bf16[80,896]{1,0:T(8,128)(2,1)S(1)}, bf16[80,896]{1,0:T(8,128)(2,1)S(1)}) custom-call(s32[8]{0:T(128)S(1)} %fusion.pos_ref, bf16[4,32,4096]{2,1,0:T(8,128)(2,1)S(1)} %bitcast.25, bf16[4,32,4096]{2,1,0:T(8,128)(2,1)S(1)} %collective-permute-done.13.far_ref, ...), custom_call_target="tpu_custom_call" | custom-call | flops 99999997952 | bytes 1024 | tf_op jit(solution)/shard_map/pallas_call | solution.py:144
  58.6 2.2 %collective-permute-start.22 = (bf16[80,896]{1,0:T(8,128)(2,1)S(1)}, bf16[80,896]{1,0:T(8,128)(2,1)S(1)}, u32[]{:S(2)}, u32[]{:S(2)}) collective-permute-start(bf16[80,896]{1,0:T(8,128)(2,1)S(1)} %get-tuple-element.49), channel_id=1, source_target_pairs={{0,2},{1,3},{2,0},{3,1},{4,6},{5,7},{6,4},{7,5},{8,10},{9,11},{10,... | collective-permute-start | bytes 430088 | tf_op jit(solution)/shard_map/ppermute | solution.py:31
  67.1 4.5 %collective-permute-done.22.refs_2_ = bf16[80,896]{1,0:T(8,128)(2,1)S(1)} collective-permute-done((bf16[80,896]{1,0:T(8,128)(2,1)S(1)}, bf16[80,896]{1,0:T(8,128)(2,1)S(1)}, u32[]{:S(2)}, u32[]{:S(2)}) %collective-permute-start.22) | collective-permute-done | bytes 143392 | tf_op jit(solution)/shard_map/ppermute | solution.py:31
  71.7 2.4 %collective-permute-start.24 = (bf16[64,896]{1,0:T(8,128)(2,1)S(1)}, bf16[64,896]{1,0:T(8,128)(2,1)S(1)}, u32[]{:S(2)}, u32[]{:S(2)}) collective-permute-start(bf16[64,896]{1,0:T(8,128)(2,1)S(1)} %get-tuple-element.53.refs_0_), channel_id=1, source_target_pairs={{0,1},{1,0},{2,3},{3,2},{4,5},{5,4},{6,7},{7,6},{8,9},{9,8},{10,11... | collective-permute-start | bytes 344072 | tf_op jit(solution)/shard_map/ppermute | solution.py:31
  75.3 2.8 %collective-permute-done.24.refs_1_ = bf16[64,896]{1,0:T(8,128)(2,1)S(1)} collective-permute-done((bf16[64,896]{1,0:T(8,128)(2,1)S(1)}, bf16[64,896]{1,0:T(8,128)(2,1)S(1)}, u32[]{:S(2)}, u32[]{:S(2)}) %collective-permute-start.24) | collective-permute-done | bytes 114720 | tf_op jit(solution)/shard_map/ppermute | solution.py:31
  78.0 2.0 %collective-permute-start.26 = (bf16[64,896]{1,0:T(8,128)(2,1)S(1)}, bf16[64,896]{1,0:T(8,128)(2,1)S(1)}, u32[]{:S(2)}, u32[]{:S(2)}) collective-permute-start(bf16[64,896]{1,0:T(8,128)(2,1)S(1)} %get-tuple-element.53.refs_0_), channel_id=1, source_target_pairs={{0,3},{1,2},{2,1},{3,0},{4,7},{5,6},{6,5},{7,4},{8,11},{9,10},{10,... | collective-permute-start | bytes 344072 | tf_op jit(solution)/shard_map/ppermute | solution.py:31
  80.4 4.6 %collective-permute-done.25.refs_2_ = bf16[64,896]{1,0:T(8,128)(2,1)S(1)} collective-permute-done((bf16[64,896]{1,0:T(8,128)(2,1)S(1)}, bf16[64,896]{1,0:T(8,128)(2,1)S(1)}, u32[]{:S(2)}, u32[]{:S(2)}) %collective-permute-start.25) | collective-permute-done | bytes 114720 | tf_op jit(solution)/shard_map/ppermute | solution.py:31
  91.2 8.0 %shard_map.127 = (bf16[256,512]{1,0:T(8,128)(2,1)S(1)}, f32[4,1792]{1,0:T(4,128)S(1)}) custom-call(s32[8]{0:T(128)S(1)} %stack.39.idx_ref, bf16[272,896]{1,0:T(8,128)(2,1)S(1)} %shard_map.125.refs_4_.refs_0_, bf16[272,896]{1,0:T(8,128)(2,1)S(1)} %collective-permute-done.14.refs_1_.refs_4_, bf16[272,896]{1,0:T(8,128)(2,1)S(1)} %collective-permute-done.15.refs_2_.refs_5_, ...), custom_call_target="tpu_custom_call" | custom-call | flops 99999997952 | bytes 1024 | tf_op jit(solution)/shard_map/pallas_call | solution.py:255
  109.6 2.5 %collective-permute-done.34.refs_2_ = bf16[256,896]{1,0:T(8,128)(2,1)} collective-permute-done((bf16[256,896]{1,0:T(8,128)(2,1)}, bf16[256,896]{1,0:T(8,128)(2,1)}, u32[]{:S(2)}, u32[]{:S(2)}) %collective-permute-start.34) | collective-permute-done | bytes 458784 | tf_op jit(solution)/shard_map/ppermute | solution.py:31
  114.1 3.1 %collective-permute-done.35.refs_3_ = bf16[3,256,896]{2,1,0:T(8,128)(2,1)S(1)} collective-permute-done((bf16[3,256,896]{2,1,0:T(8,128)(2,1)S(1)}, bf16[3,256,896]{2,1,0:T(8,128)(2,1)S(1)}, u32[]{:S(2)}, u32[]{:S(2)}) %collective-permute-start.35) | collective-permute-done | bytes 1376288 | tf_op jit(solution)/shard_map/ppermute | solution.py:31
  117.2 7.9 %shard_map.134 = (bf16[256,512]{1,0:T(8,128)(2,1)S(1)}, f32[4,1792]{1,0:T(4,128)}) custom-call(s32[8]{0:T(128)S(1)} %stack.39.idx_ref, bf16[256,896]{1,0:T(8,128)(2,1)} %shard_map.128.refs_0_, bf16[3,256,896]{2,1,0:T(8,128)(2,1)S(1)} %bitcast.33, bf16[256,896]{1,0:T(8,128)(2,1)} %collective-permute-done.27.refs_0_.refs_2_, ...), custom_call_target="tpu_custom_call" | custom-call | flops 99999997952 | bytes 1024 | tf_op jit(solution)/shard_map/pallas_call | solution.py:255
  139.1 3.5 %collective-permute-done.37.refs_5_.refs_2_ = bf16[64,896]{1,0:T(8,128)(2,1)S(1)} collective-permute-done((bf16[64,896]{1,0:T(8,128)(2,1)S(1)}, bf16[64,896]{1,0:T(8,128)(2,1)S(1)}, u32[]{:S(2)}, u32[]{:S(2)}) %collective-permute-start.37) | collective-permute-done | bytes 114720 | tf_op jit(solution)/shard_map/ppermute | solution.py:31
  142.6 2.3 %collective-permute-start.39 = (bf16[64,896]{1,0:T(8,128)(2,1)S(1)}, bf16[64,896]{1,0:T(8,128)(2,1)S(1)}, u32[]{:S(2)}, u32[]{:S(2)}) collective-permute-start(bf16[64,896]{1,0:T(8,128)(2,1)S(1)} %get-tuple-element.64), channel_id=1, source_target_pairs={{0,3},{1,2},{2,1},{3,0},{4,7},{5,6},{6,5},{7,4},{8,11},{9,10},{10,... | collective-permute-start | bytes 344072 | tf_op jit(solution)/shard_map/ppermute | solution.py:31
  144.9 2.2 %collective-permute-start.46 = (bf16[128,896]{1,0:T(8,128)(2,1)S(1)}, bf16[128,896]{1,0:T(8,128)(2,1)S(1)}, u32[]{:S(2)}, u32[]{:S(2)}) collective-permute-start(bf16[128,896]{1,0:T(8,128)(2,1)S(1)} %get-tuple-element.73), channel_id=1, source_target_pairs={{0,8},{4,12},{8,0},{12,4},{1,9},{5,13},{9,1},{13,5},{2,10},{6,14},... | collective-permute-start | bytes 688136 | tf_op jit(solution)/shard_map/ppermute | solution.py:31
  151.7 3.0 %collective-permute-done.46.refs_2_ = bf16[128,896]{1,0:T(8,128)(2,1)S(1)} collective-permute-done((bf16[128,896]{1,0:T(8,128)(2,1)S(1)}, bf16[128,896]{1,0:T(8,128)(2,1)S(1)}, u32[]{:S(2)}, u32[]{:S(2)}) %collective-permute-start.46) | collective-permute-done | bytes 229408 | tf_op jit(solution)/shard_map/ppermute | solution.py:31
  155.4 2.0 %collective-permute-done.43.refs_1_ = bf16[64,896]{1,0:T(8,128)(2,1)S(1)} collective-permute-done((bf16[64,896]{1,0:T(8,128)(2,1)S(1)}, bf16[64,896]{1,0:T(8,128)(2,1)S(1)}, u32[]{:S(2)}, u32[]{:S(2)}) %collective-permute-start.43) | collective-permute-done | bytes 114720 | tf_op jit(solution)/shard_map/ppermute | solution.py:31
  157.5 2.1 %collective-permute-done.48.refs_7_ = bf16[64,896]{1,0:T(8,128)(2,1)S(1)} collective-permute-done((bf16[64,896]{1,0:T(8,128)(2,1)S(1)}, bf16[64,896]{1,0:T(8,128)(2,1)S(1)}, u32[]{:S(2)}, u32[]{:S(2)}) %collective-permute-start.48) | collective-permute-done | bytes 114720 | tf_op jit(solution)/shard_map/ppermute | solution.py:31
  (127 shorter events, 62.0 us)
Async XLA Ops:
  8.3 12.2 %collective-permute-start = (bf16[32,4096]{1,0:T(8,128)(2,1)S(1)}, bf16[32,4096]{1,0:T(8,128)(2,1)S(1)}, u32[]{:S(2)}, u32[]{:S(2)}) collective-permute-start(bf16[32,4096]{1,0:T(8,128)(2,1)S(1)} %shard_map.118.refs_0_), channel_id=1, source_target_pairs={{0,4},{4,0},{8,12},{12,8},{1,5},{5,1},{9,13},{13,9},{2,6},{6,2},{1... | collective-permute-start | bytes 786440 | tf_op jit(solution)/shard_map/ppermute | solution.py:31
  11.3 13.4 %collective-permute-start.1 = (bf16[32,4096]{1,0:T(8,128)(2,1)S(1)}, bf16[32,4096]{1,0:T(8,128)(2,1)S(1)}, u32[]{:S(2)}, u32[]{:S(2)}) collective-permute-start(bf16[32,4096]{1,0:T(8,128)(2,1)S(1)} %shard_map.118.refs_0_), channel_id=1, source_target_pairs={{0,8},{4,12},{8,0},{12,4},{1,9},{5,13},{9,1},{13,5},{2,10},{6,14},... | collective-permute-start | bytes 786440 | tf_op jit(solution)/shard_map/ppermute | solution.py:31
  12.9 11.9 %collective-permute-start.2 = (bf16[32,4096]{1,0:T(8,128)(2,1)S(1)}, bf16[32,4096]{1,0:T(8,128)(2,1)S(1)}, u32[]{:S(2)}, u32[]{:S(2)}) collective-permute-start(bf16[32,4096]{1,0:T(8,128)(2,1)S(1)} %shard_map.118.refs_0_), channel_id=1, source_target_pairs={{0,12},{4,8},{8,4},{12,0},{1,13},{5,9},{9,5},{13,1},{2,14},{6,10},... | collective-permute-start | bytes 786440 | tf_op jit(solution)/shard_map/ppermute | solution.py:31
  25.0 13.6 %collective-permute-start.10 = (bf16[32,4096]{1,0:T(8,128)(2,1)S(1)}, bf16[32,4096]{1,0:T(8,128)(2,1)S(1)}, u32[]{:S(2)}, u32[]{:S(2)}) collective-permute-start(bf16[32,4096]{1,0:T(8,128)(2,1)S(1)} %shard_map.119.refs_4_.refs_0_), channel_id=1, source_target_pairs={{0,4},{4,0},{8,12},{12,8},{1,5},{5,1},{9,13},{13,9},{2,6},{6,2},{1... | collective-permute-start | bytes 786440 | tf_op jit(solution)/shard_map/ppermute | solution.py:31
  26.3 12.5 %collective-permute-start.11 = (bf16[32,4096]{1,0:T(8,128)(2,1)S(1)}, bf16[32,4096]{1,0:T(8,128)(2,1)S(1)}, u32[]{:S(2)}, u32[]{:S(2)}) collective-permute-start(bf16[32,4096]{1,0:T(8,128)(2,1)S(1)} %shard_map.119.refs_4_.refs_0_), channel_id=1, source_target_pairs={{0,8},{4,12},{8,0},{12,4},{1,9},{5,13},{9,1},{13,5},{2,10},{6,14},... | collective-permute-start | bytes 786440 | tf_op jit(solution)/shard_map/ppermute | solution.py:31
  27.2 13.2 %collective-permute-start.12 = (bf16[32,4096]{1,0:T(8,128)(2,1)S(1)}, bf16[32,4096]{1,0:T(8,128)(2,1)S(1)}, u32[]{:S(2)}, u32[]{:S(2)}) collective-permute-start(bf16[32,4096]{1,0:T(8,128)(2,1)S(1)} %shard_map.119.refs_4_.refs_0_), channel_id=1, source_target_pairs={{0,12},{4,8},{8,4},{12,0},{1,13},{5,9},{9,5},{13,1},{2,14},{6,10},... | collective-permute-start | bytes 786440 | tf_op jit(solution)/shard_map/ppermute | solution.py:31
  36.0 11.5 %collective-permute-start.5 = (bf16[64,896]{1,0:T(8,128)(2,1)S(1)}, bf16[64,896]{1,0:T(8,128)(2,1)S(1)}, u32[]{:S(2)}, u32[]{:S(2)}) collective-permute-start(bf16[64,896]{1,0:T(8,128)(2,1)S(1)} %get-tuple-element.43), channel_id=1, source_target_pairs={{0,2},{1,3},{2,0},{3,1},{4,6},{5,7},{6,4},{7,5},{8,10},{9,11},{10,... | collective-permute-start | bytes 344072 | tf_op jit(solution)/shard_map/ppermute | solution.py:31
  40.6 11.5 %collective-permute-start.13 = (bf16[4,32,4096]{2,1,0:T(8,128)(2,1)S(1)}, bf16[4,32,4096]{2,1,0:T(8,128)(2,1)S(1)}, u32[]{:S(2)}, u32[]{:S(2)}) collective-permute-start(bf16[4,32,4096]{2,1,0:T(8,128)(2,1)S(1)} %bitcast.24), channel_id=1, source_target_pairs={{0,16},{16,0},{1,17},{17,1},{2,18},{18,2},{3,19},{19,3},{4,20},{20... | collective-permute-start | bytes 3145736 | tf_op jit(solution)/shard_map/ppermute | solution.py:31
  47.6 13.2 %collective-permute-start.7 = (bf16[64,896]{1,0:T(8,128)(2,1)S(1)}, bf16[64,896]{1,0:T(8,128)(2,1)S(1)}, u32[]{:S(2)}, u32[]{:S(2)}) collective-permute-start(bf16[64,896]{1,0:T(8,128)(2,1)S(1)} %get-tuple-element.46.refs_1_.refs_0_), channel_id=1, source_target_pairs={{0,1},{1,0},{2,3},{3,2},{4,5},{5,4},{6,7},{7,6},{8,9},{9,8},{10,11... | collective-permute-start | bytes 344072 | tf_op jit(solution)/shard_map/ppermute | solution.py:31
  49.4 12.7 %collective-permute-start.8 = (bf16[64,896]{1,0:T(8,128)(2,1)S(1)}, bf16[64,896]{1,0:T(8,128)(2,1)S(1)}, u32[]{:S(2)}, u32[]{:S(2)}) collective-permute-start(bf16[64,896]{1,0:T(8,128)(2,1)S(1)} %get-tuple-element.46.refs_1_.refs_0_), channel_id=1, source_target_pairs={{0,2},{1,3},{2,0},{3,1},{4,6},{5,7},{6,4},{7,5},{8,10},{9,11},{10,... | collective-permute-start | bytes 344072 | tf_op jit(solution)/shard_map/ppermute | solution.py:31
  58.6 12.9 %collective-permute-start.22 = (bf16[80,896]{1,0:T(8,128)(2,1)S(1)}, bf16[80,896]{1,0:T(8,128)(2,1)S(1)}, u32[]{:S(2)}, u32[]{:S(2)}) collective-permute-start(bf16[80,896]{1,0:T(8,128)(2,1)S(1)} %get-tuple-element.49), channel_id=1, source_target_pairs={{0,2},{1,3},{2,0},{3,1},{4,6},{5,7},{6,4},{7,5},{8,10},{9,11},{10,... | collective-permute-start | bytes 430088 | tf_op jit(solution)/shard_map/ppermute | solution.py:31
  63.5 21.5 %collective-permute-start.14 = (bf16[272,896]{1,0:T(8,128)(2,1)S(1)}, bf16[272,896]{1,0:T(8,128)(2,1)S(1)}, u32[]{:S(2)}, u32[]{:S(2)}) collective-permute-start(bf16[272,896]{1,0:T(8,128)(2,1)S(1)} %shard_map.125.refs_4_.refs_0_), channel_id=1, source_target_pairs={{0,4},{4,0},{8,12},{12,8},{1,5},{5,1},{9,13},{13,9},{2,6},{6,2},{1... | collective-permute-start | bytes 1462280 | tf_op jit(solution)/shard_map/ppermute | solution.py:31
  64.8 20.7 %collective-permute-start.15 = (bf16[272,896]{1,0:T(8,128)(2,1)S(1)}, bf16[272,896]{1,0:T(8,128)(2,1)S(1)}, u32[]{:S(2)}, u32[]{:S(2)}) collective-permute-start(bf16[272,896]{1,0:T(8,128)(2,1)S(1)} %shard_map.125.refs_4_.refs_0_), channel_id=1, source_target_pairs={{0,8},{4,12},{8,0},{12,4},{1,9},{5,13},{9,1},{13,5},{2,10},{6,14},... | collective-permute-start | bytes 1462280 | tf_op jit(solution)/shard_map/ppermute | solution.py:31
  65.6 20.0 %collective-permute-start.16 = (bf16[272,896]{1,0:T(8,128)(2,1)S(1)}, bf16[272,896]{1,0:T(8,128)(2,1)S(1)}, u32[]{:S(2)}, u32[]{:S(2)}) collective-permute-start(bf16[272,896]{1,0:T(8,128)(2,1)S(1)} %shard_map.125.refs_4_.refs_0_), channel_id=1, source_target_pairs={{0,12},{4,8},{8,4},{12,0},{1,13},{5,9},{9,5},{13,1},{2,14},{6,10},... | collective-permute-start | bytes 1462280 | tf_op jit(solution)/shard_map/ppermute | solution.py:31
  87.5 13.6 %collective-permute-start.27 = (bf16[256,896]{1,0:T(8,128)(2,1)}, bf16[256,896]{1,0:T(8,128)(2,1)}, u32[]{:S(2)}, u32[]{:S(2)}) collective-permute-start(bf16[256,896]{1,0:T(8,128)(2,1)} %shard_map.128.refs_0_), channel_id=1, source_target_pairs={{0,16},{16,0},{1,17},{17,1},{2,18},{18,2},{3,19},{19,3},{4,20},{20... | collective-permute-start | bytes 1376264 | tf_op jit(solution)/shard_map/ppermute | solution.py:31
  87.6 20.5 %collective-permute-start.32 = (bf16[256,896]{1,0:T(8,128)(2,1)}, bf16[256,896]{1,0:T(8,128)(2,1)}, u32[]{:S(2)}, u32[]{:S(2)}) collective-permute-start(bf16[256,896]{1,0:T(8,128)(2,1)} %shard_map.128.refs_0_), channel_id=1, source_target_pairs={{0,4},{4,0},{8,12},{12,8},{1,5},{5,1},{9,13},{13,9},{2,6},{6,2},{1... | collective-permute-start | bytes 1376264 | tf_op jit(solution)/shard_map/ppermute | solution.py:31
  88.9 20.7 %collective-permute-start.33 = (bf16[256,896]{1,0:T(8,128)(2,1)}, bf16[256,896]{1,0:T(8,128)(2,1)}, u32[]{:S(2)}, u32[]{:S(2)}) collective-permute-start(bf16[256,896]{1,0:T(8,128)(2,1)} %shard_map.128.refs_0_), channel_id=1, source_target_pairs={{0,8},{4,12},{8,0},{12,4},{1,9},{5,13},{9,1},{13,5},{2,10},{6,14},... | collective-permute-start | bytes 1376264 | tf_op jit(solution)/shard_map/ppermute | solution.py:31
  89.7 22.4 %collective-permute-start.34 = (bf16[256,896]{1,0:T(8,128)(2,1)}, bf16[256,896]{1,0:T(8,128)(2,1)}, u32[]{:S(2)}, u32[]{:S(2)}) collective-permute-start(bf16[256,896]{1,0:T(8,128)(2,1)} %shard_map.128.refs_0_), channel_id=1, source_target_pairs={{0,12},{4,8},{8,4},{12,0},{1,13},{5,9},{9,5},{13,1},{2,14},{6,10},... | collective-permute-start | bytes 1376264 | tf_op jit(solution)/shard_map/ppermute | solution.py:31
  106.1 27.4 %collective-permute-start.29 = (bf16[256,896]{1,0:T(8,128)(2,1)}, bf16[256,896]{1,0:T(8,128)(2,1)}, u32[]{:S(2)}, u32[]{:S(2)}) collective-permute-start(bf16[256,896]{1,0:T(8,128)(2,1)} %get-tuple-element.55.refs_3_), channel_id=1, source_target_pairs={{0,4},{4,0},{8,12},{12,8},{1,5},{5,1},{9,13},{13,9},{2,6},{6,2},{1... | collective-permute-start | bytes 1376264 | tf_op jit(solution)/shard_map/ppermute | solution.py:31
  107.3 27.4 %collective-permute-start.30 = (bf16[256,896]{1,0:T(8,128)(2,1)}, bf16[256,896]{1,0:T(8,128)(2,1)}, u32[]{:S(2)}, u32[]{:S(2)}) collective-permute-start(bf16[256,896]{1,0:T(8,128)(2,1)} %get-tuple-element.56.refs_4_), channel_id=1, source_target_pairs={{0,8},{4,12},{8,0},{12,4},{1,9},{5,13},{9,1},{13,5},{2,10},{6,14},... | collective-permute-start | bytes 1376264 | tf_op jit(solution)/shard_map/ppermute | solution.py:31
  108.1 26.6 %collective-permute-start.31 = (bf16[256,896]{1,0:T(8,128)(2,1)}, bf16[256,896]{1,0:T(8,128)(2,1)}, u32[]{:S(2)}, u32[]{:S(2)}) collective-permute-start(bf16[256,896]{1,0:T(8,128)(2,1)} %get-tuple-element.57.refs_5_), channel_id=1, source_target_pairs={{0,12},{4,8},{8,4},{12,0},{1,13},{5,9},{9,5},{13,1},{2,14},{6,10},... | collective-permute-start | bytes 1376264 | tf_op jit(solution)/shard_map/ppermute | solution.py:31
  131.2 13.7 %collective-permute-start.40 = (bf16[128,896]{1,0:T(8,128)(2,1)S(1)}, bf16[128,896]{1,0:T(8,128)(2,1)S(1)}, u32[]{:S(2)}, u32[]{:S(2)}) collective-permute-start(bf16[128,896]{1,0:T(8,128)(2,1)S(1)} %get-tuple-element.67), channel_id=1, source_target_pairs={{0,4},{4,0},{8,12},{12,8},{1,5},{5,1},{9,13},{13,9},{2,6},{6,2},{1... | collective-permute-start | bytes 688136 | tf_op jit(solution)/shard_map/ppermute | solution.py:31
  131.8 13.1 %collective-permute-start.41 = (bf16[128,896]{1,0:T(8,128)(2,1)S(1)}, bf16[128,896]{1,0:T(8,128)(2,1)S(1)}, u32[]{:S(2)}, u32[]{:S(2)}) collective-permute-start(bf16[128,896]{1,0:T(8,128)(2,1)S(1)} %get-tuple-element.68), channel_id=1, source_target_pairs={{0,8},{4,12},{8,0},{12,4},{1,9},{5,13},{9,1},{13,5},{2,10},{6,14},... | collective-permute-start | bytes 688136 | tf_op jit(solution)/shard_map/ppermute | solution.py:31
  133.5 13.6 %collective-permute-start.42 = (bf16[128,896]{1,0:T(8,128)(2,1)S(1)}, bf16[128,896]{1,0:T(8,128)(2,1)S(1)}, u32[]{:S(2)}, u32[]{:S(2)}) collective-permute-start(bf16[128,896]{1,0:T(8,128)(2,1)S(1)} %get-tuple-element.69), channel_id=1, source_target_pairs={{0,12},{4,8},{8,4},{12,0},{1,13},{5,9},{9,5},{13,1},{2,14},{6,10},... | collective-permute-start | bytes 688136 | tf_op jit(solution)/shard_map/ppermute | solution.py:31
  (33 other events, 241.3 us)

commit v5 on v4

--- a/solution.py
+++ b/solution.py
@@ -310,7 +310,8 @@
     )(owners, act, w_down, *after)
 
 
-def combine_kernel(n, parts, near_ref, got_ref, *outs):
+def combine_kernel(n, parts, near_ref, got_ref, *refs):
+    outs = refs[-n * parts :]
     size = near_ref.shape[1] // parts
     for p in range(parts):
         at = slice(p * size, (p + 1) * size)
@@ -319,11 +320,11 @@
             outs[p * n + d][...] = both.astype(outs[p * n + d].dtype)
 
 
-def combine(near, got, parts):
+def combine(near, got, parts, after):
     n, rows, width = near.shape
     outs = pl.pallas_call(
         functools.partial(combine_kernel, n, parts),
-        in_specs=[VMEM] * 2,
+        in_specs=[VMEM] * 2 + [ANY] * len(after),
         out_specs=[VMEM] * (n * parts),
         out_shape=[
             jax.ShapeDtypeStruct((rows // parts, width), jnp.bfloat16 if d else jnp.float32)
@@ -332,7 +333,7 @@
         * parts,
         compiler_params=pltpu.CompilerParams(vmem_limit_bytes=12 * MIB),
         cost_estimate=HEAVY,
-    )(near, got)
+    )(near, got, *after)
     return [outs[p * n : (p + 1) * n] for p in range(parts)]
 
 
@@ -347,7 +348,7 @@
         outs[b][...] = total.astype(outs[b].dtype)
 
 
-def reduce(pieces, blocks, own, after):
+def reduce(pieces, blocks, own, after, estimate=HEAVY):
     n = len(pieces)
     rows, width = pieces[0].shape
     return pl.pallas_call(
@@ -359,7 +360,7 @@
             for b in range(blocks)
         ],
         compiler_params=pltpu.CompilerParams(vmem_limit_bytes=8 * MIB),
-        cost_estimate=HEAVY,
+        cost_estimate=estimate,
     )(*pieces, *after)
 
 
@@ -518,11 +519,11 @@
     def other_core(x):
         return swap(x, "side", 2, 1)
 
-    def experts(pieces, held, inverse_gain, parts, after):
+    def experts(pieces, held, inverse_gain, after):
         act, inverse_gain = gate_up(pieces, owners, gate_dev, up_dev, held, inverse_gain)
         far_rows = down(act, owners[n_row:], down_dev, width, [])
         near_rows = down(act, owners[:n_row], down_dev, width, after)
-        return combine(near_rows, other_core(far_rows), parts), inverse_gain
+        return near_rows, other_core(far_rows), inverse_gain
 
     def stack_rows(x, after, estimate=HEAVY):
         return stack(over_row([x] * n_row), after, estimate).reshape(n_row, *x.shape)
@@ -543,12 +544,14 @@
     no_gain = jnp.zeros((2 * n_row, width), jnp.float32)
     rows_1 = stack(over_col([scaled_1] * n_col), near_0[1:])
     far_own = other_core(rows_1)
-    [both_0], inverse_gain = experts(near_0 + far_0, weight[0], no_gain, 1, [far_own])
+    near_rows, got, inverse_gain = experts(near_0 + far_0, weight[0], no_gain, [far_own])
+    [both_0] = combine(near_rows, got, 1, [])
     near_1 = stack(over_row([rows_1] * n_row)[1:], both_0[1:])
     near_1 = near_1.reshape(n_row - 1, *rows_1.shape)
     pieces = [rows_1, near_1, far_own, other_core(near_1)]
-    both_1, _ = experts(pieces, hand_on(weight[1], [near_1]), inverse_gain, 2, [])
-    total_0 = reduce(over_row(both_0), n_col, True, both_1[0][:1])
+    near_rows, got, _ = experts(pieces, hand_on(weight[1], [near_1]), inverse_gain, [])
+    total_0 = reduce(over_row(both_0), n_col, True, [near_rows], LIGHT)
+    both_1 = combine(near_rows, got, 2, total_0[:1])
     terms_0 = [hidden_0, *over_col(total_0)]
     half = n_col // 2
     far_1 = reduce(over_row(both_1[1]), half, False, total_0[:1])

time: 161 us -> 162 us (level)
  starting transfers between devices: 54.4 us -> 56.6 us
    ppermute x49, starting transfers between devices: 54.4 us -> 56.6 us  [swap(): return lax.ppermute(x, axis, [(i, i ^ d) for i in range(count)])]
  transfers between devices with their start and end apart: 49 -> 49, of which waited for: 15 -> 15; matrix products, arithmetic and copies ran while one was open for 0% -> 0% of each run, Pallas kernels for 32% -> 31%
where the time goes in v5:
time: 162 us
  Pallas kernels  59.6 us (37%)
  starting transfers between devices  56.6 us (35%)
  waiting for transfers between devices  44.1 us (27%)
    ppermute x49, starting transfers between devices, swap(): return lax.ppermute(x, axis, [(i, i ^ d) for i in range(count)])  56.6 us
    ppermute x49, waiting for transfers between devices, swap(): return lax.ppermute(x, axis, [(i, i ^ d) for i in range(count)])  44.1 us
    pallas_call x2, Pallas kernels, gate_up(): pl.pallas_call(functools.partial(gate_up_kernel, len(pieces)), in_specs=[...  16 us
    pallas_call x2, Pallas kernels, attend(): pl.pallas_call(functools.partial(attend_kernel, (size + ROPE) ** (-0.5),...  15.3 us
    pallas_call x2, Pallas kernels, project(): pl.pallas_call(functools.partial(project_kernel, blocks, len(gate)), in_s...  11.2 us
    pallas_call x4, Pallas kernels, down(): pl.pallas_call(down_kernel, in_specs=[SMEM, VMEM, VMEM] + [ANY] * len(aft...  7.51 us
    pallas_call x5, Pallas kernels, stack(): pl.pallas_call(functools.partial(stack_kernel, n), in_specs=[ANY] * (n +...  5.13 us
  transfers between devices with their start and end apart: 49, of which 15 were waited for; matrix products, arithmetic and copies ran while one was open for 0% of the time, Pallas kernels for 31%

profile of v5, /device:TPU:0, one launch (start us, length us, event | category | flops | bytes accessed | tf_op | source)
XLA Modules:
  0.0 162.0 jit_solution(12083491492637411286)
XLA Ops:
  0.7 7.7 %shard_map.118.refs_0_ = bf16[32,4096]{1,0:T(8,128)(2,1)S(1)} custom-call(s32[64]{0:T(128)S(1)} %copy-done.4, bf16[64,32,576]{2,1,0:T(8,128)(2,1)} %q_ref.3, bf16[64,576,128]{2,1,0:T(8,128)(2,1)} %bitcast.36, bf16[32,512,128]{2,1,0:T(8,128)(2,1)} %w_hbm.5), custom_call_target="tpu_custom_call" | custom-call | flops 99999997952 | bytes 1024 | tf_op jit(solution)/shard_map/pallas_call | solution.py:446
  8.3 3.0 %collective-permute-start = (bf16[32,4096]{1,0:T(8,128)(2,1)S(1)}, bf16[32,4096]{1,0:T(8,128)(2,1)S(1)}, u32[]{:S(2)}, u32[]{:S(2)}) collective-permute-start(bf16[32,4096]{1,0:T(8,128)(2,1)S(1)} %shard_map.118.refs_0_), channel_id=1, source_target_pairs={{0,4},{4,0},{8,12},{12,8},{1,5},{5,1},{9,13},{13,9},{2,6},{6,2},{1... | collective-permute-start | bytes 786440 | tf_op jit(solution)/shard_map/ppermute | solution.py:31
  12.9 7.7 %shard_map.119.refs_4_.refs_0_ = bf16[32,4096]{1,0:T(8,128)(2,1)S(1)} custom-call(s32[64]{0:T(128)S(1)} %copy-done.4, bf16[64,32,576]{2,1,0:T(8,128)(2,1)} %q_ref.3, bf16[64,576,128]{2,1,0:T(8,128)(2,1)} %bitcast.37, bf16[32,512,128]{2,1,0:T(8,128)(2,1)} %w_hbm.5, bf16[32,4096]{1,0:T(8,128)(2,1)S(1)} %shard_map.118.refs_0_), custom_call_target="tpu_custom_call" | custom-call | flops 99999997952 | bytes 1024 | tf_op jit(solution)/shard_map/pallas_call | solution.py:446
  20.6 4.1 %collective-permute-done.1.refs_2_ = bf16[32,4096]{1,0:T(8,128)(2,1)S(1)} collective-permute-done((bf16[32,4096]{1,0:T(8,128)(2,1)S(1)}, bf16[32,4096]{1,0:T(8,128)(2,1)S(1)}, u32[]{:S(2)}, u32[]{:S(2)}) %collective-permute-start.1) | collective-permute-done | bytes 262176 | tf_op jit(solution)/shard_map/ppermute | solution.py:31
  28.7 5.6 %shard_map.121 = (bf16[64,896]{1,0:T(8,128)(2,1)S(1)}, bf16[64,896]{1,0:T(8,128)(2,1)S(1)}, bf16[64,896]{1,0:T(8,128)(2,1)S(1)}, bf16[64,896]{1,0:T(8,128)(2,1)S(1)}) custom-call(s32[8]{0:T(128)S(1)} %fusion.pos_ref, bf16[4,32,4096]{2,1,0:T(8,128)(2,1)S(1)} %bitcast.23, bf16[4,32,4096]{2,1,0:T(8,128)(2,1)S(1)} %collective-permute-done.3.far_ref, ...), custom_call_target="tpu_custom_call" | custom-call | flops 99999997952 | bytes 1024 | tf_op jit(solution)/shard_map/pallas_call | solution.py:144
  36.0 2.6 %collective-permute-start.5 = (bf16[64,896]{1,0:T(8,128)(2,1)S(1)}, bf16[64,896]{1,0:T(8,128)(2,1)S(1)}, u32[]{:S(2)}, u32[]{:S(2)}) collective-permute-start(bf16[64,896]{1,0:T(8,128)(2,1)S(1)} %get-tuple-element.43), channel_id=1, source_target_pairs={{0,2},{1,3},{2,0},{3,1},{4,6},{5,7},{6,4},{7,5},{8,10},{9,11},{10,... | collective-permute-start | bytes 344072 | tf_op jit(solution)/shard_map/ppermute | solution.py:31
  40.7 6.8 %collective-permute-done.5.refs_2_ = bf16[64,896]{1,0:T(8,128)(2,1)S(1)} collective-permute-done((bf16[64,896]{1,0:T(8,128)(2,1)S(1)}, bf16[64,896]{1,0:T(8,128)(2,1)S(1)}, u32[]{:S(2)}, u32[]{:S(2)}) %collective-permute-start.5) | collective-permute-done | bytes 114720 | tf_op jit(solution)/shard_map/ppermute | solution.py:31
  52.0 5.6 %shard_map.124 = (bf16[80,896]{1,0:T(8,128)(2,1)S(1)}, bf16[80,896]{1,0:T(8,128)(2,1)S(1)}, bf16[80,896]{1,0:T(8,128)(2,1)S(1)}, bf16[80,896]{1,0:T(8,128)(2,1)S(1)}) custom-call(s32[8]{0:T(128)S(1)} %fusion.pos_ref, bf16[4,32,4096]{2,1,0:T(8,128)(2,1)S(1)} %bitcast.25, bf16[4,32,4096]{2,1,0:T(8,128)(2,1)S(1)} %collective-permute-done.13.far_ref, ...), custom_call_target="tpu_custom_call" | custom-call | flops 99999997952 | bytes 1024 | tf_op jit(solution)/shard_map/pallas_call | solution.py:144
  58.6 2.2 %collective-permute-start.22 = (bf16[80,896]{1,0:T(8,128)(2,1)S(1)}, bf16[80,896]{1,0:T(8,128)(2,1)S(1)}, u32[]{:S(2)}, u32[]{:S(2)}) collective-permute-start(bf16[80,896]{1,0:T(8,128)(2,1)S(1)} %get-tuple-element.49), channel_id=1, source_target_pairs={{0,2},{1,3},{2,0},{3,1},{4,6},{5,7},{6,4},{7,5},{8,10},{9,11},{10,... | collective-permute-start | bytes 430088 | tf_op jit(solution)/shard_map/ppermute | solution.py:31
  67.1 4.5 %collective-permute-done.22.refs_2_ = bf16[80,896]{1,0:T(8,128)(2,1)S(1)} collective-permute-done((bf16[80,896]{1,0:T(8,128)(2,1)S(1)}, bf16[80,896]{1,0:T(8,128)(2,1)S(1)}, u32[]{:S(2)}, u32[]{:S(2)}) %collective-permute-start.22) | collective-permute-done | bytes 143392 | tf_op jit(solution)/shard_map/ppermute | solution.py:31
  71.7 2.4 %collective-permute-start.24 = (bf16[64,896]{1,0:T(8,128)(2,1)S(1)}, bf16[64,896]{1,0:T(8,128)(2,1)S(1)}, u32[]{:S(2)}, u32[]{:S(2)}) collective-permute-start(bf16[64,896]{1,0:T(8,128)(2,1)S(1)} %get-tuple-element.53.refs_0_), channel_id=1, source_target_pairs={{0,1},{1,0},{2,3},{3,2},{4,5},{5,4},{6,7},{7,6},{8,9},{9,8},{10,11... | collective-permute-start | bytes 344072 | tf_op jit(solution)/shard_map/ppermute | solution.py:31
  75.3 2.8 %collective-permute-done.24.refs_1_ = bf16[64,896]{1,0:T(8,128)(2,1)S(1)} collective-permute-done((bf16[64,896]{1,0:T(8,128)(2,1)S(1)}, bf16[64,896]{1,0:T(8,128)(2,1)S(1)}, u32[]{:S(2)}, u32[]{:S(2)}) %collective-permute-start.24) | collective-permute-done | bytes 114720 | tf_op jit(solution)/shard_map/ppermute | solution.py:31
  78.0 2.0 %collective-permute-start.26 = (bf16[64,896]{1,0:T(8,128)(2,1)S(1)}, bf16[64,896]{1,0:T(8,128)(2,1)S(1)}, u32[]{:S(2)}, u32[]{:S(2)}) collective-permute-start(bf16[64,896]{1,0:T(8,128)(2,1)S(1)} %get-tuple-element.53.refs_0_), channel_id=1, source_target_pairs={{0,3},{1,2},{2,1},{3,0},{4,7},{5,6},{6,5},{7,4},{8,11},{9,10},{10,... | collective-permute-start | bytes 344072 | tf_op jit(solution)/shard_map/ppermute | solution.py:31
  80.4 4.6 %collective-permute-done.25.refs_2_ = bf16[64,896]{1,0:T(8,128)(2,1)S(1)} collective-permute-done((bf16[64,896]{1,0:T(8,128)(2,1)S(1)}, bf16[64,896]{1,0:T(8,128)(2,1)S(1)}, u32[]{:S(2)}, u32[]{:S(2)}) %collective-permute-start.25) | collective-permute-done | bytes 114720 | tf_op jit(solution)/shard_map/ppermute | solution.py:31
  91.2 8.0 %shard_map.127 = (bf16[256,512]{1,0:T(8,128)(2,1)S(1)}, f32[4,1792]{1,0:T(4,128)S(1)}) custom-call(s32[8]{0:T(128)S(1)} %stack.39.idx_ref, bf16[272,896]{1,0:T(8,128)(2,1)S(1)} %shard_map.125.refs_4_.refs_0_, bf16[272,896]{1,0:T(8,128)(2,1)S(1)} %collective-permute-done.14.refs_1_.refs_4_, bf16[272,896]{1,0:T(8,128)(2,1)S(1)} %collective-permute-done.15.refs_2_.refs_5_, ...), custom_call_target="tpu_custom_call" | custom-call | flops 99999997952 | bytes 1024 | tf_op jit(solution)/shard_map/pallas_call | solution.py:255
  109.6 2.5 %collective-permute-done.34.refs_2_ = bf16[256,896]{1,0:T(8,128)(2,1)} collective-permute-done((bf16[256,896]{1,0:T(8,128)(2,1)}, bf16[256,896]{1,0:T(8,128)(2,1)}, u32[]{:S(2)}, u32[]{:S(2)}) %collective-permute-start.34) | collective-permute-done | bytes 458784 | tf_op jit(solution)/shard_map/ppermute | solution.py:31
  114.1 3.1 %collective-permute-done.35.refs_3_ = bf16[3,256,896]{2,1,0:T(8,128)(2,1)S(1)} collective-permute-done((bf16[3,256,896]{2,1,0:T(8,128)(2,1)S(1)}, bf16[3,256,896]{2,1,0:T(8,128)(2,1)S(1)}, u32[]{:S(2)}, u32[]{:S(2)}) %collective-permute-start.35) | collective-permute-done | bytes 1376288 | tf_op jit(solution)/shard_map/ppermute | solution.py:31
  117.2 8.1 %shard_map.134 = (bf16[256,512]{1,0:T(8,128)(2,1)S(1)}, f32[4,1792]{1,0:T(4,128)}) custom-call(s32[8]{0:T(128)S(1)} %stack.39.idx_ref, bf16[256,896]{1,0:T(8,128)(2,1)} %shard_map.128.refs_0_, bf16[3,256,896]{2,1,0:T(8,128)(2,1)S(1)} %bitcast.33, bf16[256,896]{1,0:T(8,128)(2,1)} %collective-permute-done.27.refs_0_.refs_2_, ...), custom_call_target="tpu_custom_call" | custom-call | flops 99999997952 | bytes 1024 | tf_op jit(solution)/shard_map/pallas_call | solution.py:255
  129.2 2.1 %collective-permute-done.31.refs_3_ = bf16[256,896]{1,0:T(8,128)(2,1)} collective-permute-done((bf16[256,896]{1,0:T(8,128)(2,1)}, bf16[256,896]{1,0:T(8,128)(2,1)}, u32[]{:S(2)}, u32[]{:S(2)}) %collective-permute-start.31) | collective-permute-done | bytes 458784 | tf_op jit(solution)/shard_map/ppermute | solution.py:31
  139.6 2.5 %collective-permute-done.36.refs_5_.refs_2_ = bf16[64,896]{1,0:T(8,128)(2,1)S(1)} collective-permute-done((bf16[64,896]{1,0:T(8,128)(2,1)S(1)}, bf16[64,896]{1,0:T(8,128)(2,1)S(1)}, u32[]{:S(2)}, u32[]{:S(2)}) %collective-permute-start.36) | collective-permute-done | bytes 114720 | tf_op jit(solution)/shard_map/ppermute | solution.py:31
  142.1 2.4 %collective-permute-start.38 = (bf16[64,896]{1,0:T(8,128)(2,1)S(1)}, bf16[64,896]{1,0:T(8,128)(2,1)S(1)}, u32[]{:S(2)}, u32[]{:S(2)}) collective-permute-start(bf16[64,896]{1,0:T(8,128)(2,1)S(1)} %get-tuple-element.63), channel_id=1, source_target_pairs={{0,3},{1,2},{2,1},{3,0},{4,7},{5,6},{6,5},{7,4},{8,11},{9,10},{10,... | collective-permute-start | bytes 344072 | tf_op jit(solution)/shard_map/ppermute | solution.py:31
  148.5 2.4 %collective-permute-start.43 = (bf16[64,896]{1,0:T(8,128)(2,1)S(1)}, bf16[64,896]{1,0:T(8,128)(2,1)S(1)}, u32[]{:S(2)}, u32[]{:S(2)}) collective-permute-start(bf16[64,896]{1,0:T(8,128)(2,1)S(1)} %get-tuple-element.69.refs_4_), channel_id=1, source_target_pairs={{0,2},{1,3},{2,0},{3,1},{4,6},{5,7},{6,4},{7,5},{8,10},{9,11},{10,... | collective-permute-start | bytes 344072 | tf_op jit(solution)/shard_map/ppermute | solution.py:31
  152.8 3.5 %collective-permute-done.46.refs_2_ = bf16[128,896]{1,0:T(8,128)(2,1)S(1)} collective-permute-done((bf16[128,896]{1,0:T(8,128)(2,1)S(1)}, bf16[128,896]{1,0:T(8,128)(2,1)S(1)}, u32[]{:S(2)}, u32[]{:S(2)}) %collective-permute-start.46) | collective-permute-done | bytes 229408 | tf_op jit(solution)/shard_map/ppermute | solution.py:31
  158.4 2.8 %collective-permute-done.48.refs_7_ = bf16[64,896]{1,0:T(8,128)(2,1)S(1)} collective-permute-done((bf16[64,896]{1,0:T(8,128)(2,1)S(1)}, bf16[64,896]{1,0:T(8,128)(2,1)S(1)}, u32[]{:S(2)}, u32[]{:S(2)}) %collective-permute-start.48) | collective-permute-done | bytes 114720 | tf_op jit(solution)/shard_map/ppermute | solution.py:31
  (129 shorter events, 62.9 us)
Async XLA Ops:
  8.3 12.2 %collective-permute-start = (bf16[32,4096]{1,0:T(8,128)(2,1)S(1)}, bf16[32,4096]{1,0:T(8,128)(2,1)S(1)}, u32[]{:S(2)}, u32[]{:S(2)}) collective-permute-start(bf16[32,4096]{1,0:T(8,128)(2,1)S(1)} %shard_map.118.refs_0_), channel_id=1, source_target_pairs={{0,4},{4,0},{8,12},{12,8},{1,5},{5,1},{9,13},{13,9},{2,6},{6,2},{1... | collective-permute-start | bytes 786440 | tf_op jit(solution)/shard_map/ppermute | solution.py:31
  11.3 13.4 %collective-permute-start.1 = (bf16[32,4096]{1,0:T(8,128)(2,1)S(1)}, bf16[32,4096]{1,0:T(8,128)(2,1)S(1)}, u32[]{:S(2)}, u32[]{:S(2)}) collective-permute-start(bf16[32,4096]{1,0:T(8,128)(2,1)S(1)} %shard_map.118.refs_0_), channel_id=1, source_target_pairs={{0,8},{4,12},{8,0},{12,4},{1,9},{5,13},{9,1},{13,5},{2,10},{6,14},... | collective-permute-start | bytes 786440 | tf_op jit(solution)/shard_map/ppermute | solution.py:31
  12.9 11.9 %collective-permute-start.2 = (bf16[32,4096]{1,0:T(8,128)(2,1)S(1)}, bf16[32,4096]{1,0:T(8,128)(2,1)S(1)}, u32[]{:S(2)}, u32[]{:S(2)}) collective-permute-start(bf16[32,4096]{1,0:T(8,128)(2,1)S(1)} %shard_map.118.refs_0_), channel_id=1, source_target_pairs={{0,12},{4,8},{8,4},{12,0},{1,13},{5,9},{9,5},{13,1},{2,14},{6,10},... | collective-permute-start | bytes 786440 | tf_op jit(solution)/shard_map/ppermute | solution.py:31
  25.0 13.6 %collective-permute-start.10 = (bf16[32,4096]{1,0:T(8,128)(2,1)S(1)}, bf16[32,4096]{1,0:T(8,128)(2,1)S(1)}, u32[]{:S(2)}, u32[]{:S(2)}) collective-permute-start(bf16[32,4096]{1,0:T(8,128)(2,1)S(1)} %shard_map.119.refs_4_.refs_0_), channel_id=1, source_target_pairs={{0,4},{4,0},{8,12},{12,8},{1,5},{5,1},{9,13},{13,9},{2,6},{6,2},{1... | collective-permute-start | bytes 786440 | tf_op jit(solution)/shard_map/ppermute | solution.py:31
  26.3 12.5 %collective-permute-start.11 = (bf16[32,4096]{1,0:T(8,128)(2,1)S(1)}, bf16[32,4096]{1,0:T(8,128)(2,1)S(1)}, u32[]{:S(2)}, u32[]{:S(2)}) collective-permute-start(bf16[32,4096]{1,0:T(8,128)(2,1)S(1)} %shard_map.119.refs_4_.refs_0_), channel_id=1, source_target_pairs={{0,8},{4,12},{8,0},{12,4},{1,9},{5,13},{9,1},{13,5},{2,10},{6,14},... | collective-permute-start | bytes 786440 | tf_op jit(solution)/shard_map/ppermute | solution.py:31
  27.2 13.2 %collective-permute-start.12 = (bf16[32,4096]{1,0:T(8,128)(2,1)S(1)}, bf16[32,4096]{1,0:T(8,128)(2,1)S(1)}, u32[]{:S(2)}, u32[]{:S(2)}) collective-permute-start(bf16[32,4096]{1,0:T(8,128)(2,1)S(1)} %shard_map.119.refs_4_.refs_0_), channel_id=1, source_target_pairs={{0,12},{4,8},{8,4},{12,0},{1,13},{5,9},{9,5},{13,1},{2,14},{6,10},... | collective-permute-start | bytes 786440 | tf_op jit(solution)/shard_map/ppermute | solution.py:31
  36.0 11.5 %collective-permute-start.5 = (bf16[64,896]{1,0:T(8,128)(2,1)S(1)}, bf16[64,896]{1,0:T(8,128)(2,1)S(1)}, u32[]{:S(2)}, u32[]{:S(2)}) collective-permute-start(bf16[64,896]{1,0:T(8,128)(2,1)S(1)} %get-tuple-element.43), channel_id=1, source_target_pairs={{0,2},{1,3},{2,0},{3,1},{4,6},{5,7},{6,4},{7,5},{8,10},{9,11},{10,... | collective-permute-start | bytes 344072 | tf_op jit(solution)/shard_map/ppermute | solution.py:31
  40.6 11.5 %collective-permute-start.13 = (bf16[4,32,4096]{2,1,0:T(8,128)(2,1)S(1)}, bf16[4,32,4096]{2,1,0:T(8,128)(2,1)S(1)}, u32[]{:S(2)}, u32[]{:S(2)}) collective-permute-start(bf16[4,32,4096]{2,1,0:T(8,128)(2,1)S(1)} %bitcast.24), channel_id=1, source_target_pairs={{0,16},{16,0},{1,17},{17,1},{2,18},{18,2},{3,19},{19,3},{4,20},{20... | collective-permute-start | bytes 3145736 | tf_op jit(solution)/shard_map/ppermute | solution.py:31
  47.6 13.2 %collective-permute-start.7 = (bf16[64,896]{1,0:T(8,128)(2,1)S(1)}, bf16[64,896]{1,0:T(8,128)(2,1)S(1)}, u32[]{:S(2)}, u32[]{:S(2)}) collective-permute-start(bf16[64,896]{1,0:T(8,128)(2,1)S(1)} %get-tuple-element.46.refs_1_.refs_0_), channel_id=1, source_target_pairs={{0,1},{1,0},{2,3},{3,2},{4,5},{5,4},{6,7},{7,6},{8,9},{9,8},{10,11... | collective-permute-start | bytes 344072 | tf_op jit(solution)/shard_map/ppermute | solution.py:31
  49.4 12.7 %collective-permute-start.8 = (bf16[64,896]{1,0:T(8,128)(2,1)S(1)}, bf16[64,896]{1,0:T(8,128)(2,1)S(1)}, u32[]{:S(2)}, u32[]{:S(2)}) collective-permute-start(bf16[64,896]{1,0:T(8,128)(2,1)S(1)} %get-tuple-element.46.refs_1_.refs_0_), channel_id=1, source_target_pairs={{0,2},{1,3},{2,0},{3,1},{4,6},{5,7},{6,4},{7,5},{8,10},{9,11},{10,... | collective-permute-start | bytes 344072 | tf_op jit(solution)/shard_map/ppermute | solution.py:31
  50.7 11.4 %collective-permute-start.9 = (bf16[64,896]{1,0:T(8,128)(2,1)S(1)}, bf16[64,896]{1,0:T(8,128)(2,1)S(1)}, u32[]{:S(2)}, u32[]{:S(2)}) collective-permute-start(bf16[64,896]{1,0:T(8,128)(2,1)S(1)} %get-tuple-element.46.refs_1_.refs_0_), channel_id=1, source_target_pairs={{0,3},{1,2},{2,1},{3,0},{4,7},{5,6},{6,5},{7,4},{8,11},{9,10},{10,... | collective-permute-start | bytes 344072 | tf_op jit(solution)/shard_map/ppermute | solution.py:31
  58.6 12.9 %collective-permute-start.22 = (bf16[80,896]{1,0:T(8,128)(2,1)S(1)}, bf16[80,896]{1,0:T(8,128)(2,1)S(1)}, u32[]{:S(2)}, u32[]{:S(2)}) collective-permute-start(bf16[80,896]{1,0:T(8,128)(2,1)S(1)} %get-tuple-element.49), channel_id=1, source_target_pairs={{0,2},{1,3},{2,0},{3,1},{4,6},{5,7},{6,4},{7,5},{8,10},{9,11},{10,... | collective-permute-start | bytes 430088 | tf_op jit(solution)/shard_map/ppermute | solution.py:31
  63.5 21.5 %collective-permute-start.14 = (bf16[272,896]{1,0:T(8,128)(2,1)S(1)}, bf16[272,896]{1,0:T(8,128)(2,1)S(1)}, u32[]{:S(2)}, u32[]{:S(2)}) collective-permute-start(bf16[272,896]{1,0:T(8,128)(2,1)S(1)} %shard_map.125.refs_4_.refs_0_), channel_id=1, source_target_pairs={{0,4},{4,0},{8,12},{12,8},{1,5},{5,1},{9,13},{13,9},{2,6},{6,2},{1... | collective-permute-start | bytes 1462280 | tf_op jit(solution)/shard_map/ppermute | solution.py:31
  64.8 20.7 %collective-permute-start.15 = (bf16[272,896]{1,0:T(8,128)(2,1)S(1)}, bf16[272,896]{1,0:T(8,128)(2,1)S(1)}, u32[]{:S(2)}, u32[]{:S(2)}) collective-permute-start(bf16[272,896]{1,0:T(8,128)(2,1)S(1)} %shard_map.125.refs_4_.refs_0_), channel_id=1, source_target_pairs={{0,8},{4,12},{8,0},{12,4},{1,9},{5,13},{9,1},{13,5},{2,10},{6,14},... | collective-permute-start | bytes 1462280 | tf_op jit(solution)/shard_map/ppermute | solution.py:31
  65.6 20.0 %collective-permute-start.16 = (bf16[272,896]{1,0:T(8,128)(2,1)S(1)}, bf16[272,896]{1,0:T(8,128)(2,1)S(1)}, u32[]{:S(2)}, u32[]{:S(2)}) collective-permute-start(bf16[272,896]{1,0:T(8,128)(2,1)S(1)} %shard_map.125.refs_4_.refs_0_), channel_id=1, source_target_pairs={{0,12},{4,8},{8,4},{12,0},{1,13},{5,9},{9,5},{13,1},{2,14},{6,10},... | collective-permute-start | bytes 1462280 | tf_op jit(solution)/shard_map/ppermute | solution.py:31
  87.5 13.6 %collective-permute-start.27 = (bf16[256,896]{1,0:T(8,128)(2,1)}, bf16[256,896]{1,0:T(8,128)(2,1)}, u32[]{:S(2)}, u32[]{:S(2)}) collective-permute-start(bf16[256,896]{1,0:T(8,128)(2,1)} %shard_map.128.refs_0_), channel_id=1, source_target_pairs={{0,16},{16,0},{1,17},{17,1},{2,18},{18,2},{3,19},{19,3},{4,20},{20... | collective-permute-start | bytes 1376264 | tf_op jit(solution)/shard_map/ppermute | solution.py:31
  87.6 20.5 %collective-permute-start.32 = (bf16[256,896]{1,0:T(8,128)(2,1)}, bf16[256,896]{1,0:T(8,128)(2,1)}, u32[]{:S(2)}, u32[]{:S(2)}) collective-permute-start(bf16[256,896]{1,0:T(8,128)(2,1)} %shard_map.128.refs_0_), channel_id=1, source_target_pairs={{0,4},{4,0},{8,12},{12,8},{1,5},{5,1},{9,13},{13,9},{2,6},{6,2},{1... | collective-permute-start | bytes 1376264 | tf_op jit(solution)/shard_map/ppermute | solution.py:31
  88.9 20.7 %collective-permute-start.33 = (bf16[256,896]{1,0:T(8,128)(2,1)}, bf16[256,896]{1,0:T(8,128)(2,1)}, u32[]{:S(2)}, u32[]{:S(2)}) collective-permute-start(bf16[256,896]{1,0:T(8,128)(2,1)} %shard_map.128.refs_0_), channel_id=1, source_target_pairs={{0,8},{4,12},{8,0},{12,4},{1,9},{5,13},{9,1},{13,5},{2,10},{6,14},... | collective-permute-start | bytes 1376264 | tf_op jit(solution)/shard_map/ppermute | solution.py:31
  89.7 22.4 %collective-permute-start.34 = (bf16[256,896]{1,0:T(8,128)(2,1)}, bf16[256,896]{1,0:T(8,128)(2,1)}, u32[]{:S(2)}, u32[]{:S(2)}) collective-permute-start(bf16[256,896]{1,0:T(8,128)(2,1)} %shard_map.128.refs_0_), channel_id=1, source_target_pairs={{0,12},{4,8},{8,4},{12,0},{1,13},{5,9},{9,5},{13,1},{2,14},{6,10},... | collective-permute-start | bytes 1376264 | tf_op jit(solution)/shard_map/ppermute | solution.py:31
  106.1 23.1 %collective-permute-start.29 = (bf16[256,896]{1,0:T(8,128)(2,1)}, bf16[256,896]{1,0:T(8,128)(2,1)}, u32[]{:S(2)}, u32[]{:S(2)}) collective-permute-start(bf16[256,896]{1,0:T(8,128)(2,1)} %get-tuple-element.55.refs_3_), channel_id=1, source_target_pairs={{0,4},{4,0},{8,12},{12,8},{1,5},{5,1},{9,13},{13,9},{2,6},{6,2},{1... | collective-permute-start | bytes 1376264 | tf_op jit(solution)/shard_map/ppermute | solution.py:31
  107.3 21.9 %collective-permute-start.30 = (bf16[256,896]{1,0:T(8,128)(2,1)}, bf16[256,896]{1,0:T(8,128)(2,1)}, u32[]{:S(2)}, u32[]{:S(2)}) collective-permute-start(bf16[256,896]{1,0:T(8,128)(2,1)} %get-tuple-element.56.refs_4_), channel_id=1, source_target_pairs={{0,8},{4,12},{8,0},{12,4},{1,9},{5,13},{9,1},{13,5},{2,10},{6,14},... | collective-permute-start | bytes 1376264 | tf_op jit(solution)/shard_map/ppermute | solution.py:31
  108.1 23.1 %collective-permute-start.31 = (bf16[256,896]{1,0:T(8,128)(2,1)}, bf16[256,896]{1,0:T(8,128)(2,1)}, u32[]{:S(2)}, u32[]{:S(2)}) collective-permute-start(bf16[256,896]{1,0:T(8,128)(2,1)} %get-tuple-element.57.refs_5_), channel_id=1, source_target_pairs={{0,12},{4,8},{8,4},{12,0},{1,13},{5,9},{9,5},{13,1},{2,14},{6,10},... | collective-permute-start | bytes 1376264 | tf_op jit(solution)/shard_map/ppermute | solution.py:31
  134.1 11.7 %collective-permute-start.41 = (bf16[128,896]{1,0:T(8,128)(2,1)S(1)}, bf16[128,896]{1,0:T(8,128)(2,1)S(1)}, u32[]{:S(2)}, u32[]{:S(2)}) collective-permute-start(bf16[128,896]{1,0:T(8,128)(2,1)S(1)} %get-tuple-element.67), channel_id=1, source_target_pairs={{0,8},{4,12},{8,0},{12,4},{1,9},{5,13},{9,1},{13,5},{2,10},{6,14},... | collective-permute-start | bytes 688136 | tf_op jit(solution)/shard_map/ppermute | solution.py:31
  135.6 11.7 %collective-permute-start.42 = (bf16[128,896]{1,0:T(8,128)(2,1)S(1)}, bf16[128,896]{1,0:T(8,128)(2,1)S(1)}, u32[]{:S(2)}, u32[]{:S(2)}) collective-permute-start(bf16[128,896]{1,0:T(8,128)(2,1)S(1)} %get-tuple-element.68), channel_id=1, source_target_pairs={{0,12},{4,8},{8,4},{12,0},{1,13},{5,9},{9,5},{13,1},{2,14},{6,10},... | collective-permute-start | bytes 688136 | tf_op jit(solution)/shard_map/ppermute | solution.py:31
  (34 other events, 255.4 us)

commit v6 on v4

--- a/solution.py
+++ b/solution.py
@@ -440,7 +440,7 @@
     rows, heads, entries = queries.shape
     slots = cache.shape[1]
     _, latent_width, size = w_uv.shape
-    group = 16
+    group = 8
     steps = rows // chunks // group
     return pl.pallas_call(
         functools.partial(attend_kernel, (size + ROPE) ** (-0.5), chunk),

time: 161 us -> 163 us (1.012)
  transfers between devices with their start and end apart: 49 -> 49, of which waited for: 15 -> 16; matrix products, arithmetic and copies ran while one was open for 0% -> 0% of each run, Pallas kernels for 32% -> 32%
where the time goes in v6:
time: 163 us
  Pallas kernels  60.9 us (37%)
  starting transfers between devices  55.7 us (34%)
  waiting for transfers between devices  44.2 us (27%)
    ppermute x49, starting transfers between devices, swap(): return lax.ppermute(x, axis, [(i, i ^ d) for i in range(count)])  55.7 us
    ppermute x49, waiting for transfers between devices, swap(): return lax.ppermute(x, axis, [(i, i ^ d) for i in range(count)])  44.2 us
    pallas_call x2, Pallas kernels, attend(): pl.pallas_call(functools.partial(attend_kernel, (size + ROPE) ** (-0.5),...  16.8 us
    pallas_call x2, Pallas kernels, gate_up(): pl.pallas_call(functools.partial(gate_up_kernel, len(pieces)), in_specs=[...  15.8 us
    pallas_call x2, Pallas kernels, project(): pl.pallas_call(functools.partial(project_kernel, blocks, len(gate)), in_s...  11.2 us
    pallas_call x4, Pallas kernels, down(): pl.pallas_call(down_kernel, in_specs=[SMEM, VMEM, VMEM] + [ANY] * len(aft...  7.69 us
    pallas_call x5, Pallas kernels, stack(): pl.pallas_call(functools.partial(stack_kernel, n), in_specs=[ANY] * (n +...  5.12 us
  transfers between devices with their start and end apart: 49, of which 16 were waited for; matrix products, arithmetic and copies ran while one was open for 0% of the time, Pallas kernels for 32%

profile of v6, /device:TPU:0, one launch (start us, length us, event | category | flops | bytes accessed | tf_op | source)
XLA Modules:
  0.0 162.5 jit_solution(11376894175010268882)
XLA Ops:
  0.7 8.5 %shard_map.118.refs_0_ = bf16[32,4096]{1,0:T(8,128)(2,1)S(1)} custom-call(s32[64]{0:T(128)S(1)} %copy-done.3, bf16[64,32,576]{2,1,0:T(8,128)(2,1)} %q_ref.3, bf16[64,576,128]{2,1,0:T(8,128)(2,1)} %bitcast.36, bf16[32,512,128]{2,1,0:T(8,128)(2,1)} %w_hbm.5), custom_call_target="tpu_custom_call" | custom-call | flops 99999997952 | bytes 1024 | tf_op jit(solution)/shard_map/pallas_call | solution.py:445
  9.2 3.0 %collective-permute-start = (bf16[32,4096]{1,0:T(8,128)(2,1)S(1)}, bf16[32,4096]{1,0:T(8,128)(2,1)S(1)}, u32[]{:S(2)}, u32[]{:S(2)}) collective-permute-start(bf16[32,4096]{1,0:T(8,128)(2,1)S(1)} %shard_map.118.refs_0_), channel_id=1, source_target_pairs={{0,4},{4,0},{8,12},{12,8},{1,5},{5,1},{9,13},{13,9},{2,6},{6,2},{1... | collective-permute-start | bytes 786440 | tf_op jit(solution)/shard_map/ppermute | solution.py:31
  13.7 8.3 %shard_map.119.refs_4_.refs_0_ = bf16[32,4096]{1,0:T(8,128)(2,1)S(1)} custom-call(s32[64]{0:T(128)S(1)} %copy-done.3, bf16[64,32,576]{2,1,0:T(8,128)(2,1)} %q_ref.3, bf16[64,576,128]{2,1,0:T(8,128)(2,1)} %bitcast.37, bf16[32,512,128]{2,1,0:T(8,128)(2,1)} %w_hbm.5, bf16[32,4096]{1,0:T(8,128)(2,1)S(1)} %shard_map.118.refs_0_), custom_call_target="tpu_custom_call" | custom-call | flops 99999997952 | bytes 1024 | tf_op jit(solution)/shard_map/pallas_call | solution.py:445
  22.0 3.5 %collective-permute-done.1.refs_2_ = bf16[32,4096]{1,0:T(8,128)(2,1)S(1)} collective-permute-done((bf16[32,4096]{1,0:T(8,128)(2,1)S(1)}, bf16[32,4096]{1,0:T(8,128)(2,1)S(1)}, u32[]{:S(2)}, u32[]{:S(2)}) %collective-permute-start.1) | collective-permute-done | bytes 262176 | tf_op jit(solution)/shard_map/ppermute | solution.py:31
  29.6 5.6 %shard_map.121 = (bf16[64,896]{1,0:T(8,128)(2,1)S(1)}, bf16[64,896]{1,0:T(8,128)(2,1)S(1)}, bf16[64,896]{1,0:T(8,128)(2,1)S(1)}, bf16[64,896]{1,0:T(8,128)(2,1)S(1)}) custom-call(s32[8]{0:T(128)S(1)} %fusion.pos_ref, bf16[4,32,4096]{2,1,0:T(8,128)(2,1)S(1)} %bitcast.23, bf16[4,32,4096]{2,1,0:T(8,128)(2,1)S(1)} %collective-permute-done.3.far_ref, ...), custom_call_target="tpu_custom_call" | custom-call | flops 99999997952 | bytes 1024 | tf_op jit(solution)/shard_map/pallas_call | solution.py:144
  36.8 2.6 %collective-permute-start.5 = (bf16[64,896]{1,0:T(8,128)(2,1)S(1)}, bf16[64,896]{1,0:T(8,128)(2,1)S(1)}, u32[]{:S(2)}, u32[]{:S(2)}) collective-permute-start(bf16[64,896]{1,0:T(8,128)(2,1)S(1)} %get-tuple-element.43), channel_id=1, source_target_pairs={{0,2},{1,3},{2,0},{3,1},{4,6},{5,7},{6,4},{7,5},{8,10},{9,11},{10,... | collective-permute-start | bytes 344072 | tf_op jit(solution)/shard_map/ppermute | solution.py:31
  41.5 6.8 %collective-permute-done.5.refs_2_ = bf16[64,896]{1,0:T(8,128)(2,1)S(1)} collective-permute-done((bf16[64,896]{1,0:T(8,128)(2,1)S(1)}, bf16[64,896]{1,0:T(8,128)(2,1)S(1)}, u32[]{:S(2)}, u32[]{:S(2)}) %collective-permute-start.5) | collective-permute-done | bytes 114720 | tf_op jit(solution)/shard_map/ppermute | solution.py:31
  52.9 5.6 %shard_map.124 = (bf16[80,896]{1,0:T(8,128)(2,1)S(1)}, bf16[80,896]{1,0:T(8,128)(2,1)S(1)}, bf16[80,896]{1,0:T(8,128)(2,1)S(1)}, bf16[80,896]{1,0:T(8,128)(2,1)S(1)}) custom-call(s32[8]{0:T(128)S(1)} %fusion.pos_ref, bf16[4,32,4096]{2,1,0:T(8,128)(2,1)S(1)} %bitcast.25, bf16[4,32,4096]{2,1,0:T(8,128)(2,1)S(1)} %collective-permute-done.13.far_ref, ...), custom_call_target="tpu_custom_call" | custom-call | flops 99999997952 | bytes 1024 | tf_op jit(solution)/shard_map/pallas_call | solution.py:144
  59.4 2.1 %collective-permute-start.22 = (bf16[80,896]{1,0:T(8,128)(2,1)S(1)}, bf16[80,896]{1,0:T(8,128)(2,1)S(1)}, u32[]{:S(2)}, u32[]{:S(2)}) collective-permute-start(bf16[80,896]{1,0:T(8,128)(2,1)S(1)} %get-tuple-element.49), channel_id=1, source_target_pairs={{0,2},{1,3},{2,0},{3,1},{4,6},{5,7},{6,4},{7,5},{8,10},{9,11},{10,... | collective-permute-start | bytes 430088 | tf_op jit(solution)/shard_map/ppermute | solution.py:31
  67.9 4.5 %collective-permute-done.22.refs_2_ = bf16[80,896]{1,0:T(8,128)(2,1)S(1)} collective-permute-done((bf16[80,896]{1,0:T(8,128)(2,1)S(1)}, bf16[80,896]{1,0:T(8,128)(2,1)S(1)}, u32[]{:S(2)}, u32[]{:S(2)}) %collective-permute-start.22) | collective-permute-done | bytes 143392 | tf_op jit(solution)/shard_map/ppermute | solution.py:31
  72.5 2.4 %collective-permute-start.24 = (bf16[64,896]{1,0:T(8,128)(2,1)S(1)}, bf16[64,896]{1,0:T(8,128)(2,1)S(1)}, u32[]{:S(2)}, u32[]{:S(2)}) collective-permute-start(bf16[64,896]{1,0:T(8,128)(2,1)S(1)} %get-tuple-element.53.refs_0_), channel_id=1, source_target_pairs={{0,1},{1,0},{2,3},{3,2},{4,5},{5,4},{6,7},{7,6},{8,9},{9,8},{10,11... | collective-permute-start | bytes 344072 | tf_op jit(solution)/shard_map/ppermute | solution.py:31
  76.1 2.8 %collective-permute-done.24.refs_1_ = bf16[64,896]{1,0:T(8,128)(2,1)S(1)} collective-permute-done((bf16[64,896]{1,0:T(8,128)(2,1)S(1)}, bf16[64,896]{1,0:T(8,128)(2,1)S(1)}, u32[]{:S(2)}, u32[]{:S(2)}) %collective-permute-start.24) | collective-permute-done | bytes 114720 | tf_op jit(solution)/shard_map/ppermute | solution.py:31
  78.8 2.0 %collective-permute-start.26 = (bf16[64,896]{1,0:T(8,128)(2,1)S(1)}, bf16[64,896]{1,0:T(8,128)(2,1)S(1)}, u32[]{:S(2)}, u32[]{:S(2)}) collective-permute-start(bf16[64,896]{1,0:T(8,128)(2,1)S(1)} %get-tuple-element.53.refs_0_), channel_id=1, source_target_pairs={{0,3},{1,2},{2,1},{3,0},{4,7},{5,6},{6,5},{7,4},{8,11},{9,10},{10,... | collective-permute-start | bytes 344072 | tf_op jit(solution)/shard_map/ppermute | solution.py:31
  81.2 4.6 %collective-permute-done.25.refs_2_ = bf16[64,896]{1,0:T(8,128)(2,1)S(1)} collective-permute-done((bf16[64,896]{1,0:T(8,128)(2,1)S(1)}, bf16[64,896]{1,0:T(8,128)(2,1)S(1)}, u32[]{:S(2)}, u32[]{:S(2)}) %collective-permute-start.25) | collective-permute-done | bytes 114720 | tf_op jit(solution)/shard_map/ppermute | solution.py:31
  92.0 8.0 %shard_map.127 = (bf16[256,512]{1,0:T(8,128)(2,1)S(1)}, f32[4,1792]{1,0:T(4,128)S(1)}) custom-call(s32[8]{0:T(128)S(1)} %stack.39.idx_ref, bf16[272,896]{1,0:T(8,128)(2,1)S(1)} %shard_map.125.refs_4_.refs_0_, bf16[272,896]{1,0:T(8,128)(2,1)S(1)} %collective-permute-done.14.refs_1_.refs_4_, bf16[272,896]{1,0:T(8,128)(2,1)S(1)} %collective-permute-done.15.refs_2_.refs_5_, ...), custom_call_target="tpu_custom_call" | custom-call | flops 99999997952 | bytes 1024 | tf_op jit(solution)/shard_map/pallas_call | solution.py:255
  100.0 2.1 %shard_map.130 = bf16[4,256,896]{2,1,0:T(8,128)(2,1)S(1)} custom-call(s32[4]{0:T(128)S(1)} %pad_add_fusion.1.idx_ref, bf16[256,512]{1,0:T(8,128)(2,1)S(1)} %get-tuple-element.52.act_ref, bf16[512,7168]{1,0:T(8,128)(2,1)S(1)} %bitcast.27), custom_call_target="tpu_custom_call" | custom-call | flops 99999997952 | bytes 1024 | tf_op jit(solution)/shard_map/pallas_call | solution.py:303
  110.6 2.3 %collective-permute-done.34.refs_2_ = bf16[256,896]{1,0:T(8,128)(2,1)} collective-permute-done((bf16[256,896]{1,0:T(8,128)(2,1)}, bf16[256,896]{1,0:T(8,128)(2,1)}, u32[]{:S(2)}, u32[]{:S(2)}) %collective-permute-start.34) | collective-permute-done | bytes 458784 | tf_op jit(solution)/shard_map/ppermute | solution.py:31
  114.9 3.1 %collective-permute-done.35.refs_3_ = bf16[3,256,896]{2,1,0:T(8,128)(2,1)S(1)} collective-permute-done((bf16[3,256,896]{2,1,0:T(8,128)(2,1)S(1)}, bf16[3,256,896]{2,1,0:T(8,128)(2,1)S(1)}, u32[]{:S(2)}, u32[]{:S(2)}) %collective-permute-start.35) | collective-permute-done | bytes 1376288 | tf_op jit(solution)/shard_map/ppermute | solution.py:31
  118.0 7.9 %shard_map.134 = (bf16[256,512]{1,0:T(8,128)(2,1)S(1)}, f32[4,1792]{1,0:T(4,128)}) custom-call(s32[8]{0:T(128)S(1)} %stack.39.idx_ref, bf16[256,896]{1,0:T(8,128)(2,1)} %shard_map.128.refs_0_, bf16[3,256,896]{2,1,0:T(8,128)(2,1)S(1)} %bitcast.33, bf16[256,896]{1,0:T(8,128)(2,1)} %collective-permute-done.27.refs_0_.refs_2_, ...), custom_call_target="tpu_custom_call" | custom-call | flops 99999997952 | bytes 1024 | tf_op jit(solution)/shard_map/pallas_call | solution.py:255
  138.1 2.2 %collective-permute-start.38 = (bf16[64,896]{1,0:T(8,128)(2,1)S(1)}, bf16[64,896]{1,0:T(8,128)(2,1)S(1)}, u32[]{:S(2)}, u32[]{:S(2)}) collective-permute-start(bf16[64,896]{1,0:T(8,128)(2,1)S(1)} %get-tuple-element.63), channel_id=1, source_target_pairs={{0,2},{1,3},{2,0},{3,1},{4,6},{5,7},{6,4},{7,5},{8,10},{9,11},{10,... | collective-permute-start | bytes 344072 | tf_op jit(solution)/shard_map/ppermute | solution.py:31
  140.3 3.6 %collective-permute-done.37.refs_5_.refs_2_ = bf16[64,896]{1,0:T(8,128)(2,1)S(1)} collective-permute-done((bf16[64,896]{1,0:T(8,128)(2,1)S(1)}, bf16[64,896]{1,0:T(8,128)(2,1)S(1)}, u32[]{:S(2)}, u32[]{:S(2)}) %collective-permute-start.37) | collective-permute-done | bytes 114720 | tf_op jit(solution)/shard_map/ppermute | solution.py:31
  149.0 2.9 %collective-permute-start.43 = (bf16[64,896]{1,0:T(8,128)(2,1)S(1)}, bf16[64,896]{1,0:T(8,128)(2,1)S(1)}, u32[]{:S(2)}, u32[]{:S(2)}) collective-permute-start(bf16[64,896]{1,0:T(8,128)(2,1)S(1)} %get-tuple-element.70.refs_4_), channel_id=1, source_target_pairs={{0,2},{1,3},{2,0},{3,1},{4,6},{5,7},{6,4},{7,5},{8,10},{9,11},{10,... | collective-permute-start | bytes 344072 | tf_op jit(solution)/shard_map/ppermute | solution.py:31
  153.2 2.1 %collective-permute-done.46.refs_2_ = bf16[128,896]{1,0:T(8,128)(2,1)S(1)} collective-permute-done((bf16[128,896]{1,0:T(8,128)(2,1)S(1)}, bf16[128,896]{1,0:T(8,128)(2,1)S(1)}, u32[]{:S(2)}, u32[]{:S(2)}) %collective-permute-start.46) | collective-permute-done | bytes 229408 | tf_op jit(solution)/shard_map/ppermute | solution.py:31
  159.8 2.0 %collective-permute-done.48.refs_7_ = bf16[64,896]{1,0:T(8,128)(2,1)S(1)} collective-permute-done((bf16[64,896]{1,0:T(8,128)(2,1)S(1)}, bf16[64,896]{1,0:T(8,128)(2,1)S(1)}, u32[]{:S(2)}, u32[]{:S(2)}) %collective-permute-start.48) | collective-permute-done | bytes 114720 | tf_op jit(solution)/shard_map/ppermute | solution.py:31
  (127 shorter events, 63.7 us)
Async XLA Ops:
  9.2 12.9 %collective-permute-start = (bf16[32,4096]{1,0:T(8,128)(2,1)S(1)}, bf16[32,4096]{1,0:T(8,128)(2,1)S(1)}, u32[]{:S(2)}, u32[]{:S(2)}) collective-permute-start(bf16[32,4096]{1,0:T(8,128)(2,1)S(1)} %shard_map.118.refs_0_), channel_id=1, source_target_pairs={{0,4},{4,0},{8,12},{12,8},{1,5},{5,1},{9,13},{13,9},{2,6},{6,2},{1... | collective-permute-start | bytes 786440 | tf_op jit(solution)/shard_map/ppermute | solution.py:31
  12.2 13.4 %collective-permute-start.1 = (bf16[32,4096]{1,0:T(8,128)(2,1)S(1)}, bf16[32,4096]{1,0:T(8,128)(2,1)S(1)}, u32[]{:S(2)}, u32[]{:S(2)}) collective-permute-start(bf16[32,4096]{1,0:T(8,128)(2,1)S(1)} %shard_map.118.refs_0_), channel_id=1, source_target_pairs={{0,8},{4,12},{8,0},{12,4},{1,9},{5,13},{9,1},{13,5},{2,10},{6,14},... | collective-permute-start | bytes 786440 | tf_op jit(solution)/shard_map/ppermute | solution.py:31
  13.7 11.9 %collective-permute-start.2 = (bf16[32,4096]{1,0:T(8,128)(2,1)S(1)}, bf16[32,4096]{1,0:T(8,128)(2,1)S(1)}, u32[]{:S(2)}, u32[]{:S(2)}) collective-permute-start(bf16[32,4096]{1,0:T(8,128)(2,1)S(1)} %shard_map.118.refs_0_), channel_id=1, source_target_pairs={{0,12},{4,8},{8,4},{12,0},{1,13},{5,9},{9,5},{13,1},{2,14},{6,10},... | collective-permute-start | bytes 786440 | tf_op jit(solution)/shard_map/ppermute | solution.py:31
  25.9 13.5 %collective-permute-start.10 = (bf16[32,4096]{1,0:T(8,128)(2,1)S(1)}, bf16[32,4096]{1,0:T(8,128)(2,1)S(1)}, u32[]{:S(2)}, u32[]{:S(2)}) collective-permute-start(bf16[32,4096]{1,0:T(8,128)(2,1)S(1)} %shard_map.119.refs_4_.refs_0_), channel_id=1, source_target_pairs={{0,4},{4,0},{8,12},{12,8},{1,5},{5,1},{9,13},{13,9},{2,6},{6,2},{1... | collective-permute-start | bytes 786440 | tf_op jit(solution)/shard_map/ppermute | solution.py:31
  27.2 12.5 %collective-permute-start.11 = (bf16[32,4096]{1,0:T(8,128)(2,1)S(1)}, bf16[32,4096]{1,0:T(8,128)(2,1)S(1)}, u32[]{:S(2)}, u32[]{:S(2)}) collective-permute-start(bf16[32,4096]{1,0:T(8,128)(2,1)S(1)} %shard_map.119.refs_4_.refs_0_), channel_id=1, source_target_pairs={{0,8},{4,12},{8,0},{12,4},{1,9},{5,13},{9,1},{13,5},{2,10},{6,14},... | collective-permute-start | bytes 786440 | tf_op jit(solution)/shard_map/ppermute | solution.py:31
  28.0 13.2 %collective-permute-start.12 = (bf16[32,4096]{1,0:T(8,128)(2,1)S(1)}, bf16[32,4096]{1,0:T(8,128)(2,1)S(1)}, u32[]{:S(2)}, u32[]{:S(2)}) collective-permute-start(bf16[32,4096]{1,0:T(8,128)(2,1)S(1)} %shard_map.119.refs_4_.refs_0_), channel_id=1, source_target_pairs={{0,12},{4,8},{8,4},{12,0},{1,13},{5,9},{9,5},{13,1},{2,14},{6,10},... | collective-permute-start | bytes 786440 | tf_op jit(solution)/shard_map/ppermute | solution.py:31
  36.8 11.5 %collective-permute-start.5 = (bf16[64,896]{1,0:T(8,128)(2,1)S(1)}, bf16[64,896]{1,0:T(8,128)(2,1)S(1)}, u32[]{:S(2)}, u32[]{:S(2)}) collective-permute-start(bf16[64,896]{1,0:T(8,128)(2,1)S(1)} %get-tuple-element.43), channel_id=1, source_target_pairs={{0,2},{1,3},{2,0},{3,1},{4,6},{5,7},{6,4},{7,5},{8,10},{9,11},{10,... | collective-permute-start | bytes 344072 | tf_op jit(solution)/shard_map/ppermute | solution.py:31
  41.4 11.5 %collective-permute-start.13 = (bf16[4,32,4096]{2,1,0:T(8,128)(2,1)S(1)}, bf16[4,32,4096]{2,1,0:T(8,128)(2,1)S(1)}, u32[]{:S(2)}, u32[]{:S(2)}) collective-permute-start(bf16[4,32,4096]{2,1,0:T(8,128)(2,1)S(1)} %bitcast.24), channel_id=1, source_target_pairs={{0,16},{16,0},{1,17},{17,1},{2,18},{18,2},{3,19},{19,3},{4,20},{20... | collective-permute-start | bytes 3145736 | tf_op jit(solution)/shard_map/ppermute | solution.py:31
  48.4 13.2 %collective-permute-start.7 = (bf16[64,896]{1,0:T(8,128)(2,1)S(1)}, bf16[64,896]{1,0:T(8,128)(2,1)S(1)}, u32[]{:S(2)}, u32[]{:S(2)}) collective-permute-start(bf16[64,896]{1,0:T(8,128)(2,1)S(1)} %get-tuple-element.46.refs_1_.refs_0_), channel_id=1, source_target_pairs={{0,1},{1,0},{2,3},{3,2},{4,5},{5,4},{6,7},{7,6},{8,9},{9,8},{10,11... | collective-permute-start | bytes 344072 | tf_op jit(solution)/shard_map/ppermute | solution.py:31
  50.3 12.7 %collective-permute-start.8 = (bf16[64,896]{1,0:T(8,128)(2,1)S(1)}, bf16[64,896]{1,0:T(8,128)(2,1)S(1)}, u32[]{:S(2)}, u32[]{:S(2)}) collective-permute-start(bf16[64,896]{1,0:T(8,128)(2,1)S(1)} %get-tuple-element.46.refs_1_.refs_0_), channel_id=1, source_target_pairs={{0,2},{1,3},{2,0},{3,1},{4,6},{5,7},{6,4},{7,5},{8,10},{9,11},{10,... | collective-permute-start | bytes 344072 | tf_op jit(solution)/shard_map/ppermute | solution.py:31
  59.4 12.9 %collective-permute-start.22 = (bf16[80,896]{1,0:T(8,128)(2,1)S(1)}, bf16[80,896]{1,0:T(8,128)(2,1)S(1)}, u32[]{:S(2)}, u32[]{:S(2)}) collective-permute-start(bf16[80,896]{1,0:T(8,128)(2,1)S(1)} %get-tuple-element.49), channel_id=1, source_target_pairs={{0,2},{1,3},{2,0},{3,1},{4,6},{5,7},{6,4},{7,5},{8,10},{9,11},{10,... | collective-permute-start | bytes 430088 | tf_op jit(solution)/shard_map/ppermute | solution.py:31
  64.3 21.5 %collective-permute-start.14 = (bf16[272,896]{1,0:T(8,128)(2,1)S(1)}, bf16[272,896]{1,0:T(8,128)(2,1)S(1)}, u32[]{:S(2)}, u32[]{:S(2)}) collective-permute-start(bf16[272,896]{1,0:T(8,128)(2,1)S(1)} %shard_map.125.refs_4_.refs_0_), channel_id=1, source_target_pairs={{0,4},{4,0},{8,12},{12,8},{1,5},{5,1},{9,13},{13,9},{2,6},{6,2},{1... | collective-permute-start | bytes 1462280 | tf_op jit(solution)/shard_map/ppermute | solution.py:31
  65.6 20.7 %collective-permute-start.15 = (bf16[272,896]{1,0:T(8,128)(2,1)S(1)}, bf16[272,896]{1,0:T(8,128)(2,1)S(1)}, u32[]{:S(2)}, u32[]{:S(2)}) collective-permute-start(bf16[272,896]{1,0:T(8,128)(2,1)S(1)} %shard_map.125.refs_4_.refs_0_), channel_id=1, source_target_pairs={{0,8},{4,12},{8,0},{12,4},{1,9},{5,13},{9,1},{13,5},{2,10},{6,14},... | collective-permute-start | bytes 1462280 | tf_op jit(solution)/shard_map/ppermute | solution.py:31
  66.5 20.0 %collective-permute-start.16 = (bf16[272,896]{1,0:T(8,128)(2,1)S(1)}, bf16[272,896]{1,0:T(8,128)(2,1)S(1)}, u32[]{:S(2)}, u32[]{:S(2)}) collective-permute-start(bf16[272,896]{1,0:T(8,128)(2,1)S(1)} %shard_map.125.refs_4_.refs_0_), channel_id=1, source_target_pairs={{0,12},{4,8},{8,4},{12,0},{1,13},{5,9},{9,5},{13,1},{2,14},{6,10},... | collective-permute-start | bytes 1462280 | tf_op jit(solution)/shard_map/ppermute | solution.py:31
  88.3 13.8 %collective-permute-start.27 = (bf16[256,896]{1,0:T(8,128)(2,1)}, bf16[256,896]{1,0:T(8,128)(2,1)}, u32[]{:S(2)}, u32[]{:S(2)}) collective-permute-start(bf16[256,896]{1,0:T(8,128)(2,1)} %shard_map.128.refs_0_), channel_id=1, source_target_pairs={{0,16},{16,0},{1,17},{17,1},{2,18},{18,2},{3,19},{19,3},{4,20},{20... | collective-permute-start | bytes 1376264 | tf_op jit(solution)/shard_map/ppermute | solution.py:31
  88.4 20.7 %collective-permute-start.32 = (bf16[256,896]{1,0:T(8,128)(2,1)}, bf16[256,896]{1,0:T(8,128)(2,1)}, u32[]{:S(2)}, u32[]{:S(2)}) collective-permute-start(bf16[256,896]{1,0:T(8,128)(2,1)} %shard_map.128.refs_0_), channel_id=1, source_target_pairs={{0,4},{4,0},{8,12},{12,8},{1,5},{5,1},{9,13},{13,9},{2,6},{6,2},{1... | collective-permute-start | bytes 1376264 | tf_op jit(solution)/shard_map/ppermute | solution.py:31
  89.7 20.9 %collective-permute-start.33 = (bf16[256,896]{1,0:T(8,128)(2,1)}, bf16[256,896]{1,0:T(8,128)(2,1)}, u32[]{:S(2)}, u32[]{:S(2)}) collective-permute-start(bf16[256,896]{1,0:T(8,128)(2,1)} %shard_map.128.refs_0_), channel_id=1, source_target_pairs={{0,8},{4,12},{8,0},{12,4},{1,9},{5,13},{9,1},{13,5},{2,10},{6,14},... | collective-permute-start | bytes 1376264 | tf_op jit(solution)/shard_map/ppermute | solution.py:31
  90.5 22.4 %collective-permute-start.34 = (bf16[256,896]{1,0:T(8,128)(2,1)}, bf16[256,896]{1,0:T(8,128)(2,1)}, u32[]{:S(2)}, u32[]{:S(2)}) collective-permute-start(bf16[256,896]{1,0:T(8,128)(2,1)} %shard_map.128.refs_0_), channel_id=1, source_target_pairs={{0,12},{4,8},{8,4},{12,0},{1,13},{5,9},{9,5},{13,1},{2,14},{6,10},... | collective-permute-start | bytes 1376264 | tf_op jit(solution)/shard_map/ppermute | solution.py:31
  107.1 27.3 %collective-permute-start.29 = (bf16[256,896]{1,0:T(8,128)(2,1)}, bf16[256,896]{1,0:T(8,128)(2,1)}, u32[]{:S(2)}, u32[]{:S(2)}) collective-permute-start(bf16[256,896]{1,0:T(8,128)(2,1)} %get-tuple-element.55.refs_3_), channel_id=1, source_target_pairs={{0,4},{4,0},{8,12},{12,8},{1,5},{5,1},{9,13},{13,9},{2,6},{6,2},{1... | collective-permute-start | bytes 1376264 | tf_op jit(solution)/shard_map/ppermute | solution.py:31
  108.3 27.3 %collective-permute-start.30 = (bf16[256,896]{1,0:T(8,128)(2,1)}, bf16[256,896]{1,0:T(8,128)(2,1)}, u32[]{:S(2)}, u32[]{:S(2)}) collective-permute-start(bf16[256,896]{1,0:T(8,128)(2,1)} %get-tuple-element.56.refs_4_), channel_id=1, source_target_pairs={{0,8},{4,12},{8,0},{12,4},{1,9},{5,13},{9,1},{13,5},{2,10},{6,14},... | collective-permute-start | bytes 1376264 | tf_op jit(solution)/shard_map/ppermute | solution.py:31
  109.1 26.4 %collective-permute-start.31 = (bf16[256,896]{1,0:T(8,128)(2,1)}, bf16[256,896]{1,0:T(8,128)(2,1)}, u32[]{:S(2)}, u32[]{:S(2)}) collective-permute-start(bf16[256,896]{1,0:T(8,128)(2,1)} %get-tuple-element.57.refs_5_), channel_id=1, source_target_pairs={{0,12},{4,8},{8,4},{12,0},{1,13},{5,9},{9,5},{13,1},{2,14},{6,10},... | collective-permute-start | bytes 1376264 | tf_op jit(solution)/shard_map/ppermute | solution.py:31
  132.0 13.3 %collective-permute-start.40 = (bf16[128,896]{1,0:T(8,128)(2,1)S(1)}, bf16[128,896]{1,0:T(8,128)(2,1)S(1)}, u32[]{:S(2)}, u32[]{:S(2)}) collective-permute-start(bf16[128,896]{1,0:T(8,128)(2,1)S(1)} %get-tuple-element.67), channel_id=1, source_target_pairs={{0,4},{4,0},{8,12},{12,8},{1,5},{5,1},{9,13},{13,9},{2,6},{6,2},{1... | collective-permute-start | bytes 688136 | tf_op jit(solution)/shard_map/ppermute | solution.py:31
  132.6 14.1 %collective-permute-start.41 = (bf16[128,896]{1,0:T(8,128)(2,1)S(1)}, bf16[128,896]{1,0:T(8,128)(2,1)S(1)}, u32[]{:S(2)}, u32[]{:S(2)}) collective-permute-start(bf16[128,896]{1,0:T(8,128)(2,1)S(1)} %get-tuple-element.68), channel_id=1, source_target_pairs={{0,8},{4,12},{8,0},{12,4},{1,9},{5,13},{9,1},{13,5},{2,10},{6,14},... | collective-permute-start | bytes 688136 | tf_op jit(solution)/shard_map/ppermute | solution.py:31
  134.3 13.6 %collective-permute-start.42 = (bf16[128,896]{1,0:T(8,128)(2,1)S(1)}, bf16[128,896]{1,0:T(8,128)(2,1)S(1)}, u32[]{:S(2)}, u32[]{:S(2)}) collective-permute-start(bf16[128,896]{1,0:T(8,128)(2,1)S(1)} %get-tuple-element.69), channel_id=1, source_target_pairs={{0,12},{4,8},{8,4},{12,0},{1,13},{5,9},{9,5},{13,1},{2,14},{6,10},... | collective-permute-start | bytes 688136 | tf_op jit(solution)/shard_map/ppermute | solution.py:31
  (33 other events, 244.7 us)
